TPU v7x, 32 devices: a whole 2x2x4 slice. The times are simulated.
32 devices in a mesh: rows: 8 (over z, y), seq: 4 (over x, core).
Axes of the slice: x: 2, y: 2, z: 4, core: 2. Of those that a mesh axis runs over, the one named last changes fastest.
Arguments:
- tokens: bfloat16 [32, 512, 768], P('rows', 'seq'), may hold values from -6 to 6
- w_query: bfloat16 [768, 768], replicated, may hold values from -0.4375 to 0.4375
- b_query: float32 [768], replicated, may hold values from -3 to 3
- w_key: bfloat16 [768, 768], replicated, may hold values from -0.21875 to 0.21875
- w_value: bfloat16 [768, 768], replicated, may hold values from -0.21875 to 0.21875
- b_value: float32 [768], replicated, may hold values from -0.6 to 0.6
- w_out: bfloat16 [768, 768], replicated, may hold values from -0.875 to 0.875
- b_out: float32 [768], replicated, may hold values from -1.8 to 1.8
- gain_one: float32 [768], replicated, may hold values from 0.5 to 1.5
- shift_one: float32 [768], replicated, may hold values from -1.2 to 1.2
- w_up: bfloat16 [768, 3072], replicated, may hold values from -0.21875 to 0.21875
- b_up: float32 [3072], replicated, may hold values from -3 to 3
- w_down: bfloat16 [3072, 768], replicated, may hold values from -0.109375 to 0.109375
- b_down: float32 [768], replicated, may hold values from -1.2 to 1.2
- gain_two: float32 [768], replicated, may hold values from 0.5 to 1.5
- shift_two: float32 [768], replicated, may hold values from -1.2 to 1.2
- passage_starts: int32 [32, 6], P('rows'), may hold values from 0 to 511, as said below
- queries: bfloat16 [1024, 768], P(('rows', 'seq')), may hold values from -3 to 3
- choices: int32 [1024, 32], P(('rows', 'seq')), may hold values from 0 to 191
- cotangent: bfloat16 [32, 512, 768], P('rows', 'seq'), may hold values from -6 to 6
Outputs:
- mixed: bfloat16 [32, 512, 768], P('rows', 'seq')
- query_losses: float32 [1024], P(('rows', 'seq'))
- grad_tokens: bfloat16 [32, 512, 768], P('rows', 'seq')
- grad_w_query: float32 [768, 768], P('seq')
- grad_b_query: float32 [768], P('seq')
- grad_w_key: float32 [768, 768], P('seq')
- grad_w_value: float32 [768, 768], P('seq')
- grad_b_value: float32 [768], P('seq')
- grad_w_out: float32 [768, 768], P('seq')
- grad_b_out: float32 [768], P('seq')
- grad_gain_one: float32 [768], P('seq')
- grad_shift_one: float32 [768], P('seq')
- grad_w_up: float32 [768, 3072], P('seq')
- grad_b_up: float32 [3072], P('seq')
- grad_w_down: float32 [3072, 768], P('seq')
- grad_b_down: float32 [768], P('seq')
- grad_gain_two: float32 [768], P('seq')
- grad_shift_two: float32 [768], P('seq')
Inputs may be any that keep to these rules, and one draw needn't show every extreme that they name: `passage_starts`: each row lists the first positions of its 6 passages in rising order, the first being 0; a passage runs up to the next one's first position or to the row's end. In every aligned block of 4 rows one row's first passage reaches into the row's last 128 positions, and that row's last passage is its last position alone. `choices`: entry 0 of each row is the query's positive passage; passage r * 6 + j is passage j of row r.
All inputs are finite; a program needn't handle non-finite values.
Results may differ from a plain program's by a relative error of at most 0.015.
The roundings to bfloat16 on the way count: a program that leaves them out, or rounds other values in their place, can miss the bound.
Values may be sent and summed in bfloat16 or wider, within the bound.
No kernel may reach another device: no remote copies, remote signals or barrier semaphores. Data moves between devices by JAX's collectives and lax.ppermute only.
A program may use at most 192 MiB of HBM per device.

v0:
```python
import jax
import jax.numpy as jnp
from jax import lax
from jax.sharding import PartitionSpec as P

HEADS = 12
HEAD = 64
PASS = 6
CH = 32


norm_eps = 1e-05


def layer_norm(values, gain, shift):
    center = values - jnp.mean(values, -1, keepdims=True)
    spread = jnp.mean(center * center, -1, keepdims=True)
    return center * lax.rsqrt(spread + norm_eps) * gain + shift


def gelu_exact(values):
    return jax.nn.gelu(values, approximate=False)


def per_device(
    tokens,
    w_query,
    b_query,
    w_key,
    w_value,
    b_value,
    w_out,
    b_out,
    gain_one,
    shift_one,
    w_up,
    b_up,
    w_down,
    b_down,
    gain_two,
    shift_two,
    passage_starts,
    queries,
    choices,
    cotangent,
):
    f32 = jnp.float32
    bf16 = jnp.bfloat16
    seq_count = lax.axis_size("seq")
    seq_index = lax.axis_index("seq")
    row_block, piece_len, model_width = tokens.shape
    length = piece_len * seq_count
    score_scale = HEAD ** (-0.5)
    places = jnp.arange(length, dtype=jnp.int32)
    seg_all = (
        jnp.sum((passage_starts[:, None, :] <= places[None, :, None]).astype(jnp.int32), -1) - 1
    )
    seg_local = lax.dynamic_slice_in_dim(seg_all, seq_index * piece_len, piece_len, 1)
    same_passage = seg_local[:, None, :, None] == seg_all[:, None, None, :]
    local_places = seq_index * piece_len + jnp.arange(piece_len, dtype=jnp.int32)
    query_b = (jnp.dot(tokens, w_query, preferred_element_type=f32) + b_query).astype(bf16)
    key_b = jnp.dot(tokens, w_key, preferred_element_type=f32).astype(bf16)
    value_b = (jnp.dot(tokens, w_value, preferred_element_type=f32) + b_value).astype(bf16)
    keys_all, values_all = (
        lax.all_gather(key_b, "seq", axis=1, tiled=True),
        lax.all_gather(value_b, "seq", axis=1, tiled=True),
    )
    query_heads = query_b.reshape(row_block, piece_len, HEADS, HEAD)
    key_heads = keys_all.reshape(row_block, length, HEADS, HEAD)
    value_heads = values_all.reshape(row_block, length, HEADS, HEAD)

    def masked_scores():
        raw = jnp.einsum("rqhd,rkhd->rhqk", query_heads, key_heads, preferred_element_type=f32)
        return jnp.where(same_passage, raw * score_scale, -1e30)

    scores = masked_scores()
    log_total = jax.nn.logsumexp(scores, axis=-1, keepdims=True)
    attention_b = jnp.exp(scores - log_total).astype(bf16)
    context = jnp.einsum("rhqk,rkhd->rqhd", attention_b, value_heads, preferred_element_type=f32)
    context = context.reshape(row_block, piece_len, model_width).astype(bf16)
    attended = jnp.dot(context, w_out, preferred_element_type=f32) + b_out
    resid_one = tokens.astype(f32) + attended
    hidden_f, ln_one_back = jax.vjp(layer_norm, resid_one, gain_one, shift_one)
    hidden_one = hidden_f.astype(bf16)
    up_f = jnp.dot(hidden_one, w_up, preferred_element_type=f32) + b_up
    act_f, gelu_back = jax.vjp(gelu_exact, up_f)
    act_b = act_f.astype(bf16)
    resid_two = hidden_one.astype(f32) + jnp.dot(act_b, w_down, preferred_element_type=f32) + b_down
    mixed_f, ln_two_back = jax.vjp(layer_norm, resid_two, gain_two, shift_two)
    mixed = mixed_f.astype(bf16)
    owner_table = passage_starts[:, :, None] == local_places[None, None, :]
    own_slab = jnp.einsum(
        "rjp,rpd->rjd", owner_table.astype(bf16), mixed, preferred_element_type=f32
    )
    own_slab = own_slab.reshape(row_block * PASS, model_width)
    group_pool = lax.psum(own_slab.astype(jnp.bfloat16), "seq").astype(jnp.float32).astype(bf16)
    pooled = lax.all_gather(group_pool, "rows", axis=0, tiled=True)
    candidates = pooled[choices]
    logits = jnp.einsum("ncd,nd->nc", candidates, queries, preferred_element_type=f32)
    query_losses = jax.nn.logsumexp(logits, axis=-1) - logits[:, 0]
    first_column = (jnp.arange(CH, dtype=jnp.int32) == 0).astype(f32)
    grad_logits = jax.nn.softmax(logits, axis=-1) - first_column[None, :]
    grad_cand = grad_logits[:, :, None] * queries.astype(f32)[:, None, :]
    pool_grad = jax.ops.segment_sum(
        grad_cand.reshape(-1, model_width), choices.reshape(-1), num_segments=pooled.shape[0]
    )
    group_grad = lax.psum_scatter(pool_grad, "rows", scatter_dimension=0, tiled=True)
    group_grad = lax.psum(group_grad, "seq")
    grad_mixed = cotangent.astype(f32) + jnp.einsum(
        "rjp,rjd->rpd",
        owner_table.astype(f32),
        group_grad.reshape(row_block, PASS, model_width),
        precision=lax.Precision.HIGHEST,
        preferred_element_type=f32,
    )
    grad_resid_two, grad_gain_two, grad_shift_two = ln_two_back(grad_mixed)
    grad_down_b = grad_resid_two.astype(bf16)
    grad_b_down = jnp.sum(grad_down_b.astype(f32), axis=(0, 1))
    grad_w_down = jnp.einsum("rpf,rpd->fd", act_b, grad_down_b, preferred_element_type=f32)
    grad_act = jnp.einsum("rpd,fd->rpf", grad_down_b, w_down, preferred_element_type=f32)
    grad_up_b = gelu_back(grad_act)[0].astype(bf16)
    grad_b_up = jnp.sum(grad_up_b.astype(f32), axis=(0, 1))
    grad_w_up = jnp.einsum("rpd,rpf->df", hidden_one, grad_up_b, preferred_element_type=f32)
    grad_hidden = grad_resid_two + jnp.einsum(
        "rpf,df->rpd", grad_up_b, w_up, preferred_element_type=f32
    )
    grad_resid_one, grad_gain_one, grad_shift_one = ln_one_back(grad_hidden)
    grad_attended_b = grad_resid_one.astype(bf16)
    grad_b_out = jnp.sum(grad_attended_b.astype(f32), axis=(0, 1))
    grad_w_out = jnp.einsum("rpc,rpd->cd", context, grad_attended_b, preferred_element_type=f32)
    grad_context = jnp.einsum("rpd,cd->rpc", grad_attended_b, w_out, preferred_element_type=f32)
    grad_context = grad_context.astype(bf16).reshape(row_block, piece_len, HEADS, HEAD)
    probability = jnp.exp(masked_scores() - log_total)
    grad_attention = jnp.einsum(
        "rqhd,rkhd->rhqk", grad_context, value_heads, preferred_element_type=f32
    )
    row_dots = jnp.sum(probability * grad_attention, -1, keepdims=True)
    grad_scores = probability * (grad_attention - row_dots)
    grad_raw = (grad_scores * score_scale).astype(bf16)
    grad_query = jnp.einsum("rhqk,rkhd->rqhd", grad_raw, key_heads, preferred_element_type=f32)
    grad_query = grad_query.reshape(row_block, piece_len, model_width).astype(bf16)
    grad_key_part = jnp.einsum("rhqk,rqhd->rkhd", grad_raw, query_heads, preferred_element_type=f32)
    grad_value_part = jnp.einsum(
        "rhqk,rqhd->rkhd", probability.astype(bf16), grad_context, preferred_element_type=f32
    )
    grad_key_part = grad_key_part.reshape(row_block, length, model_width)
    grad_value_part = grad_value_part.reshape(row_block, length, model_width)
    grad_key, grad_value = (
        lax.psum_scatter(grad_key_part, "seq", scatter_dimension=1, tiled=True),
        lax.psum_scatter(grad_value_part, "seq", scatter_dimension=1, tiled=True),
    )
    grad_key = grad_key.astype(bf16)
    grad_value = grad_value.astype(bf16)
    grad_b_query = jnp.sum(grad_query.astype(f32), axis=(0, 1))
    grad_w_query = jnp.einsum("rpc,rpd->cd", tokens, grad_query, preferred_element_type=f32)
    grad_w_key = jnp.einsum("rpc,rpd->cd", tokens, grad_key, preferred_element_type=f32)
    grad_w_value = jnp.einsum("rpc,rpd->cd", tokens, grad_value, preferred_element_type=f32)
    grad_b_value = jnp.sum(grad_value.astype(f32), axis=(0, 1))
    grad_tokens = (
        grad_resid_one
        + jnp.einsum("rpd,cd->rpc", grad_query, w_query, preferred_element_type=f32)
        + jnp.einsum("rpd,cd->rpc", grad_key, w_key, preferred_element_type=f32)
        + jnp.einsum("rpd,cd->rpc", grad_value, w_value, preferred_element_type=f32)
    ).astype(bf16)
    (
        part_wq,
        part_bq,
        part_wk,
        part_wv,
        part_bv,
        part_wo,
        part_bo,
        part_go,
        part_so,
        part_wu,
        part_bu,
        part_wd,
        part_bd,
        part_gt,
        part_st,
    ) = (
        lax.psum_scatter(grad_w_query, "seq", scatter_dimension=0, tiled=True),
        lax.psum_scatter(grad_b_query, "seq", scatter_dimension=0, tiled=True),
        lax.psum_scatter(grad_w_key, "seq", scatter_dimension=0, tiled=True),
        lax.psum_scatter(grad_w_value, "seq", scatter_dimension=0, tiled=True),
        lax.psum_scatter(grad_b_value, "seq", scatter_dimension=0, tiled=True),
        lax.psum_scatter(grad_w_out, "seq", scatter_dimension=0, tiled=True),
        lax.psum_scatter(grad_b_out, "seq", scatter_dimension=0, tiled=True),
        lax.psum_scatter(grad_gain_one, "seq", scatter_dimension=0, tiled=True),
        lax.psum_scatter(grad_shift_one, "seq", scatter_dimension=0, tiled=True),
        lax.psum_scatter(grad_w_up, "seq", scatter_dimension=0, tiled=True),
        lax.psum_scatter(grad_b_up, "seq", scatter_dimension=0, tiled=True),
        lax.psum_scatter(grad_w_down, "seq", scatter_dimension=0, tiled=True),
        lax.psum_scatter(grad_b_down, "seq", scatter_dimension=0, tiled=True),
        lax.psum_scatter(grad_gain_two, "seq", scatter_dimension=0, tiled=True),
        lax.psum_scatter(grad_shift_two, "seq", scatter_dimension=0, tiled=True),
    )
    shards = lax.psum(
        (
            part_wq,
            part_bq,
            part_wk,
            part_wv,
            part_bv,
            part_wo,
            part_bo,
            part_go,
            part_so,
            part_wu,
            part_bu,
            part_wd,
            part_bd,
            part_gt,
            part_st,
        ),
        "rows",
    )
    return (
        mixed,
        query_losses,
        grad_tokens,
        shards[0],
        shards[1],
        shards[2],
        shards[3],
        shards[4],
        shards[5],
        shards[6],
        shards[7],
        shards[8],
        shards[9],
        shards[10],
        shards[11],
        shards[12],
        shards[13],
        shards[14],
    )


def solution(mesh):
    placed = (
        P("rows", "seq", None),
        P(),
        P(),
        P(),
        P(),
        P(),
        P(),
        P(),
        P(),
        P(),
        P(),
        P(),
        P(),
        P(),
        P(),
        P(),
        P("rows", None),
        P(("rows", "seq"), None),
        P(("rows", "seq"), None),
        P("rows", "seq", None),
    )
    return jax.shard_map(
        per_device,
        mesh=mesh,
        in_specs=placed,
        out_specs=(
            P("rows", "seq", None),
            P(("rows", "seq")),
            P("rows", "seq", None),
            P("seq", None),
            P("seq"),
            P("seq", None),
            P("seq", None),
            P("seq"),
            P("seq", None),
            P("seq"),
            P("seq"),
            P("seq"),
            P("seq", None),
            P("seq"),
            P("seq", None),
            P("seq"),
            P("seq"),
            P("seq"),
        ),
        check_vma=False,
    )
```

profile of v0, /device:TPU:0, one launch (start us, length us, event | category | flops | bytes accessed | tf_op | source)
XLA Modules:
  0.0 1018.0 jit_solution(9151528649372246721)
XLA Ops:
  19.6 22.4 %all-gather.5.cloned.1.call-done = bf16[4,512,768]{2,1,0:T(8,128)(2,1)} async-done(((bf16[4,128,768]{2,1,0:T(8,128)(2,1)}), bf16[4,512,768]{2,1,0:T(8,128)(2,1)}) %all-gather.5.cloned.1.call-update) | async-done | bytes 3145744 | tf_op jit(solution)/shard_map/all_gather | solution.py:65
  56.1 16.6 %all-gather.3.cloned.1.call-done = bf16[4,512,768]{2,1,0:T(8,128)(2,1)} async-done(((bf16[4,128,768]{2,1,0:T(8,128)(2,1)}), bf16[4,512,768]{2,1,0:T(8,128)(2,1)}) %all-gather.3.cloned.1.call-update) | async-done | bytes 3145744 | tf_op jit(solution)/shard_map/all_gather | solution.py:66
  77.4 8.9 convolution_convert_fusion.2
  95.1 15.6 %multiply_convert_fusion.1 = (bf16[4,128,3072]{2,1,0:T(8,128)(2,1)S(1)}, f32[4,128,3072]{2,1,0:T(8,128)}) fusion(f32[4,128,3072]{2,1,0:T(8,128)S(1)} %get-tuple-element.156, f32[3072]{0:T(1024)S(1)} %copy-done.47, u8[128,3072]{1,0:T(8,128)(4,1)S(1)} %get-tuple-element.109, u8[128,3072]{1,0:T(8,128)(4,1)S(1)} %get-tuple-element.108), kind=kLoop, calls=%fused_computation.21 | loop fusion | flops 111673344 | bytes 16527360 | tf_op jit(solution)/shard_map/convert_element_type | solution.py:87
  116.7 10.7 %psum.119 = bf16[24,768]{1,0:T(8,128)(2,1)S(1)} all-reduce(bf16[24,768]{1,0:T(8,128)(2,1)S(1)} %convert_element_type.129), channel_id=1, replica_groups=mesh['rows'=8,'seq'=4] {'seq'}, use_global_device_ids=true, to_apply=%region_7.8 | all-reduce | flops 18432 | bytes 73728 | tf_op jit(solution)/shard_map/psum | solution.py:96
  127.3 31.1 %all_gather.11 = bf16[192,768]{1,0:T(8,128)(2,1)S(1)} all-gather(bf16[24,768]{1,0:T(8,128)(2,1)S(1)} %psum.119), channel_id=1, replica_groups=mesh['rows'=8,'seq'=4] {'rows'}, dimensions={0}, use_global_device_ids=true | all-gather | bytes 331776 | tf_op jit(solution)/shard_map/all_gather | solution.py:97
  173.9 8.8 scatter_custom_fusion
  182.7 63.1 %reduce-scatter.16.cloned.1.call-done = f32[24,768]{1,0:T(8,128)} async-done(((f32[192,768]{1,0:T(8,128)}), f32[24,768]{1,0:T(8,128)}) %reduce-scatter.16.cloned.1.call-update) | async-done | bytes 73744 | tf_op jit(solution)/shard_map/reduce_scatter | solution.py:107
  247.5 31.6 %all-reduce.15.cloned.1.call-done = f32[4,6,768]{2,1,0:T(8,128)} async-done(((f32[4,6,768]{2,1,0:T(8,128)}), f32[4,6,768]{2,1,0:T(8,128)}) %all-reduce.15.cloned.1.call-update) | async-done | bytes 73744 | tf_op jit(solution)/shard_map/psum | solution.py:108
  285.7 10.1 convert_reduce_fusion
  304.2 8.1 fusion.57
  312.4 10.6 %fusion.90 = f32[4,12,128,512]{3,2,1,0:T(8,128)} fusion(bf16[4,128,12,64]{1,3,2,0:T(8,128)(2,1)S(1)} %bitcast.127, bf16[4,512,12,64]{1,3,2,0:T(8,128)(2,1)} %bitcast.125), kind=kOutput, calls=%fused_computation.149 | convolution fusion | flops 402653184 | bytes 16515072 | tf_op jit(solution)/shard_map/rqhd,rkhd->rhqk/dot_general | solution.py:134
  323.0 45.0 %fusion.6 = f32[4,12,64,512]{3,2,1,0:T(8,128)} fusion(bf16[4,128,12,64]{1,3,2,0:T(8,128)(2,1)S(1)} %bitcast.130, f32[4,12,128,512]{3,2,1,0:T(8,128)} %fusion.90, f32[4,12,128,512]{3,2,1,0:T(8,128)} %copy-done.2, f32[4,12,128]{2,1,0:T(8,128)S(1)} %copy-done.29, pred[4,128,512]{2,1,0:T(8,128)(4,1)S(1)} %copy-done.11), kind=kOutput, calls=%fused_computation.11 | convolution fusion | flops 437262848 | bytes 32530432 | tf_op jit(solution)/shard_map/rhqk,rqhd->rkhd/dot_general | solution.py:142
  368.1 53.1 %convert_reduce_fusion.4 = (f32[12,64]{1,0:T(8,128)S(1)}, bf16[4,12,64,128]{3,2,1,0:T(8,128)(2,1)}) fusion(bf16[4,512,12,64]{1,3,2,0:T(8,128)(2,1)} %bitcast.123, f32[4,12,128,512]{3,2,1,0:T(8,128)} %fusion.90, f32[4,12,128]{2,1,0:T(8,128)S(1)} %copy-done.29, f32[4,12,128,512]{3,2,1,0:T(8,128)} %copy-done.2, pred[4,128,512]{2,1,0:T(8,128)(4,1)S(1)} %copy-done.11), kind=kOutput, calls=%fused_computation.59 | convolution fusion | flops 438441728 | bytes 29387776 | tf_op jit(solution)/shard_map/rhqk,rkhd->rqhd/dot_general | solution.py:140
  448.2 8.2 convolution_bitcast_fusion
  456.4 11.7 %reduce-scatter.28.cloned.1.call-done = f32[192,768]{1,0:T(8,128)} async-done(((f32[768,768]{1,0:T(8,128)}), f32[192,768]{1,0:T(8,128)}) %reduce-scatter.28.cloned.1.call-update) | async-done | bytes 589840
  470.4 33.6 %reduce-scatter.32.cloned.1.call-done = f32[192,768]{1,0:T(8,128)} async-done(((f32[768,768]{1,0:T(8,128)}), f32[192,768]{1,0:T(8,128)}) %reduce-scatter.32.cloned.1.call-update) | async-done | bytes 589840
  506.2 34.0 %reduce-scatter.30.cloned.1.call-done = f32[192,768]{1,0:T(8,128)} async-done(((f32[768,768]{1,0:T(8,128)}), f32[192,768]{1,0:T(8,128)}) %reduce-scatter.30.cloned.1.call-update) | async-done | bytes 589840
  542.4 33.5 %reduce-scatter.22.cloned.1.call-done = f32[192,768]{1,0:T(8,128)} async-done(((f32[768,768]{1,0:T(8,128)}), f32[192,768]{1,0:T(8,128)}) %reduce-scatter.22.cloned.1.call-update) | async-done | bytes 589840 | tf_op jit(solution)/shard_map/reduce_scatter | solution.py:187
  575.9 81.0 %reduce-scatter.24.cloned.1.call-done = f32[192,3072]{1,0:T(8,128)} async-done(((f32[768,3072]{1,0:T(8,128)}), f32[192,3072]{1,0:T(8,128)}) %reduce-scatter.24.cloned.1.call-update) | async-done | bytes 2359312 | tf_op jit(solution)/shard_map/reduce_scatter | solution.py:191
  656.9 80.9 %reduce-scatter.26.cloned.1.call-done = f32[768,768]{1,0:T(8,128)} async-done(((f32[3072,768]{1,0:T(8,128)}), f32[768,768]{1,0:T(8,128)}) %reduce-scatter.26.cloned.1.call-update) | async-done | bytes 2359312 | tf_op jit(solution)/shard_map/reduce_scatter | solution.py:193
  745.5 11.6 %all-reduce.11 = (f32[768]{0:T(1024)S(1)}, f32[768]{0:T(1024)S(1)}, f32[768]{0:T(1024)S(1)}, f32[768]{0:T(1024)S(1)}, f32[768]{0:T(1024)S(1)}, /*index=5*/f32[30...) all-reduce(f32[768]{0:T(1024)S(1)} %reduce_sum.246, ...), channel_id=6, replica_groups=mesh['rows'=8,'seq'=4] {'seq'}, use_global_device_ids=true, to_apply=%region_24.25.clone | all-reduce | flops 9216 | bytes 73728
  757.7 39.8 %all-reduce.9 = (f32[192]{0:T(256)}, f32[192]{0:T(256)}, f32[192]{0:T(256)}, f32[192]{0:T(256)}, f32[192]{0:T(256)}, /*index=5*/f32[768]{0:T(1024)}, f32[192]{0:T(256)}, f32[192]{0:T(256)}, f32[192]{0:T(256)}) all-reduce(f32[192]{0:T(256)S(1)} %dynamic-slice.1, ...), channel_id=1, replica_groups=mesh['rows'=8,'seq'=4] {'rows'}, use_global_device_ids=true, to_apply=%region_25.26 | all-reduce | flops 2304 | bytes 18432 | tf_op jit(solution)/shard_map/psum | solution.py:198
  803.6 194.2 %all-reduce.17.cloned.1.call-done = (f32[192,768]{0,1:T(8,128)}, f32[192,768]{0,1:T(8,128)}, f32[192,768]{0,1:T(8,128)}, f32[192,768]{1,0:T(8,128)}, f32[192,3072]{1,0:T(8,128)}, /*index=5*/f32[768,768]{1,0:T(8,128)}) async-done(((f32[192,768]{0,1:T(8,128)}, f32[192,768]{0,1:T(8,128)}, f32[192,768]{0,1:T(8,128)}, f32[192,768]{1,0:T(8,128)}, f32[192,3072]{1,0:T(8,128)}, /*index=5*/f32[768,768]{1,0:T(8,128)}), ...) | async-done | bytes 7077904 | tf_op jit(solution)/shard_map/psum | solution.py:198
  (246 shorter events, 137.6 us)
Async XLA Ops:
  7.2 79.2 %copy-start = (bf16[768,768]{1,0:T(8,128)(2,1)S(1)}, bf16[768,768]{1,0:T(8,128)(2,1)}, u32[]{:S(2)}) copy-start(bf16[768,768]{1,0:T(8,128)(2,1)} %param.26) | copy-start | bytes 3538948
  7.3 34.8 %all-gather.5.cloned.1.call-start = ((), (), s32[]{:S(2)}) async-start(), calls=%async_computation.10 | async-start | bytes 3932160 | tf_op jit(solution)/shard_map/all_gather | solution.py:65
  10.7 62.1 %all-gather.3.cloned.1.call-start = ((), (), s32[]{:S(2)}) async-start(), calls=%async_computation.9 | async-start | bytes 3932160 | tf_op jit(solution)/shard_map/all_gather | solution.py:66
  13.9 232.0 %reduce-scatter.16.cloned.1.call-start = ((), (), s32[]{:S(2)}) async-start(), calls=%async_computation.11 | async-start | bytes 663552 | tf_op jit(solution)/shard_map/reduce_scatter | solution.py:107
  18.7 96.8 %copy-start.54 = (s32[128]{0:T(128)}, s32[128]{0:T(128)S(1)}, u32[]{:S(2)}) copy-start(s32[128]{0:T(128)S(1)} %iota_add_fusion) | copy-start | bytes 1540
  19.6 57.8 %copy-start.10 = (pred[4,128,512]{2,1,0:T(8,128)(4,1)}, pred[4,128,512]{2,1,0:T(8,128)(4,1)S(1)}, u32[]{:S(2)}) copy-start(pred[4,128,512]{2,1,0:T(8,128)(4,1)S(1)} %broadcast_compare_fusion) | copy-start | bytes 786436
  163.6 115.5 %copy-start.24 = (bf16[4,128,768]{2,1,0:T(8,128)(2,1)S(1)}, bf16[4,128,768]{2,1,0:T(8,128)(2,1)}, u32[]{:S(2)}) copy-start(bf16[4,128,768]{2,1,0:T(8,128)(2,1)} %param.39) | copy-start | bytes 2359300
  182.7 96.4 %all-reduce.15.cloned.1.call-start = ((), (), s32[]{:S(2)}) async-start(), calls=%async_computation.12 | async-start | bytes 196608 | tf_op jit(solution)/shard_map/psum | solution.py:108
  247.4 177.8 %reduce-scatter.20.cloned.1.call-start = ((), (), s32[]{:S(2)}) async-start(), calls=%async_computation.14 | async-start | bytes 7864320 | tf_op jit(solution)/shard_map/reduce_scatter | solution.py:150
  312.4 119.6 %reduce-scatter.18.cloned.1.call-start = ((), (), s32[]{:S(2)}) async-start(), calls=%async_computation.13 | async-start | bytes 7864320 | tf_op jit(solution)/shard_map/reduce_scatter | solution.py:149
  368.1 100.1 %reduce-scatter.28.cloned.1.call-start = ((), (), s32[]{:S(2)}) async-start(), calls=%async_computation.18 | async-start | bytes 2949120
  425.2 78.8 %reduce-scatter.32.cloned.1.call-start = ((), (), s32[]{:S(2)}) async-start(), calls=%async_computation.20 | async-start | bytes 2949120
  429.4 110.8 %reduce-scatter.30.cloned.1.call-start = ((), (), s32[]{:S(2)}) async-start(), calls=%async_computation.19 | async-start | bytes 2949120
  436.2 139.7 %reduce-scatter.22.cloned.1.call-start = ((), (), s32[]{:S(2)}) async-start(), calls=%async_computation.15 | async-start | bytes 2949120 | tf_op jit(solution)/shard_map/reduce_scatter | solution.py:187
  439.9 217.0 %reduce-scatter.24.cloned.1.call-start = ((), (), s32[]{:S(2)}) async-start(), calls=%async_computation.16 | async-start | bytes 11796480 | tf_op jit(solution)/shard_map/reduce_scatter | solution.py:191
  447.1 290.8 %reduce-scatter.26.cloned.1.call-start = ((), (), s32[]{:S(2)}) async-start(), calls=%async_computation.17 | async-start | bytes 11796480 | tf_op jit(solution)/shard_map/reduce_scatter | solution.py:193
  456.4 541.4 %all-reduce.17.cloned.1.call-start = ((), (), s32[]{:S(2)}) async-start(), calls=%async_computation.21 | async-start | bytes 15335424 | tf_op jit(solution)/shard_map/psum | solution.py:198
  506.2 231.6 %copy-start.58 = (u32[32]{0:T(128)S(1)}, u32[32]{0:T(128)}, u32[]{:S(2)}) copy-start(u32[32]{0:T(128)} %constant.110) | copy-start | bytes 388
  506.2 233.7 %copy-start.49 = (f32[32]{0:T(128)S(1)}, f32[32]{0:T(128)}, u32[]{:S(2)}) copy-start(f32[32]{0:T(128)} %reduce_max.20) | copy-start | bytes 388
  506.2 233.7 %copy-start.53 = (f32[32]{0:T(128)S(1)}, f32[32]{0:T(128)}, u32[]{:S(2)}) copy-start(f32[32]{0:T(128)} %get-tuple-element.117) | copy-start | bytes 388
  506.2 234.3 %copy-start.27 = (bf16[4,12,64,128]{3,2,1,0:T(8,128)(2,1)S(1)}, bf16[4,12,64,128]{3,2,1,0:T(8,128)(2,1)}, u32[]{:S(2)}) copy-start(bf16[4,12,64,128]{3,2,1,0:T(8,128)(2,1)} %get-tuple-element.162) | copy-start | bytes 2359300
  740.5 59.7 %copy-start.6 = (f32[4,128,768]{2,1,0:T(8,128)S(1)}, f32[4,128,768]{2,1,0:T(8,128)}, u32[]{:S(2)}) copy-start(f32[4,128,768]{2,1,0:T(8,128)} %copy-done.5) | copy-start | bytes 4718596
  740.5 59.7 %copy-start.23 = (bf16[768,768]{1,0:T(8,128)(2,1)S(1)}, bf16[768,768]{1,0:T(8,128)(2,1)}, u32[]{:S(2)}) copy-start(bf16[768,768]{1,0:T(8,128)(2,1)} %param.24) | copy-start | bytes 3538948
  740.5 59.7 %copy-start.44 = (f32[4,128]{1,0:T(4,128)S(1)}, f32[4,128]{1,0:T(4,128)}, u32[]{:S(2)}) copy-start(f32[4,128]{1,0:T(4,128)} %copy-done.43) | copy-start | bytes 6148
  (52 other events, 456.6 us)
Sparse Core Ops, SparseCore 0:
  10.8 31.2 all-gather.4
  44.2 28.5 all-gather.2
  182.8 63.0 reduce-scatter.15
  248.7 30.3 all-reduce.14
  312.5 58.4 reduce-scatter.19
  373.6 58.3 reduce-scatter.17
  435.1 33.0 reduce-scatter.27
  470.9 33.0 reduce-scatter.31
  507.1 33.0 reduce-scatter.29
  542.7 33.0 reduce-scatter.21
  578.5 78.3 reduce-scatter.23
  659.4 78.4 reduce-scatter.25
  743.7 254.0 all-reduce.16
where the time goes:
time: 1020 us
  waiting for transfers between devices  605 us (59%)
  matrix products  204 us (20%)
  blocking collectives  93.1 us (9%)
  local copies, waits for them, and re-layouts  54.3 us (5%)
  other arithmetic  44.1 us (4%)
  between operations  16.3 us (2%)
    psum x1, waiting for transfers between devices, per_device(): lax.psum((part_wq, part_bq, part_wk, part_wv, part_bv, part_wo, part_bo,...  194 us
    reduce_scatter x1, waiting for transfers between devices, per_device(): lax.psum_scatter(grad_w_up, 'seq', scatter_dimension=0, tiled=True)  81 us
    reduce_scatter x1, waiting for transfers between devices, per_device(): lax.psum_scatter(grad_w_down, 'seq', scatter_dimension=0, tiled=True)  80.9 us
    unnamed x16, waiting for transfers between devices  79.5 us
    reduce_scatter x1, waiting for transfers between devices, per_device(): lax.psum_scatter(pool_grad, 'rows', scatter_dimension=0, tiled=True)  63.1 us
    dot_general x1, matrix products, per_device(): jnp.einsum('rhqk,rkhd->rqhd', grad_raw, key_heads, preferred_element_type...  53.1 us
    dot_general x1, matrix products, per_device(): jnp.einsum('rhqk,rqhd->rkhd', grad_raw, query_heads, preferred_element_ty...  45 us
    psum x1, blocking collectives, per_device(): lax.psum((part_wq, part_bq, part_wk, part_wv, part_bv, part_wo, part_bo,...  39.8 us
  transfers between devices with their start and end apart: 13, of which 12 were waited for; matrix products, arithmetic and copies ran while one was open for 18% of the time, Pallas kernels for 0%

commit v1 on v0

v1 whole, which is shorter than its diff:
```python
import functools

import jax
import jax.numpy as jnp
from jax import lax
from jax.experimental import pallas as pl
from jax.experimental.pallas import tpu as pltpu
from jax.sharding import PartitionSpec as P

HEADS = 12
HEAD = 64
PASS = 6
CH = 32
SLOT = 8
GROUP = 4

norm_eps = 1e-05
f32 = jnp.float32
bf16 = jnp.bfloat16
VMEM_BYTES = 56 * 1024 * 1024


def params():
    return pltpu.CompilerParams(
        dimension_semantics=None, vmem_limit_bytes=VMEM_BYTES
    )


def nt(a, b):
    return lax.dot_general(a, b, (((1,), (1,)), ((), ())), preferred_element_type=f32)


def tn(a, b):
    return lax.dot_general(a, b, (((0,), (0,)), ((), ())), preferred_element_type=f32)


def nn(a, b):
    return jnp.dot(a, b, preferred_element_type=f32)


def stats(values):
    center = values - jnp.mean(values, -1, keepdims=True)
    inv = lax.rsqrt(jnp.mean(center * center, -1, keepdims=True) + norm_eps)
    return center * inv, inv


def norm_back(grad, xhat, inv, gain):
    gx = grad * gain
    return inv * (
        gx - jnp.mean(gx, -1, keepdims=True) - xhat * jnp.mean(gx * xhat, -1, keepdims=True)
    )


def true_places(own_seq, count, piece, axis):
    shape = (count, 1) if axis == 0 else (1, count)
    local = lax.broadcasted_iota(jnp.int32, shape, axis)
    block = local // piece
    return (block ^ own_seq) * piece + (local - block * piece)


def segments(sc_ref, places):
    total = jnp.zeros(places.shape, jnp.int32)
    for j in range(PASS):
        total += (sc_ref[1 + j] <= places).astype(jnp.int32)
    return total


def attention_kernel(
    piece, sc_ref, x_ref, wq_ref, wk_ref, wv_ref, bq_ref, bv_ref, wo_ref, bo_ref, go_ref, so_ref,
    q_ref, k_ref, v_ref, ctxt_ref, lse_ref, resid_ref, hid_ref, hidt_ref, xt_ref,
    acc, ctx,
):
    step = pl.program_id(0)
    length = x_ref.shape[0]
    x = x_ref[...]
    q_ref[...] = (nn(x, wq_ref[...]) + bq_ref[...]).astype(bf16)
    k_ref[...] = nn(x, wk_ref[...]).astype(bf16)
    v_ref[...] = (nn(x, wv_ref[...]) + bv_ref[...]).astype(bf16)

    @pl.when(step == 0)
    def _():
        xt_ref[...] = x.T
        lse_ref[...] = jnp.zeros_like(lse_ref)
        acc[...] = jnp.zeros_like(acc)

    seg_col = segments(sc_ref, true_places(sc_ref[0], length, piece, 0))
    seg_row = segments(sc_ref, true_places(sc_ref[0], length, piece, 1))
    lanes = lax.broadcasted_iota(jnp.int32, (1, 128), 1)
    for h in range(GROUP):
        cols = slice(h * HEAD, (h + 1) * HEAD)
        k = k_ref[:, cols]
        v = v_ref[:, cols]
        for b in range(length // 128):
            rows = slice(b * 128, (b + 1) * 128)
            raw = nt(q_ref[rows, cols], k)
            scores = jnp.where(seg_col[rows] == seg_row, raw * (HEAD ** (-0.5)), -1e30)
            top = jnp.max(scores, -1, keepdims=True)
            e = jnp.exp(scores - top)
            total = jnp.sum(e, -1, keepdims=True)
            p = (e * (1.0 / total)).astype(bf16)
            ctx[rows, cols] = nn(p, v).astype(bf16)
            lse = top + jnp.log(total)
            lse_ref[rows, :] = jnp.where(lanes == step * GROUP + h, lse, lse_ref[rows, :])
    c = ctx[...]
    ctxt_ref[...] = c.T
    acc[...] += nn(c, wo_ref[...])

    @pl.when(step == pl.num_programs(0) - 1)
    def _():
        resid = x_ref[...].astype(f32) + (acc[...] + bo_ref[...])
        resid_ref[...] = resid
        xhat, _ = stats(resid)
        hid = (xhat * go_ref[...] + so_ref[...]).astype(bf16)
        hid_ref[...] = hid
        hidt_ref[...] = hid.T


def attention_forward(sc, x, wq, wk, wv, bq, bv, wo, bo, go, so, piece):
    length, d = x.shape
    wide = GROUP * HEAD
    steps = d // wide
    whole = lambda r, c: pl.BlockSpec((r, c), lambda i, s: (0, 0))
    cols = lambda r: pl.BlockSpec((r, wide), lambda i, s: (0, i))
    rows = lambda c: pl.BlockSpec((wide, c), lambda i, s: (i, 0))
    return pl.pallas_call(
        functools.partial(attention_kernel, piece),
        grid_spec=pltpu.PrefetchScalarGridSpec(
            num_scalar_prefetch=1,
            grid=(steps,),
            in_specs=[
                whole(length, d), cols(d), cols(d), cols(d), cols(1), cols(1), rows(d),
                whole(1, d), whole(1, d), whole(1, d),
            ],
            out_specs=[
                cols(length), cols(length), cols(length), rows(length), whole(length, 128),
                whole(length, d), whole(length, d), whole(d, length), whole(d, length),
            ],
            scratch_shapes=[pltpu.VMEM((length, d), f32), pltpu.VMEM((length, wide), bf16)],
        ),
        out_shape=[
            jax.ShapeDtypeStruct((length, d), bf16),
            jax.ShapeDtypeStruct((length, d), bf16),
            jax.ShapeDtypeStruct((length, d), bf16),
            jax.ShapeDtypeStruct((d, length), bf16),
            jax.ShapeDtypeStruct((length, 128), f32),
            jax.ShapeDtypeStruct((length, d), f32),
            jax.ShapeDtypeStruct((length, d), bf16),
            jax.ShapeDtypeStruct((d, length), bf16),
            jax.ShapeDtypeStruct((d, length), bf16),
        ],
        compiler_params=params(),
        name="attention_forward",
    )(sc, x, wq, wk, wv, bq, bv, wo, bo, go, so)


def feed_kernel(
    piece, sc_ref, hid_ref, wu_ref, bu_ref, wd_ref, bd_ref, gt_ref, st_ref,
    actt_ref, slope_ref, resid_ref, mixed_ref, pool_ref,
    acc,
):
    step = pl.program_id(0)
    length = hid_ref.shape[0]
    up = nn(hid_ref[...], wu_ref[...]) + bu_ref[...]
    phi_cum = 0.5 * (1.0 + lax.erf(up * (2.0 ** -0.5)))
    density = jnp.exp(-0.5 * up * up) * (0.3989422804014327)
    slope_ref[0] = phi_cum + up * density
    act = (up * phi_cum).astype(bf16)
    actt_ref[...] = act.T
    part = nn(act, wd_ref[...])

    @pl.when(step == 0)
    def _():
        acc[...] = part

    @pl.when(step > 0)
    def _():
        acc[...] += part

    @pl.when(step == pl.num_programs(0) - 1)
    def _():
        resid = hid_ref[...].astype(f32) + acc[...] + bd_ref[...]
        resid_ref[...] = resid
        xhat, _ = stats(resid)
        mixed = (xhat * gt_ref[...] + st_ref[...]).astype(bf16)
        mixed_ref[...] = mixed
        places = true_places(sc_ref[0], length, piece, 1)
        slot = lax.broadcasted_iota(jnp.int32, (SLOT, 1), 0)
        start = jnp.full((SLOT, 1), -1, jnp.int32)
        for j in range(PASS):
            start = jnp.where(slot == j, sc_ref[1 + j], start)
        pool_ref[...] = nn((places == start).astype(f32).astype(bf16), mixed)


def feed_forward(sc, hid, wu, bu, wd, bd, gt, st, piece, wide):
    length, d = hid.shape
    ff = wu.shape[1]
    steps = ff // wide
    whole = lambda r, c: pl.BlockSpec((r, c), lambda i, s: (0, 0))
    return pl.pallas_call(
        functools.partial(feed_kernel, piece),
        grid_spec=pltpu.PrefetchScalarGridSpec(
            num_scalar_prefetch=1,
            grid=(steps,),
            in_specs=[
                whole(length, d),
                pl.BlockSpec((d, wide), lambda i, s: (0, i)),
                pl.BlockSpec((1, wide), lambda i, s: (0, i)),
                pl.BlockSpec((wide, d), lambda i, s: (i, 0)),
                whole(1, d), whole(1, d), whole(1, d),
            ],
            out_specs=[
                pl.BlockSpec((wide, length), lambda i, s: (i, 0)),
                pl.BlockSpec((1, length, wide), lambda i, s: (i, 0, 0)),
                whole(length, d), whole(length, d), whole(SLOT, d),
            ],
            scratch_shapes=[pltpu.VMEM((length, d), f32)],
        ),
        out_shape=[
            jax.ShapeDtypeStruct((ff, length), bf16),
            jax.ShapeDtypeStruct((steps, length, wide), f32),
            jax.ShapeDtypeStruct((length, d), f32),
            jax.ShapeDtypeStruct((length, d), bf16),
            jax.ShapeDtypeStruct((SLOT, d), f32),
        ],
        compiler_params=params(),
        name="feed_forward",
    )(sc, hid, wu, bu, wd, bd, gt, st)


def loss_kernel(q_ref, pos_ref, pool_ref, loss_ref, grad_ref):
    step = pl.program_id(0)
    queries = q_ref[...]
    logits = nt(queries, pool_ref[...])
    count, width = logits.shape
    lanes = lax.broadcasted_iota(jnp.int32, (1, width), 1)
    pos = pos_ref[...]
    first = (pos[:, 0:1] == lanes).astype(f32)
    times = first
    for c in range(1, CH):
        times += (pos[:, c : c + 1] == lanes).astype(f32)
    held = times > 0.0
    top = jnp.max(jnp.where(held, logits, -jnp.inf), -1, keepdims=True)
    e = jnp.where(held, times * jnp.exp(jnp.minimum(logits - top, 0.0)), 0.0)
    total = jnp.sum(e, -1, keepdims=True)
    positive = jnp.sum(first * logits, -1, keepdims=True)
    loss_ref[...] = top + jnp.log(total) - positive
    grad = e[:, :128] * (1.0 / total) - first[:, :128]
    high = grad.astype(bf16)
    lower = (grad - high.astype(f32)).astype(bf16)
    part = (tn(high, queries) + tn(lower, queries))[:SLOT]

    @pl.when(step == 0)
    def _():
        grad_ref[...] = part

    @pl.when(step > 0)
    def _():
        grad_ref[...] += part


def retrieval(queries, pos, pooled):
    count, d = queries.shape
    block = 256
    return pl.pallas_call(
        loss_kernel,
        grid=(count // block,),
        in_specs=[
            pl.BlockSpec((block, d), lambda i: (i, 0)),
            pl.BlockSpec((block, CH), lambda i: (i, 0)),
            pl.BlockSpec(pooled.shape, lambda i: (0, 0)),
        ],
        out_specs=[
            pl.BlockSpec((block, 1), lambda i: (i, 0)),
            pl.BlockSpec((SLOT, d), lambda i: (0, 0)),
        ],
        out_shape=[
            jax.ShapeDtypeStruct((count, 1), f32),
            jax.ShapeDtypeStruct((SLOT, d), f32),
        ],
        compiler_params=params(),
        name="retrieval",
    )(queries, pos, pooled)


def norm_two_kernel(piece, sc_ref, cot_ref, gp_ref, resid_ref, gt_ref, gd_ref, gr_ref, sums_ref):
    length = cot_ref.shape[0]
    places = true_places(sc_ref[0], length, piece, 0)
    grad = cot_ref[...].astype(f32)
    for j in range(PASS):
        grad += jnp.where(places == sc_ref[1 + j], gp_ref[j : j + 1, :], 0.0)
    xhat, inv = stats(resid_ref[...])
    back = norm_back(grad, xhat, inv, gt_ref[...])
    gr_ref[...] = back
    down = back.astype(bf16)
    gd_ref[...] = down
    sums_ref[0:1, :] = jnp.sum(down.astype(f32), 0, keepdims=True)
    sums_ref[1:2, :] = jnp.sum(grad * xhat, 0, keepdims=True)
    sums_ref[2:3, :] = jnp.sum(grad, 0, keepdims=True)


def norm_two_back(sc, cot, gp, resid, gain, piece):
    length, d = cot.shape
    whole = pl.BlockSpec(memory_space=pltpu.VMEM)
    return pl.pallas_call(
        functools.partial(norm_two_kernel, piece),
        in_specs=[pl.BlockSpec(memory_space=pltpu.SMEM)] + [whole] * 4,
        out_specs=[whole] * 3,
        out_shape=[
            jax.ShapeDtypeStruct((length, d), bf16),
            jax.ShapeDtypeStruct((length, d), f32),
            jax.ShapeDtypeStruct((SLOT, d), f32),
        ],
        compiler_params=params(),
        name="norm_two_back",
    )(sc, cot, gp, resid, gain)


def feed_back_kernel(
    gd_ref, gr_ref, wd_ref, wu_ref, slope_ref, resid_ref, go_ref, wo_ref,
    gup_ref, bup_ref, gr1_ref, gab_ref, gctx_ref, sums_ref,
    acc,
):
    step = pl.program_id(0)
    gact = nt(gd_ref[...], wd_ref[...])
    gup = (gact * slope_ref[0]).astype(bf16)
    gup_ref[0] = gup
    bup_ref[0] = jnp.sum(gup.astype(f32), 0, keepdims=True)
    part = nt(gup, wu_ref[...])

    @pl.when(step == 0)
    def _():
        acc[...] = gr_ref[...] + part

    @pl.when(step > 0)
    def _():
        acc[...] += part

    @pl.when(step == pl.num_programs(0) - 1)
    def _():
        grad = acc[...]
        xhat, inv = stats(resid_ref[...])
        back = norm_back(grad, xhat, inv, go_ref[...])
        gr1_ref[...] = back
        gab = back.astype(bf16)
        gab_ref[...] = gab
        gctx_ref[...] = nt(gab, wo_ref[...]).astype(bf16)
        sums_ref[0:1, :] = jnp.sum(gab.astype(f32), 0, keepdims=True)
        sums_ref[1:2, :] = jnp.sum(grad * xhat, 0, keepdims=True)
        sums_ref[2:3, :] = jnp.sum(grad, 0, keepdims=True)


def feed_back(gd, gr, wd, wu, slope, resid, go, wo):
    length, d = gd.shape
    steps, _, wide = slope.shape
    whole = lambda r, c: pl.BlockSpec((r, c), lambda i: (0, 0))
    return pl.pallas_call(
        feed_back_kernel,
        grid=(steps,),
        in_specs=[
            whole(length, d), whole(length, d),
            pl.BlockSpec((wide, d), lambda i: (i, 0)),
            pl.BlockSpec((d, wide), lambda i: (0, i)),
            pl.BlockSpec((1, length, wide), lambda i: (i, 0, 0)),
            whole(length, d), whole(1, d), whole(d, d),
        ],
        out_specs=[
            pl.BlockSpec((1, length, wide), lambda i: (i, 0, 0)),
            pl.BlockSpec((1, 1, wide), lambda i: (i, 0, 0)),
            whole(length, d), whole(length, d), whole(length, d), whole(SLOT, d),
        ],
        out_shape=[
            jax.ShapeDtypeStruct((steps, length, wide), bf16),
            jax.ShapeDtypeStruct((steps, 1, wide), f32),
            jax.ShapeDtypeStruct((length, d), f32),
            jax.ShapeDtypeStruct((length, d), bf16),
            jax.ShapeDtypeStruct((length, d), bf16),
            jax.ShapeDtypeStruct((SLOT, d), f32),
        ],
        scratch_shapes=[pltpu.VMEM((length, d), f32)],
        compiler_params=params(),
        name="feed_back",
    )(gd, gr, wd, wu, slope, resid, go, wo)


def attention_back_kernel(
    piece, sc_ref, q_ref, k_ref, v_ref, gctx_ref, lse_ref, wq_ref, wk_ref, wv_ref, gr_ref,
    gqkv_ref, gtok_ref, sums_ref,
    acc, prob, graw,
):
    step = pl.program_id(0)
    length = q_ref.shape[0]
    seg_col = segments(sc_ref, true_places(sc_ref[0], length, piece, 0))
    seg_row = segments(sc_ref, true_places(sc_ref[0], length, piece, 1))
    lanes = lax.broadcasted_iota(jnp.int32, (1, 128), 1)
    scale = HEAD ** (-0.5)
    for h in range(GROUP):
        cols = slice(h * HEAD, (h + 1) * HEAD)
        q = q_ref[:, cols]
        k = k_ref[:, cols]
        v = v_ref[:, cols]
        gctx = gctx_ref[:, cols]
        for b in range(length // 128):
            rows = slice(b * 128, (b + 1) * 128)
            lse = jnp.sum(
                jnp.where(lanes == step * GROUP + h, lse_ref[rows, :], 0.0), -1, keepdims=True
            )
            raw = nt(q[rows], k)
            scores = jnp.where(seg_col[rows] == seg_row, raw * scale, -1e30)
            p = jnp.exp(scores - lse)
            prob[rows, :] = p.astype(bf16)
            ga = nt(gctx[rows], v)
            dots = jnp.sum(p * ga, -1, keepdims=True)
            g = (p * (ga - dots) * scale).astype(bf16)
            graw[rows, :] = g
            gqkv_ref[0, rows, cols] = nn(g, k).astype(bf16)
        gqkv_ref[1, :, cols] = tn(graw[...], q).astype(bf16)
        gqkv_ref[2, :, cols] = tn(prob[...], gctx).astype(bf16)
    gq, gk, gv = gqkv_ref[0], gqkv_ref[1], gqkv_ref[2]
    sums_ref[0:1, :] = jnp.sum(gq.astype(f32), 0, keepdims=True)
    sums_ref[1:2, :] = jnp.sum(gv.astype(f32), 0, keepdims=True)
    part = nt(gq, wq_ref[...]) + nt(gk, wk_ref[...]) + nt(gv, wv_ref[...])

    @pl.when(step == 0)
    def _():
        acc[...] = gr_ref[...] + part

    @pl.when(step > 0)
    def _():
        acc[...] += part

    @pl.when(step == pl.num_programs(0) - 1)
    def _():
        gtok_ref[...] = acc[...].astype(bf16)


def attention_back(sc, q, k, v, gctx, lse, wq, wk, wv, gr, piece):
    length, d = q.shape
    wide = GROUP * HEAD
    steps = d // wide
    whole = lambda r, c: pl.BlockSpec((r, c), lambda i, s: (0, 0))
    cols = lambda r: pl.BlockSpec((r, wide), lambda i, s: (0, i))
    return pl.pallas_call(
        functools.partial(attention_back_kernel, piece),
        grid_spec=pltpu.PrefetchScalarGridSpec(
            num_scalar_prefetch=1,
            grid=(steps,),
            in_specs=[
                cols(length), cols(length), cols(length), cols(length), whole(length, 128),
                cols(d), cols(d), cols(d), whole(length, d),
            ],
            out_specs=[
                pl.BlockSpec((3, length, wide), lambda i, s: (0, 0, i)),
                whole(length, d), cols(SLOT),
            ],
            scratch_shapes=[
                pltpu.VMEM((length, d), f32),
                pltpu.VMEM((length, length), bf16),
                pltpu.VMEM((length, length), bf16),
            ],
        ),
        out_shape=[
            jax.ShapeDtypeStruct((3, length, d), bf16),
            jax.ShapeDtypeStruct((length, d), bf16),
            jax.ShapeDtypeStruct((SLOT, d), f32),
        ],
        compiler_params=params(),
        name="attention_back",
    )(sc, q, k, v, gctx, lse, wq, wk, wv, gr)


def weight_send_kernel(sc_ref, lo_ref, lp_ref, go_ref, gp_ref, out_ref):
    out_ref[0] = (nn(lo_ref[0], go_ref[0]) + nn(lp_ref[0], gp_ref[0])).astype(bf16)


def weight_keep_kernel(sc_ref, lo_ref, lp_ref, go_ref, gp_ref, recv_ref, out_ref):
    total = nn(lo_ref[0], go_ref[0]) + nn(lp_ref[0], gp_ref[0]) + recv_ref[0].astype(f32)
    out_ref[0] = total.astype(bf16)


def weight_split_kernel(own_slot, sc_ref, lo_ref, lp_ref, go_ref, gp_ref, recv_ref, keep_ref, send_ref):
    step = pl.program_id(0)
    total = nn(lo_ref[0], go_ref[0]) + nn(lp_ref[0], gp_ref[0]) + recv_ref[0].astype(f32)
    half = total.shape[0] // 2
    for h in range(2):
        slot = (2 * step + h) ^ sc_ref[own_slot]
        rows = total[h * half : (h + 1) * half]

        @pl.when(slot < 4)
        def _():
            keep_ref[slot] = rows

        @pl.when(slot >= 4)
        def _():
            send_ref[slot - 4] = rows.astype(bf16)


def weight_specs(lo, lp, go, gp, other, steps, walk_rows):
    rows = lo.shape[1] // (steps if walk_rows else 1)
    length = lo.shape[2]
    wide = go.shape[2]
    r = (lambda i: i) if walk_rows else (lambda i: 0)
    g = (lambda i: 0) if walk_rows else (lambda i: i)
    x = (lambda s: 1 - s[0]) if other else (lambda s: s[0])
    return [
        pl.BlockSpec((1, rows, length), lambda i, s: (2 * x(s) + s[1], r(i), 0)),
        pl.BlockSpec((1, rows, length), lambda i, s: (x(s), r(i), 0)),
        pl.BlockSpec((1, length, wide), lambda i, s: (g(i), 0, 0)),
        pl.BlockSpec((1, length, wide), lambda i, s: (g(i), 0, 0)),
    ], rows, wide


def weight_send(sc, lo, lp, go, gp, steps, walk_rows, name):
    specs, rows, wide = weight_specs(lo, lp, go, gp, True, steps, walk_rows)
    block = pl.BlockSpec((1, rows, wide), lambda i, s: (i, 0, 0))
    return pl.pallas_call(
        weight_send_kernel,
        grid_spec=pltpu.PrefetchScalarGridSpec(
            num_scalar_prefetch=1, grid=(steps,), in_specs=specs, out_specs=block
        ),
        out_shape=jax.ShapeDtypeStruct((steps, rows, wide), bf16),
        compiler_params=params(),
        name=name,
    )(sc, lo, lp, go, gp)


def weight_keep(sc, lo, lp, go, gp, recv, steps, walk_rows, name):
    specs, rows, wide = weight_specs(lo, lp, go, gp, False, steps, walk_rows)
    block = pl.BlockSpec((1, rows, wide), lambda i, s: (i, 0, 0))
    return pl.pallas_call(
        weight_keep_kernel,
        grid_spec=pltpu.PrefetchScalarGridSpec(
            num_scalar_prefetch=1, grid=(steps,), in_specs=specs + [block], out_specs=block
        ),
        out_shape=jax.ShapeDtypeStruct((steps, rows, wide), bf16),
        compiler_params=params(),
        name=name,
    )(sc, lo, lp, go, gp, recv)


def weight_split(sc, lo, lp, go, gp, recv, own_slot, walk_rows, name):
    steps = 4
    specs, rows, wide = weight_specs(lo, lp, go, gp, False, steps, walk_rows)
    block = pl.BlockSpec((1, rows, wide), lambda i, s: (i, 0, 0))
    half = pl.BlockSpec((4, rows // 2, wide), lambda i, s: (0, 0, 0))
    return pl.pallas_call(
        functools.partial(weight_split_kernel, own_slot),
        grid_spec=pltpu.PrefetchScalarGridSpec(
            num_scalar_prefetch=1, grid=(steps,), in_specs=specs + [block], out_specs=[half, half]
        ),
        out_shape=[
            jax.ShapeDtypeStruct((4, rows // 2, wide), f32),
            jax.ShapeDtypeStruct((4, rows // 2, wide), bf16),
        ],
        compiler_params=params(),
        name=name,
    )(sc, lo, lp, go, gp, recv)


def place_kernel(own_slot, wide_out, sc_ref, near_ref, far_ref, out_ref):
    own = sc_ref[own_slot]
    rows, wide = near_ref.shape[1:]
    for k in range(8):
        piece = (near_ref[k] if k < 4 else far_ref[k - 4]).astype(f32)
        spot = own ^ k
        if wide_out:
            top = pl.multiple_of((spot % 2) * rows, rows)
            left = pl.multiple_of((spot // 2) * wide, wide)
            out_ref[pl.ds(top, rows), pl.ds(left, wide)] = piece
        else:
            out_ref[pl.ds(pl.multiple_of(spot * rows, rows), rows), :] = piece


def place(sc, near, far, own_slot, wide_out, name):
    rows, wide = near.shape[1:]
    shape = (2 * rows, 4 * wide) if wide_out else (8 * rows, wide)
    whole = pl.BlockSpec(memory_space=pltpu.VMEM)
    return pl.pallas_call(
        functools.partial(place_kernel, own_slot, wide_out),
        in_specs=[pl.BlockSpec(memory_space=pltpu.SMEM), whole, whole],
        out_specs=whole,
        out_shape=jax.ShapeDtypeStruct(shape, f32),
        compiler_params=params(),
        name=name,
    )(sc, near, far)


def flip(value, axis, mask):
    count = lax.axis_size(axis)
    return lax.ppermute(value, axis, [(i, i ^ mask) for i in range(count)])


def flip_both(value, row_mask, seq_mask):
    rows, seq = lax.axis_size("rows"), lax.axis_size("seq")
    pairs = [
        (r * seq + s, (r ^ row_mask) * seq + (s ^ seq_mask)) for r in range(rows) for s in range(seq)
    ]
    return lax.ppermute(value, ("rows", "seq"), pairs)


def row_flips():
    count = lax.axis_size("rows")
    assert count >= 8 and count & (count - 1) == 0
    return [1, 2, 6], [1 << b for b in range(3, count.bit_length() - 1)]


def halving(keep, send, order, extra):
    for stage, mask in enumerate(order):
        got = flip(send, "rows", mask).astype(f32) + keep
        if stage < 2:
            cut = got.shape[0] // 2
            keep, send = got[:cut], got[cut:].astype(bf16)
    own = got.astype(bf16)
    for mask in extra:
        own = (own.astype(f32) + flip(own, "rows", mask).astype(f32)).astype(bf16)
    near = own
    for mask in (order[2], order[1]):
        near = jnp.concatenate([near, flip(near, "rows", mask)], 0)
    return near, flip(near, "rows", order[0])


def doubling(value, order):
    for mask in order:
        value = value.astype(bf16)
        value = value.astype(f32) + flip(value, "rows", mask).astype(f32)
    return value


def spread(rows):
    own = lax.axis_index("seq")
    count = lax.axis_size("seq")
    assert rows.shape[0] == count
    pieces = [
        flip(lax.dynamic_index_in_dim(rows, own ^ mask, 0, keepdims=False), "seq", mask)
        if mask
        else lax.dynamic_index_in_dim(rows, own, 0, keepdims=False)
        for mask in range(count)
    ]
    return jnp.concatenate(pieces, 0)


def gather_back(row, count):
    own = lax.axis_index("seq")
    row = row.reshape(count, -1, row.shape[-1])
    out = jnp.zeros_like(row)
    for mask in range(count):
        piece = flip(row[mask], "seq", mask) if mask else row[0]
        out = lax.dynamic_update_index_in_dim(out, piece, own ^ mask, 0)
    return out


def per_device(
    tokens,
    w_query,
    b_query,
    w_key,
    w_value,
    b_value,
    w_out,
    b_out,
    gain_one,
    shift_one,
    w_up,
    b_up,
    w_down,
    b_down,
    gain_two,
    shift_two,
    passage_starts,
    queries,
    choices,
    cotangent,
):
    seq_count = lax.axis_size("seq")
    row_count = lax.axis_size("rows")
    own_s = lax.axis_index("seq")
    own_r = lax.axis_index("rows")
    row_block, piece, d = tokens.shape
    assert row_block == seq_count == 4
    ff = w_up.shape[1]
    core, xside = own_s % 2, own_s // 2
    base, extra = row_flips()
    bit_y = own_r % 2
    bit_b = (own_r // 4) % 2
    bit_a = (own_r // 2) % 2 ^ bit_b
    coord = {base[0]: bit_y, base[1]: bit_a, base[2]: bit_b}
    order_down = [base[1], base[2], base[0]]
    order_up = [base[2], base[0], base[1]]
    slot_of = lambda order: coord[order[0]] * 4 + coord[order[1]] * 2 + coord[order[2]]
    wsc = jnp.stack([xside, core, slot_of(order_down), slot_of(order_up)]).astype(jnp.int32)
    starts = lax.dynamic_index_in_dim(passage_starts, own_s, 0, keepdims=False)
    sc = jnp.concatenate([own_s[None].astype(jnp.int32), starts, jnp.zeros((1,), jnp.int32)])
    row = lambda v: v.reshape(1, -1)

    x = spread(tokens)

    code = jnp.concatenate(
        [queries, (choices // PASS).astype(bf16), (choices % PASS).astype(bf16)], axis=1
    )
    code_all = lax.all_gather(code, ("rows", "seq"), axis=0, tiled=True)

    cot = spread(cotangent)

    q, k, v, ctxt, lse, resid_one, hid, hidt, xt = attention_forward(
        sc, x, w_query, w_key, w_value, row(b_query), row(b_value), w_out, row(b_out),
        row(gain_one), row(shift_one), piece,
    )
    actt, slope, resid_two, mixed_row, pool = feed_forward(
        sc, hid, w_up, row(b_up), w_down, row(b_down), row(gain_two), row(shift_two), piece, d
    )

    pool = pool.astype(bf16)
    own_lin = own_r * seq_count + own_s
    devices = row_count * seq_count
    queries_all = code_all[:, :d]
    owner = code_all[:, d : d + CH].astype(jnp.int32)
    inner = code_all[:, d + CH :].astype(jnp.int32)
    if row_count == 8:
        near = jnp.concatenate(
            [pool, flip(pool, "seq", 2), flip(pool, "rows", 1), flip_both(pool, 1, 2)], 0
        )
        mid = jnp.concatenate(
            [near, flip(near, "rows", 2), flip(near, "rows", 6), flip(near, "rows", 4)], 0
        )
        pooled = jnp.concatenate([mid, flip(mid, "seq", 1)], 0)
        off = owner ^ own_lin
        z = off // 8
        spot = (off % 2) * 16 + (z ^ (z // 2)) * 4 + (off // 2) % 4
    else:
        pooled = lax.all_gather(pool, ("rows", "seq"), axis=0, tiled=True)
        pooled = jnp.roll(pooled, -own_lin * SLOT, 0)
        spot = (owner - own_lin) % devices
    losses_all, grad_pool = retrieval(queries_all, spot * SLOT + inner, pooled)
    query_losses = lax.dynamic_slice_in_dim(losses_all[:, 0], own_lin * queries.shape[0], queries.shape[0])

    other_half = lambda t, rows: lax.dynamic_index_in_dim(
        t.reshape(2, 2, rows, t.shape[-1]), 1 - core, 1, keepdims=False
    )
    quarters = lambda t: t.reshape(4, -1, t.shape[-1])
    swap = lambda t: flip(t, "seq", 1)
    actt_p = swap(other_half(actt, ff // 4))
    hidt_p = swap(other_half(hidt, d // 4))
    ctxt_p = swap(other_half(ctxt, d // 4))
    xt_p = swap(other_half(xt, d // 4))

    mixed = gather_back(mixed_row, seq_count)

    gd, gr_two, sums_two = norm_two_back(sc, cot, grad_pool, resid_two, row(gain_two), piece)
    gd_p = swap(gd)
    gup, bup, gr_one, gab, gctx, sums_one = feed_back(
        gd, gr_two, w_down, w_up, slope, resid_one, row(gain_one), w_out
    )
    gup_p = swap(gup)
    gab_p = swap(gab)

    down_in = (quarters(actt), actt_p, gd[None], gd_p[None])
    up_in = (quarters(hidt), hidt_p, gup, gup_p)
    out_in = (quarters(ctxt), ctxt_p, gab[None], gab_p[None])
    down_got = flip(weight_send(wsc, *down_in, 4, True, "down_send"), "seq", 2)
    up_got = flip(weight_send(wsc, *up_in, 4, False, "up_send"), "seq", 2)
    out_got = flip(weight_send(wsc, *out_in, 1, False, "out_send"), "seq", 2)

    gqkv, gtok, sums_qkv = attention_back(
        sc, q, k, v, gctx, lse, w_query, w_key, w_value, gr_one, piece
    )
    gqkv_p = swap(gqkv)

    down_parts = weight_split(wsc, *down_in, down_got, 2, True, "down_keep")
    near_down, far_down = halving(*down_parts, order_down, extra)
    up_parts = weight_split(wsc, *up_in, up_got, 3, False, "up_keep")
    near_up, far_up = halving(*up_parts, order_up, extra)
    grad_out = weight_keep(wsc, *out_in, out_got, 1, False, "out_keep")

    qkv_in = (quarters(xt), xt_p, gqkv, gqkv_p)
    qkv_send = weight_send(wsc, *qkv_in, 3, False, "qkv_send")

    vec = jnp.concatenate(
        [sums_qkv[:2], sums_one[:3], sums_two[:3]], 0
    )
    vec = vec.reshape(8, 4, d // 4).transpose(1, 0, 2).reshape(4, 2, d)
    vec = jnp.concatenate([vec, bup.reshape(4, ff // 4 // d, d)], 1)
    vec = vec.reshape(2, 2, 3, d)
    vec = lax.dynamic_index_in_dim(vec, core, 1, keepdims=False) + swap(
        lax.dynamic_index_in_dim(vec, 1 - core, 1, keepdims=False)
    )
    vec = jnp.pad(vec, ((0, 0), (0, 13), (0, 0)))
    vec_send = lax.dynamic_index_in_dim(vec, 1 - xside, 0, keepdims=False).astype(bf16)
    vec_keep = lax.dynamic_index_in_dim(vec, xside, 0, keepdims=False)

    got_q = flip(qkv_send[0], "seq", 2)
    got_k = flip(qkv_send[1], "seq", 2)
    got_v = flip(jnp.concatenate([qkv_send[2], vec_send], 0), "seq", 2)
    quarter = d // 4
    vec_sum = vec_keep + got_v[quarter:].astype(f32)
    got_v = got_v[:quarter]
    keep = weight_keep(
        wsc, *qkv_in, jnp.stack([got_q, got_k, got_v]), 3, False, "qkv_keep"
    )
    y, a, b = base
    grad_q = doubling(keep[0], [y, a, b] + extra)
    grad_k = doubling(keep[1], [a, b, y] + extra)
    last = doubling(jnp.concatenate([keep[2].astype(f32), vec_sum], 0), [b, y, a] + extra)
    grad_v = last[:quarter]
    small = last[quarter : quarter + 3]
    grad_o = doubling(grad_out[0], [a, b, y] + extra)

    grad_down = place(wsc, near_down, far_down, 2, False, "down_place")
    grad_up = place(wsc, near_up, far_up, 3, True, "up_place")
    grad_tokens = gather_back(gtok, seq_count)

    eight = small[:2].reshape(8, quarter)
    return (
        mixed,
        query_losses,
        grad_tokens,
        grad_q,
        eight[0],
        grad_k,
        grad_v,
        eight[1],
        grad_o,
        eight[2],
        eight[3],
        eight[4],
        grad_up,
        small[2],
        grad_down,
        eight[5],
        eight[6],
        eight[7],
    )


def solution(mesh):
    weights = (P(),) * 15
    placed = (
        (P("rows", "seq", None),)
        + weights
        + (
            P("rows", None),
            P(("rows", "seq"), None),
            P(("rows", "seq"), None),
            P("rows", "seq", None),
        )
    )
    return jax.shard_map(
        per_device,
        mesh=mesh,
        in_specs=placed,
        out_specs=(
            P("rows", "seq", None),
            P(("rows", "seq")),
            P("rows", "seq", None),
            P("seq", None),
            P("seq"),
            P("seq", None),
            P("seq", None),
            P("seq"),
            P("seq", None),
            P("seq"),
            P("seq"),
            P("seq"),
            P("seq", None),
            P("seq"),
            P("seq", None),
            P("seq"),
            P("seq"),
            P("seq"),
        ),
        check_vma=False,
    )
```

time: 1020 us -> 413 us (0.40)
  waiting for transfers between devices: 605 us -> 98.2 us
  matrix products: 204 us -> 0 us
  Pallas kernels: 0 us -> 149 us
  blocking collectives: 93.1 us -> 0 us
  starting transfers between devices: 0.75 us -> 88.6 us
  other arithmetic: 44.1 us -> 21.9 us
  local copies, waits for them, and re-layouts: 54.3 us -> 38.8 us
    reduce_scatter x6 -> x0, waiting for transfers between devices: 261 us -> none  [the longest x1 81 us: per_device(): lax.psum_scatter(grad_w_up, 'seq', scatter_dimension=0, tiled=True)]
    psum x2 -> x0, waiting for transfers between devices: 226 us -> none  [the longest x1 194 us: per_device(): lax.psum((part_wq, part_bq, part_wk, part_wv, part_bv, part_wo, part_bo,...]
    dot_general x27 -> x0, matrix products: 204 us -> none  [the longest x1 53.1 us: per_device(): jnp.einsum('rhqk,rkhd->rqhd', grad_raw, key_heads, preferred_element_type...]
    pallas_call x0 -> x16, Pallas kernels: none -> 149 us  [the longest x1 28 us: attention_forward(): pl.pallas_call(functools.partial(attention_kernel, piece), grid_spec=pltp...]
    ppermute x0 -> x58, waiting for transfers between devices: none -> 98.2 us  [the longest x57 98.2 us: flip(): return lax.ppermute(value, axis, [(i, i ^ mask) for i in range(count)])]
    ppermute x0 -> x58, starting transfers between devices: none -> 88.6 us  [the longest x57 87.8 us: flip(): return lax.ppermute(value, axis, [(i, i ^ mask) for i in range(count)])]
    unnamed x16 -> x1, waiting for transfers between devices: 79.5 us -> 0.02 us
    psum x2 -> x0, blocking collectives: 50.5 us -> none  [the longest x1 39.8 us: per_device(): lax.psum((part_wq, part_bq, part_wk, part_wv, part_bv, part_wo, part_bo,...]
  transfers between devices with their start and end apart: 13 -> 59, of which waited for: 12 -> 18; matrix products, arithmetic and copies ran while one was open for 18% -> 13% of each run, Pallas kernels for 0% -> 36%
where the time goes in v1:
time: 413 us; the launch traced here: 411 us
  Pallas kernels  149 us (36%)
  waiting for transfers between devices  98.2 us (24%)
  starting transfers between devices  88.6 us (21%)
  local copies, waits for them, and re-layouts  38.8 us (9%)
  other arithmetic  21.9 us (5%)
  between operations  14.7 us (4%)
    ppermute x57, waiting for transfers between devices, flip(): return lax.ppermute(value, axis, [(i, i ^ mask) for i in range(count)])  98.2 us
    ppermute x57, starting transfers between devices, flip(): return lax.ppermute(value, axis, [(i, i ^ mask) for i in range(count)])  87.8 us
    pallas_call x1, Pallas kernels, attention_forward(): pl.pallas_call(functools.partial(attention_kernel, piece), grid_spec=pltp...  28 us
    pallas_call x1, Pallas kernels, attention_back(): pl.pallas_call(functools.partial(attention_back_kernel, piece), grid_spec...  27.4 us
    pallas_call x4, Pallas kernels, weight_send(): pl.pallas_call(weight_send_kernel, grid_spec=pltpu.PrefetchScalarGridSpec...  20.9 us
    pallas_call x1, Pallas kernels, feed_back(): pl.pallas_call(feed_back_kernel, grid=(steps,), in_specs=[whole(length, d...  15.4 us
    pallas_call x1, Pallas kernels, feed_forward(): pl.pallas_call(functools.partial(feed_kernel, piece), grid_spec=pltpu.Pre...  14.4 us
    pallas_call x2, Pallas kernels, weight_split(): pl.pallas_call(functools.partial(weight_split_kernel, own_slot), grid_spe...  13.3 us
  transfers between devices with their start and end apart: 59, of which 18 were waited for; matrix products, arithmetic and copies ran while one was open for 13% of the time, Pallas kernels for 36%

profile of v1, /device:TPU:0, one launch (start us, length us, event | category | flops | bytes accessed | tf_op | source)
XLA Modules:
  0.0 411.3 jit_solution(6223324525785129740)
XLA Ops:
  24.7 28.0 %attention_forward.1 = (bf16[512,768]{1,0:T(8,128)(2,1)}, bf16[512,768]{1,0:T(8,128)(2,1)}, bf16[512,768]{1,0:T(8,128)(2,1)}, bf16[768,512]{1,0:T(8,128)(2,1)}, ...) custom-call(s32[8]{0:T(128)} %pad_add_fusion.sc_ref, ...), custom_call_target="tpu_custom_call" | custom-call | tf_op jit(solution)/shard_map/attention_forward/pallas_call | solution.py:125
  52.8 14.4 %feed_forward.1 = (bf16[3072,512]{1,0:T(8,128)(2,1)}, f32[4,512,768]{2,1,0:T(8,128)}, f32[512,768]{1,0:T(8,128)}, bf16[512,768]{1,0:T(8,128)(2,1)}, f32[8,768]{1,0:T(8,128)}) custom-call(s32[8]{0:T(128)} %pad_add_fusion.sc_ref, bf16[512,768]{1,0:T(8,128)(2,1)} %get-tuple-element.50.hid_ref, bf16[768,3072]{1,0:T(8,128)(2,1)} %wu_ref.3, f32[1,3072]{1,0:T(1,128)} %bitcast.138, ...), custom_call_target="tpu_custom_call" | custom-call | tf_op jit(solution)/shard_map/feed_forward/pallas_call | solution.py:199
  91.9 3.9 collective-permute-done.11
  103.4 9.7 %retrieval.1 = (f32[1024,1]{1,0:T(8,128)}, f32[8,768]{1,0:T(8,128)}) custom-call(bf16[1024,768]{1,0:T(8,128)(2,1)} %slice.185.q_ref, s32[1024,32]{1,0:T(8,128)} %fusion.4.pos_ref, bf16[256,768]{1,0:T(8,128)(2,1)} %copy-done.26), custom_call_target="tpu_custom_call" | custom-call | tf_op jit(solution)/shard_map/retrieval/pallas_call | solution.py:264
  113.1 5.1 %norm_two_back.1 = (bf16[512,768]{1,0:T(8,128)(2,1)}, f32[512,768]{1,0:T(8,128)}, f32[8,768]{1,0:T(8,128)}) custom-call(s32[8]{0:T(128)} %pad_add_fusion.sc_ref, bf16[512,768]{1,0:T(8,128)(2,1)} %pad_maximum_fusion.2.cot_ref, f32[8,768]{1,0:T(8,128)} %get-tuple-element.57.gp_ref, f32[512,768]{1,0:T(8,128)} %get-tuple-element.58.resid_ref, ...), custom_call_target="tpu_custom_call" | custom-call | tf_op jit(solution)/shard_map/norm_two_back/pallas_call | solution.py:304
  118.3 15.4 %feed_back.1 = (bf16[4,512,768]{2,1,0:T(8,128)(2,1)}, f32[4,1,768]{2,1,0:T(1,128)}, f32[512,768]{1,0:T(8,128)}, bf16[512,768]{1,0:T(8,128)(2,1)}, bf16[512,768]{1,0:T(8,128)(2,1)}, /*index=5*/f32[8,768]{1,0:T(8,128)}) custom-call(bf16[512,768]{1,0:T(8,128)(2,1)} %get-tuple-element.59.gd_ref, f32[512,768]{1,0:T(8,128)} %get-tuple-element.60.gr_ref, ...), custom_call_target="tpu_custom_call" | custom-call | tf_op jit(solution)/shard_map/feed_back/pallas_call | solution.py:356
  135.1 27.4 %attention_back.1 = (bf16[3,512,768]{2,1,0:T(8,128)(2,1)}, bf16[512,768]{1,0:T(8,128)(2,1)}, f32[8,768]{1,0:T(8,128)}) custom-call(s32[8]{0:T(128)} %pad_add_fusion.sc_ref, bf16[512,768]{1,0:T(8,128)(2,1)} %get-tuple-element.54.q_ref, bf16[512,768]{1,0:T(8,128)(2,1)} %get-tuple-element.55.k_ref, bf16[512,768]{1,0:T(8,128)(2,1)} %get-tuple-element.56.v_ref, ...), custom_call_target="tpu_custom_call" | custom-call | tf_op jit(solution)/shard_map/attention_back/pallas_call | solution.py:442
  172.2 3.6 out_send.1
  180.0 5.2 %collective-permute-done.36.recv_ref = bf16[1,192,768]{2,1,0:T(8,128)(2,1)S(1)} collective-permute-done((bf16[1,192,768]{2,1,0:T(8,128)(2,1)}, bf16[1,192,768]{2,1,0:T(8,128)(2,1)S(1)}, u32[]{:S(2)}, u32[]{:S(2)}) %collective-permute-start.36) | collective-permute-done | bytes 294944 | tf_op jit(solution)/shard_map/ppermute | solution.py:589
  192.7 5.8 %down_send.1 = bf16[4,192,768]{2,1,0:T(8,128)(2,1)} custom-call(s32[4]{0:T(128)} %pad_add_fusion.1.sc_ref, bf16[4,768,512]{2,1,0:T(8,128)(2,1)} %bitcast.117, bf16[2,768,512]{2,1,0:T(8,128)(2,1)} %collective-permute-done.49.lp_ref, bf16[1,512,768]{2,1,0:T(8,128)(2,1)} %bitcast.119, bf16[1,512,768]{2,1,0:T(8,128)(2,1)} %bitcast.132), custom_call_target="tpu_custom_call" | custom-call | tf_op jit(solution)/shard_map/down_send/pallas_call | solution.py:515
  205.0 24.7 %collective-permute-done.18 = bf16[128,768]{1,0:T(8,128)(2,1)S(1)} collective-permute-done((bf16[128,768]{1,0:T(8,128)(2,1)S(1)}, bf16[128,768]{1,0:T(8,128)(2,1)S(1)}, u32[]{:S(2)}, u32[]{:S(2)}) %collective-permute-start.18) | collective-permute-done | bytes 196640 | tf_op jit(solution)/shard_map/ppermute | solution.py:589
  232.9 6.4 %down_keep.1 = (f32[4,96,768]{2,1,0:T(8,128)}, bf16[4,96,768]{2,1,0:T(8,128)(2,1)}) custom-call(s32[4]{0:T(128)} %pad_add_fusion.1.sc_ref, bf16[4,768,512]{2,1,0:T(8,128)(2,1)} %bitcast.118, bf16[2,768,512]{2,1,0:T(8,128)(2,1)} %collective-permute-done.49.lp_ref, bf16[1,512,768]{2,1,0:T(8,128)(2,1)} %bitcast.120, bf16[1,512,768]{2,1,0:T(8,128)(2,1)} %bitcast.133, ...), custom_call_target="tpu_custom_call" | custom-call | tf_op jit(solution)/shard_map/down_keep/pallas_call | solution.py:545
  240.1 5.4 %qkv_send.1 = bf16[3,192,768]{2,1,0:T(8,128)(2,1)} custom-call(s32[4]{0:T(128)} %pad_add_fusion.1.sc_ref, bf16[4,192,512]{2,1,0:T(8,128)(2,1)} %bitcast.124, bf16[2,192,512]{2,1,0:T(8,128)(2,1)} %copy-done.13, bf16[3,512,768]{2,1,0:T(8,128)(2,1)} %get-tuple-element.68.go_ref, bf16[3,512,768]{2,1,0:T(8,128)(2,1)} %collective-permute-done.20.gp_ref), custom_call_target="tpu_custom_call" | custom-call | tf_op jit(solution)/shard_map/qkv_send/pallas_call | solution.py:515
  262.5 6.0 %up_send.1 = bf16[4,192,768]{2,1,0:T(8,128)(2,1)} custom-call(s32[4]{0:T(128)} %pad_add_fusion.1.sc_ref, bf16[4,192,512]{2,1,0:T(8,128)(2,1)} %bitcast.121, bf16[2,192,512]{2,1,0:T(8,128)(2,1)} %copy-done.11, bf16[4,512,768]{2,1,0:T(8,128)(2,1)} %get-tuple-element.76.go_ref, bf16[4,512,768]{2,1,0:T(8,128)(2,1)} %copy-done.3), custom_call_target="tpu_custom_call" | custom-call | tf_op jit(solution)/shard_map/up_send/pallas_call | solution.py:515
  273.8 5.8 %qkv_keep.1 = bf16[3,192,768]{2,1,0:T(8,128)(2,1)} custom-call(s32[4]{0:T(128)} %pad_add_fusion.1.sc_ref, bf16[4,192,512]{2,1,0:T(8,128)(2,1)} %bitcast.125, bf16[2,192,512]{2,1,0:T(8,128)(2,1)} %copy-done.13, bf16[3,512,768]{2,1,0:T(8,128)(2,1)} %get-tuple-element.68.go_ref, bf16[3,512,768]{2,1,0:T(8,128)(2,1)} %collective-permute-done.20.gp_ref, ...), custom_call_target="tpu_custom_call" | custom-call | tf_op jit(solution)/shard_map/qkv_keep/pallas_call | solution.py:529
  288.5 7.6 %collective-permute-done.42.recv_ref = bf16[4,192,768]{2,1,0:T(8,128)(2,1)S(1)} collective-permute-done((bf16[4,192,768]{2,1,0:T(8,128)(2,1)}, bf16[4,192,768]{2,1,0:T(8,128)(2,1)S(1)}, u32[]{:S(2)}, u32[]{:S(2)}) %collective-permute-start.42) | collective-permute-done | bytes 1179680 | tf_op jit(solution)/shard_map/ppermute | solution.py:589
  297.2 6.9 %up_keep.1 = (f32[4,96,768]{2,1,0:T(8,128)}, bf16[4,96,768]{2,1,0:T(8,128)(2,1)}) custom-call(s32[4]{0:T(128)} %pad_add_fusion.1.sc_ref, bf16[4,192,512]{2,1,0:T(8,128)(2,1)} %bitcast.122, bf16[2,192,512]{2,1,0:T(8,128)(2,1)} %copy-done.11, bf16[4,512,768]{2,1,0:T(8,128)(2,1)} %get-tuple-element.76.go_ref, bf16[4,512,768]{2,1,0:T(8,128)(2,1)} %copy-done.3, ...), custom_call_target="tpu_custom_call" | custom-call | tf_op jit(solution)/shard_map/up_keep/pallas_call | solution.py:545
  310.4 12.1 %collective-permute-done.43 = bf16[4,96,768]{2,1,0:T(8,128)(2,1)S(1)} collective-permute-done((bf16[4,96,768]{2,1,0:T(8,128)(2,1)}, bf16[4,96,768]{2,1,0:T(8,128)(2,1)S(1)}, u32[]{:S(2)}, u32[]{:S(2)}) %collective-permute-start.43) | collective-permute-done | bytes 589856 | tf_op jit(solution)/shard_map/ppermute | solution.py:589
  331.3 23.7 %collective-permute-start.45 = (bf16[1,96,768]{2,1,0:T(8,128)(2,1)S(1)}, bf16[1,96,768]{2,1,0:T(8,128)(2,1)S(1)}, u32[]{:S(2)}, u32[]{:S(2)}) collective-permute-start(bf16[1,96,768]{2,1,0:T(8,128)(2,1)S(1)} %slice.247), channel_id=1, source_target_pairs={{0,8},{4,12},{8,0},{12,4},{16,24},{20,28},{24,16},{28,20},{1,9},{5... | collective-permute-start | bytes 442376 | tf_op jit(solution)/shard_map/ppermute | solution.py:589
  364.2 5.2 %collective-permute-done.46 = bf16[1,96,768]{2,1,0:T(8,128)(2,1)S(1)} collective-permute-done((bf16[1,96,768]{2,1,0:T(8,128)(2,1)S(1)}, bf16[1,96,768]{2,1,0:T(8,128)(2,1)S(1)}, u32[]{:S(2)}, u32[]{:S(2)}) %collective-permute-start.46) | collective-permute-done | bytes 147488 | tf_op jit(solution)/shard_map/ppermute | solution.py:589
  372.1 4.1 collective-permute-done.47
  376.3 3.6 collective-permute-start.48
  382.1 6.6 %collective-permute-done.57.far_ref = bf16[4,96,768]{2,1,0:T(8,128)(2,1)S(1)} collective-permute-done((bf16[4,96,768]{2,1,0:T(8,128)(2,1)S(1)}, bf16[4,96,768]{2,1,0:T(8,128)(2,1)S(1)}, u32[]{:S(2)}, u32[]{:S(2)}) %collective-permute-start.57) | collective-permute-done | bytes 589856 | tf_op jit(solution)/shard_map/ppermute | solution.py:589
  392.4 8.4 %collective-permute-done.48.far_ref = bf16[4,96,768]{2,1,0:T(8,128)(2,1)S(1)} collective-permute-done((bf16[4,96,768]{2,1,0:T(8,128)(2,1)S(1)}, bf16[4,96,768]{2,1,0:T(8,128)(2,1)S(1)}, u32[]{:S(2)}, u32[]{:S(2)}) %collective-permute-start.48) | collective-permute-done | bytes 589856 | tf_op jit(solution)/shard_map/ppermute | solution.py:589
  (288 shorter events, 151.6 us)
Async XLA Ops:
  7.2 90.2 %all-gather.2.cloned.1.call-start = ((), (), s32[]{:S(2)}) async-start(), calls=%async_computation | async-start | bytes 1892352 | tf_op jit(solution)/shard_map/all_gather | solution.py:699
  14.2 61.5 %collective-permute-start.13 = (bf16[128,768]{1,0:T(8,128)(2,1)S(1)}, bf16[128,768]{1,0:T(8,128)(2,1)S(1)}, u32[]{:S(2)}, u32[]{:S(2)}) collective-permute-start(bf16[128,768]{1,0:T(8,128)(2,1)S(1)} %get-tuple-element.96), channel_id=1, source_target_pairs={{0,1},{1,0},{2,3},{3,2},{4,5},{5,4},{6,7},{7,6},{8,9},{9,8},{10,11... | collective-permute-start | bytes 589832 | tf_op jit(solution)/shard_map/ppermute | solution.py:589
  14.4 62.1 %collective-permute-start.14 = (bf16[128,768]{1,0:T(8,128)(2,1)S(1)}, bf16[128,768]{1,0:T(8,128)(2,1)S(1)}, u32[]{:S(2)}, u32[]{:S(2)}) collective-permute-start(bf16[128,768]{1,0:T(8,128)(2,1)S(1)} %get-tuple-element.98), channel_id=1, source_target_pairs={{0,2},{1,3},{2,0},{3,1},{4,6},{5,7},{6,4},{7,5},{8,10},{9,11},{10,... | collective-permute-start | bytes 589832 | tf_op jit(solution)/shard_map/ppermute | solution.py:589
  22.3 54.5 %collective-permute-start.15 = (bf16[128,768]{1,0:T(8,128)(2,1)S(1)}, bf16[128,768]{1,0:T(8,128)(2,1)S(1)}, u32[]{:S(2)}, u32[]{:S(2)}) collective-permute-start(bf16[128,768]{1,0:T(8,128)(2,1)S(1)} %get-tuple-element.97), channel_id=1, source_target_pairs={{0,3},{1,2},{2,1},{3,0},{4,7},{5,6},{6,5},{7,4},{8,11},{9,10},{10,... | collective-permute-start | bytes 589832 | tf_op jit(solution)/shard_map/ppermute | solution.py:589
  76.6 112.8 %collective-permute-start.49 = (bf16[2,768,512]{2,1,0:T(8,128)(2,1)}, bf16[2,768,512]{2,1,0:T(8,128)(2,1)}, u32[]{:S(2)}, u32[]{:S(2)}) collective-permute-start(bf16[2,768,512]{2,1,0:T(8,128)(2,1)} %dynamic-slice_bitcast_fusion), channel_id=1, source_target_pairs={{0,1},{1,0},{2,3},{3,2},{4,5},{5,4},{6,7},{7,6},{8,9},{9,8},{10,11... | collective-permute-start | bytes 4718600 | tf_op jit(solution)/shard_map/ppermute | solution.py:589
  76.8 93.3 %collective-permute-start.34 = (bf16[2,192,512]{2,1,0:T(8,128)(2,1)}, bf16[2,192,512]{2,1,0:T(8,128)(2,1)S(1)}, u32[]{:S(2)}, u32[]{:S(2)}) collective-permute-start(bf16[2,192,512]{2,1,0:T(8,128)(2,1)} %dynamic-slice_bitcast_fusion.2), channel_id=1, source_target_pairs={{0,1},{1,0},{2,3},{3,2},{4,5},{5,4},{6,7},{7,6},{8,9},{9,8},{10,11... | collective-permute-start | bytes 1179656 | tf_op jit(solution)/shard_map/ppermute | solution.py:589
  78.7 55.0 %collective-permute-start.3 = (bf16[128,768]{1,0:T(8,128)(2,1)S(1)}, bf16[128,768]{1,0:T(8,128)(2,1)S(1)}, u32[]{:S(2)}, u32[]{:S(2)}) collective-permute-start(bf16[128,768]{1,0:T(8,128)(2,1)S(1)} %get-tuple-element.101), channel_id=1, source_target_pairs={{0,1},{1,0},{2,3},{3,2},{4,5},{5,4},{6,7},{7,6},{8,9},{9,8},{10,11... | collective-permute-start | bytes 589832 | tf_op jit(solution)/shard_map/ppermute | solution.py:589
  79.0 55.2 %collective-permute-start.4 = (bf16[128,768]{1,0:T(8,128)(2,1)S(1)}, bf16[128,768]{1,0:T(8,128)(2,1)S(1)}, u32[]{:S(2)}, u32[]{:S(2)}) collective-permute-start(bf16[128,768]{1,0:T(8,128)(2,1)S(1)} %get-tuple-element.100), channel_id=1, source_target_pairs={{0,2},{1,3},{2,0},{3,1},{4,6},{5,7},{6,4},{7,5},{8,10},{9,11},{10,... | collective-permute-start | bytes 589832 | tf_op jit(solution)/shard_map/ppermute | solution.py:589
  97.3 72.4 %collective-permute-start.5 = (bf16[128,768]{1,0:T(8,128)(2,1)}, bf16[128,768]{1,0:T(8,128)(2,1)}, u32[]{:S(2)}, u32[]{:S(2)}) collective-permute-start(bf16[128,768]{1,0:T(8,128)(2,1)} %get-tuple-element.99), channel_id=1, source_target_pairs={{0,3},{1,2},{2,1},{3,0},{4,7},{5,6},{6,5},{7,4},{8,11},{9,10},{10,... | collective-permute-start | bytes 589832 | tf_op jit(solution)/shard_map/ppermute | solution.py:589
  133.7 38.1 %collective-permute-start.35 = (bf16[512,768]{1,0:T(8,128)(2,1)}, bf16[512,768]{1,0:T(8,128)(2,1)}, u32[]{:S(2)}, u32[]{:S(2)}) collective-permute-start(bf16[512,768]{1,0:T(8,128)(2,1)} %get-tuple-element.74), channel_id=1, source_target_pairs={{0,1},{1,0},{2,3},{3,2},{4,5},{5,4},{6,7},{7,6},{8,9},{9,8},{10,11... | collective-permute-start | bytes 2359304 | tf_op jit(solution)/shard_map/ppermute | solution.py:589
  162.5 77.2 %collective-permute-start.20 = (bf16[3,512,768]{2,1,0:T(8,128)(2,1)}, bf16[3,512,768]{2,1,0:T(8,128)(2,1)}, u32[]{:S(2)}, u32[]{:S(2)}) collective-permute-start(bf16[3,512,768]{2,1,0:T(8,128)(2,1)} %get-tuple-element.68.go_ref), channel_id=1, source_target_pairs={{0,1},{1,0},{2,3},{3,2},{4,5},{5,4},{6,7},{7,6},{8,9},{9,8},{10,11... | collective-permute-start | bytes 7077896 | tf_op jit(solution)/shard_map/ppermute | solution.py:589
  169.7 91.1 %collective-permute-start.41 = (bf16[4,512,768]{2,1,0:T(8,128)(2,1)S(1)}, bf16[4,512,768]{2,1,0:T(8,128)(2,1)S(1)}, u32[]{:S(2)}, u32[]{:S(2)}) collective-permute-start(bf16[4,512,768]{2,1,0:T(8,128)(2,1)S(1)} %copy-done.2), channel_id=1, source_target_pairs={{0,1},{1,0},{2,3},{3,2},{4,5},{5,4},{6,7},{7,6},{8,9},{9,8},{10,11... | collective-permute-start | bytes 9437192 | tf_op jit(solution)/shard_map/ppermute | solution.py:589
  198.6 32.8 %collective-permute-start.51 = (bf16[4,192,768]{2,1,0:T(8,128)(2,1)}, bf16[4,192,768]{2,1,0:T(8,128)(2,1)}, u32[]{:S(2)}, u32[]{:S(2)}) collective-permute-start(bf16[4,192,768]{2,1,0:T(8,128)(2,1)} %down_send.1), channel_id=1, source_target_pairs={{0,2},{1,3},{2,0},{3,1},{4,6},{5,7},{6,4},{7,5},{8,10},{9,11},{10,... | collective-permute-start | bytes 3538952 | tf_op jit(solution)/shard_map/ppermute | solution.py:589
  201.0 28.7 %collective-permute-start.18 = (bf16[128,768]{1,0:T(8,128)(2,1)S(1)}, bf16[128,768]{1,0:T(8,128)(2,1)S(1)}, u32[]{:S(2)}, u32[]{:S(2)}) collective-permute-start(bf16[128,768]{1,0:T(8,128)(2,1)S(1)} %copy-done.29), channel_id=1, source_target_pairs={{0,3},{1,2},{2,1},{3,0},{4,7},{5,6},{6,5},{7,4},{8,11},{9,10},{10,... | collective-permute-start | bytes 589832 | tf_op jit(solution)/shard_map/ppermute | solution.py:589
  201.5 29.7 %collective-permute-start.38 = (bf16[192,768]{1,0:T(8,128)(2,1)S(1)}, bf16[192,768]{1,0:T(8,128)(2,1)S(1)}, u32[]{:S(2)}, u32[]{:S(2)}) collective-permute-start(bf16[192,768]{1,0:T(8,128)(2,1)S(1)} %add_convert_fusion.3), channel_id=1, source_target_pairs={{0,24},{4,28},{8,16},{12,20},{16,8},{20,12},{24,0},{28,4},{1,25},{... | collective-permute-start | bytes 884744 | tf_op jit(solution)/shard_map/ppermute | solution.py:589
  231.3 26.8 %collective-permute-start.40 = (bf16[2,192,512]{2,1,0:T(8,128)(2,1)}, bf16[2,192,512]{2,1,0:T(8,128)(2,1)S(1)}, u32[]{:S(2)}, u32[]{:S(2)}) collective-permute-start(bf16[2,192,512]{2,1,0:T(8,128)(2,1)} %dynamic-slice_bitcast_fusion.1), channel_id=1, source_target_pairs={{0,1},{1,0},{2,3},{3,2},{4,5},{5,4},{6,7},{7,6},{8,9},{9,8},{10,11... | collective-permute-start | bytes 1179656 | tf_op jit(solution)/shard_map/ppermute | solution.py:589
  258.1 27.8 %collective-permute-start.53 = (bf16[2,96,768]{2,1,0:T(8,128)(2,1)}, bf16[2,96,768]{2,1,0:T(8,128)(2,1)}, u32[]{:S(2)}, u32[]{:S(2)}) collective-permute-start(bf16[2,96,768]{2,1,0:T(8,128)(2,1)} %slice.244), channel_id=1, source_target_pairs={{0,24},{4,28},{8,16},{12,20},{16,8},{20,12},{24,0},{28,4},{1,25},{... | collective-permute-start | bytes 884744 | tf_op jit(solution)/shard_map/ppermute | solution.py:589
  268.5 27.7 %collective-permute-start.42 = (bf16[4,192,768]{2,1,0:T(8,128)(2,1)}, bf16[4,192,768]{2,1,0:T(8,128)(2,1)S(1)}, u32[]{:S(2)}, u32[]{:S(2)}) collective-permute-start(bf16[4,192,768]{2,1,0:T(8,128)(2,1)} %up_send.1), channel_id=1, source_target_pairs={{0,2},{1,3},{2,0},{3,1},{4,6},{5,7},{6,4},{7,5},{8,10},{9,11},{10,... | collective-permute-start | bytes 3538952 | tf_op jit(solution)/shard_map/ppermute | solution.py:589
  280.8 26.7 %collective-permute-start.25 = (bf16[192,768]{1,0:T(8,128)(2,1)S(1)}, bf16[192,768]{1,0:T(8,128)(2,1)S(1)}, u32[]{:S(2)}, u32[]{:S(2)}) collective-permute-start(bf16[192,768]{1,0:T(8,128)(2,1)S(1)} %get-tuple-element.88), channel_id=1, source_target_pairs={{0,4},{4,0},{8,12},{12,8},{16,20},{20,16},{24,28},{28,24},{1,5},{5... | collective-permute-start | bytes 884744 | tf_op jit(solution)/shard_map/ppermute | solution.py:589
  308.1 46.9 %collective-permute-start.26 = (bf16[192,768]{1,0:T(8,128)(2,1)S(1)}, bf16[192,768]{1,0:T(8,128)(2,1)S(1)}, u32[]{:S(2)}, u32[]{:S(2)}) collective-permute-start(bf16[192,768]{1,0:T(8,128)(2,1)S(1)} %get-tuple-element.85), channel_id=1, source_target_pairs={{0,8},{4,12},{8,0},{12,4},{16,24},{20,28},{24,16},{28,20},{1,9},{5... | collective-permute-start | bytes 884744 | tf_op jit(solution)/shard_map/ppermute | solution.py:589
  308.8 53.1 %collective-permute-start.29 = (bf16[208,768]{1,0:T(8,128)(2,1)S(1)}, bf16[208,768]{1,0:T(8,128)(2,1)S(1)}, u32[]{:S(2)}, u32[]{:S(2)}) collective-permute-start(bf16[208,768]{1,0:T(8,128)(2,1)S(1)} %add_convert_fusion.1), channel_id=1, source_target_pairs={{0,4},{4,0},{8,12},{12,8},{16,20},{20,16},{24,28},{28,24},{1,5},{5... | collective-permute-start | bytes 958472 | tf_op jit(solution)/shard_map/ppermute | solution.py:589
  323.2 39.6 %collective-permute-start.56 = (bf16[2,96,768]{2,1,0:T(8,128)(2,1)S(1)}, bf16[2,96,768]{2,1,0:T(8,128)(2,1)S(1)}, u32[]{:S(2)}, u32[]{:S(2)}) collective-permute-start(bf16[2,96,768]{2,1,0:T(8,128)(2,1)S(1)} %pad_maximum_fusion.8), channel_id=1, source_target_pairs={{0,24},{4,28},{8,16},{12,20},{16,8},{20,12},{24,0},{28,4},{1,25},{... | collective-permute-start | bytes 884744 | tf_op jit(solution)/shard_map/ppermute | solution.py:589
  328.7 41.6 %collective-permute-start.33 = (bf16[192,768]{1,0:T(8,128)(2,1)S(1)}, bf16[192,768]{1,0:T(8,128)(2,1)S(1)}, u32[]{:S(2)}, u32[]{:S(2)}) collective-permute-start(bf16[192,768]{1,0:T(8,128)(2,1)S(1)} %add_convert_fusion.4), channel_id=1, source_target_pairs={{0,4},{4,0},{8,12},{12,8},{16,20},{20,16},{24,28},{28,24},{1,5},{5... | collective-permute-start | bytes 884744 | tf_op jit(solution)/shard_map/ppermute | solution.py:589
  331.3 29.2 %collective-permute-start.45 = (bf16[1,96,768]{2,1,0:T(8,128)(2,1)S(1)}, bf16[1,96,768]{2,1,0:T(8,128)(2,1)S(1)}, u32[]{:S(2)}, u32[]{:S(2)}) collective-permute-start(bf16[1,96,768]{2,1,0:T(8,128)(2,1)S(1)} %slice.247), channel_id=1, source_target_pairs={{0,8},{4,12},{8,0},{12,4},{16,24},{20,28},{24,16},{28,20},{1,9},{5... | collective-permute-start | bytes 442376 | tf_op jit(solution)/shard_map/ppermute | solution.py:589
  (77 other events, 893.8 us)
Sparse Core Ops, SparseCore 0:
  11.5 58.5 all-gather.1

commit v2 on v0

v2 whole, which is shorter than its diff:
```python
import functools

import jax
import jax.numpy as jnp
from jax import lax
from jax.experimental import pallas as pl
from jax.experimental.pallas import tpu as pltpu
from jax.sharding import PartitionSpec as P

HEADS = 12
HEAD = 64
PASS = 6
CH = 32
SLOT = 8
GROUP = 4
SUB = 256
TAIL = (
    0.0925346463, 0.0902475115, 0.103641987, 0.0105003931,
    0.230693277, -0.20728912, 0.250823127, -0.0711517759,
)
SCALE = HEAD ** (-0.5)

norm_eps = 1e-05
f32 = jnp.float32
bf16 = jnp.bfloat16
VMEM_BYTES = 56 * 1024 * 1024


def params():
    return pltpu.CompilerParams(vmem_limit_bytes=VMEM_BYTES)


def cost(micros):
    return pl.CostEstimate(flops=int(micros * 1.15e9), bytes_accessed=0, transcendentals=0)


def nt(a, b):
    return lax.dot_general(a, b, (((1,), (1,)), ((), ())), preferred_element_type=f32)


def tn(a, b):
    return lax.dot_general(a, b, (((0,), (0,)), ((), ())), preferred_element_type=f32)


def nn(a, b):
    return jnp.dot(a, b, preferred_element_type=f32)


def stats(values):
    center = values - jnp.mean(values, -1, keepdims=True)
    inv = lax.rsqrt(jnp.mean(center * center, -1, keepdims=True) + norm_eps)
    return center * inv, inv


def norm_back(grad, xhat, inv, gain):
    gx = grad * gain
    return inv * (
        gx - jnp.mean(gx, -1, keepdims=True) - xhat * jnp.mean(gx * xhat, -1, keepdims=True)
    )


def true_places(own_seq, count, piece, axis):
    shape = (count, 1) if axis == 0 else (1, count)
    local = lax.broadcasted_iota(jnp.int32, shape, axis)
    block = local // piece
    return (block ^ own_seq) * piece + (local - block * piece)


def segments(sc_ref, places):
    total = jnp.zeros(places.shape, jnp.int32)
    for j in range(PASS):
        total += (sc_ref[1 + j] <= places).astype(jnp.int32)
    return total


def segment_bias(sc_ref, length, piece):
    col = segments(sc_ref, true_places(sc_ref[0], length, piece, 0))
    row = segments(sc_ref, true_places(sc_ref[0], length, piece, 1))
    return jnp.where(col == row, 0.0, -1e30)


def normal_tail(size):
    t = 1.0 / (1.0 + 0.2316419 * size)
    total = jnp.full_like(t, TAIL[-1])
    for term in TAIL[-2::-1]:
        total = total * t + term
    return total * t


def call(kernel, sc, args, specs, outs, out_specs, grid, scratch, name, micros, deps=()):
    count = len(args)

    def body(sc_ref, *refs):
        kernel(sc_ref, *refs[:count], *refs[count + len(deps) :])

    hold = pl.BlockSpec(memory_space=pl.ANY)
    return pl.pallas_call(
        body,
        grid_spec=pltpu.PrefetchScalarGridSpec(
            num_scalar_prefetch=1,
            grid=grid,
            in_specs=list(specs) + [hold] * len(deps),
            out_specs=out_specs,
            scratch_shapes=scratch,
        ),
        out_shape=outs,
        compiler_params=params(),
        cost_estimate=cost(micros),
        name=name,
    )(sc, *args, *deps)


def shape(t, *dims):
    return jax.ShapeDtypeStruct(dims, t)


def whole(*dims):
    return pl.BlockSpec(dims, lambda i, s: (0,) * len(dims))


def attention_kernel(
    piece, sc_ref, x_ref, wq_ref, wk_ref, wv_ref, bq_ref, bv_ref, wo_ref, bo_ref, go_ref, so_ref,
    q_ref, k_ref, v_ref, ctxt_ref, lse_ref, xt_ref, xhat_ref, inv_ref, hid_ref, hidt_ref,
    acc, bias,
):
    step = pl.program_id(0)
    length = x_ref.shape[0]
    x = x_ref[...]
    q_ref[...] = (nn(x, wq_ref[...]) + bq_ref[...]).astype(bf16)
    k_ref[...] = nn(x, wk_ref[...]).astype(bf16)
    v_ref[...] = (nn(x, wv_ref[...]) + bv_ref[...]).astype(bf16)

    @pl.when(step == 0)
    def _():
        bias[...] = segment_bias(sc_ref, length, piece)
        acc[...] = x.astype(f32) + bo_ref[...]

    for h in range(GROUP):
        cols = slice(h * HEAD, (h + 1) * HEAD)
        raw = nt(k_ref[:, cols], q_ref[:, cols] * jnp.asarray(SCALE, bf16))
        scores = raw + bias[...]
        top = jnp.max(scores, 0, keepdims=True)
        e = jnp.exp(scores - top)
        total = jnp.sum(e, 0, keepdims=True)
        p = (e * (1.0 / total)).astype(bf16)
        ctxt_ref[cols, :] = tn(v_ref[:, cols], p).astype(bf16)
        lse_ref[0, h : h + 1, :] = top + jnp.log(total)
    acc[...] += tn(ctxt_ref[...], wo_ref[...])

    for j in range(x_ref.shape[1] // xt_ref.shape[0]):
        wide = xt_ref.shape[0]

        @pl.when(step == j)
        def _():
            xt_ref[...] = x_ref[:, j * wide : (j + 1) * wide].T

    @pl.when(step == pl.num_programs(0) - 1)
    def _():
        xhat, inv = stats(acc[...])
        xhat_ref[...] = xhat
        inv_ref[...] = inv
        hid = (xhat * go_ref[...] + so_ref[...]).astype(bf16)
        hid_ref[...] = hid
        hidt_ref[...] = hid.T


def attention_forward(sc, x, wq, wk, wv, bq, bv, wo, bo, go, so, piece):
    length, d = x.shape
    wide = GROUP * HEAD
    steps = d // wide
    cols = lambda r: pl.BlockSpec((r, wide), lambda i, s: (0, i))
    rows = lambda c: pl.BlockSpec((wide, c), lambda i, s: (i, 0))
    return call(
        functools.partial(attention_kernel, piece),
        sc,
        (x, wq, wk, wv, bq, bv, wo, bo, go, so),
        [
            whole(length, d), cols(d), cols(d), cols(d), cols(1), cols(1), rows(d),
            whole(1, d), whole(1, d), whole(1, d),
        ],
        [
            shape(bf16, length, d), shape(bf16, length, d), shape(bf16, length, d),
            shape(bf16, d, length), shape(f32, steps, SLOT, length), shape(bf16, d, length),
            shape(f32, length, d), shape(f32, length, 1), shape(bf16, length, d),
            shape(bf16, d, length),
        ],
        [
            cols(length), cols(length), cols(length), rows(length),
            pl.BlockSpec((1, SLOT, length), lambda i, s: (i, 0, 0)), rows(length),
            whole(length, d), whole(length, 1), whole(length, d), whole(d, length),
        ],
        (steps,),
        [pltpu.VMEM((length, d), f32), pltpu.VMEM((length, length), f32)],
        "attention_forward", 18,
    )


def feed_kernel(
    piece, sc_ref, hid_ref, wu_ref, bu_ref, wd_ref, bd_ref, gt_ref, st_ref,
    actt_ref, slope_ref, xhat_ref, inv_ref, mixed_ref, pool_ref,
    acc,
):
    step = pl.program_id(0)
    length = hid_ref.shape[0]

    @pl.when(step == 0)
    def _():
        acc[...] = hid_ref[...].astype(f32) + bd_ref[...]

    for c in range(0, wu_ref.shape[1], SUB):
        cols = slice(c, c + SUB)
        up = nn(hid_ref[...], wu_ref[:, cols]) + bu_ref[:, cols]
        e = jnp.exp(-0.5 * up * up)
        tail = normal_tail(jnp.abs(up)) * e
        cum = jnp.where(up < 0.0, tail, 1.0 - tail)
        slope_ref[0, :, cols] = cum + up * (e * 0.3989422804014327)
        act = (up * cum).astype(bf16)
        actt_ref[cols, :] = act.T
        acc[...] += nn(act, wd_ref[cols, :])

    @pl.when(step == pl.num_programs(0) - 1)
    def _():
        xhat, inv = stats(acc[...])
        xhat_ref[...] = xhat
        inv_ref[...] = inv
        mixed = (xhat * gt_ref[...] + st_ref[...]).astype(bf16)
        mixed_ref[...] = mixed
        places = true_places(sc_ref[0], length, piece, 1)
        slot = lax.broadcasted_iota(jnp.int32, (SLOT, 1), 0)
        start = jnp.full((SLOT, 1), -1, jnp.int32)
        for j in range(PASS):
            start = jnp.where(slot == j, sc_ref[1 + j], start)
        pool_ref[...] = nn((places == start).astype(f32).astype(bf16), mixed)


def feed_forward(sc, hid, wu, bu, wd, bd, gt, st, piece, deps):
    length, d = hid.shape
    ff = wu.shape[1]
    steps = ff // d
    return call(
        functools.partial(feed_kernel, piece),
        sc,
        (hid, wu, bu, wd, bd, gt, st),
        [
            whole(length, d),
            pl.BlockSpec((d, d), lambda i, s: (0, i)),
            pl.BlockSpec((1, d), lambda i, s: (0, i)),
            pl.BlockSpec((d, d), lambda i, s: (i, 0)),
            whole(1, d), whole(1, d), whole(1, d),
        ],
        [
            shape(bf16, ff, length), shape(f32, steps, length, d), shape(f32, length, d),
            shape(f32, length, 1), shape(bf16, length, d), shape(f32, SLOT, d),
        ],
        [
            pl.BlockSpec((d, length), lambda i, s: (i, 0)),
            pl.BlockSpec((1, length, d), lambda i, s: (i, 0, 0)),
            whole(length, d), whole(length, 1), whole(length, d), whole(SLOT, d),
        ],
        (steps,),
        [pltpu.VMEM((length, d), f32)],
        "feed_forward", 14, deps,
    )


def loss_kernel(
    piece, steps, devices, code_ref, sc_ref, q_ref, pool_ref, cot_ref, xhat_ref, inv_ref, gt_ref,
    loss_ref, gd_ref, gr_ref, sums_ref, gp,
):
    step = pl.program_id(0)
    d = pool_ref.shape[1]

    @pl.when(step == 0)
    def _():
        gp[...] = jnp.zeros_like(gp)
        sums_ref[...] = jnp.zeros_like(sums_ref)

    @pl.when(step < steps)
    def _():
        queries = q_ref[:, :d]
        logits = nt(queries, pool_ref[...])
        lanes = lax.broadcasted_iota(jnp.int32, (1, logits.shape[1]), 1)
        owner = q_ref[:, d : d + CH].astype(f32).astype(jnp.int32)
        inner = q_ref[:, d + CH :].astype(f32).astype(jnp.int32)
        pos = code_ref(owner, sc_ref[7], devices) * SLOT + inner
        first = (pos[:, 0:1] == lanes).astype(f32)
        times = first
        for c in range(1, CH):
            times += (pos[:, c : c + 1] == lanes).astype(f32)
        held = times > 0.0
        top = jnp.max(jnp.where(held, logits, -jnp.inf), -1, keepdims=True)
        e = jnp.where(held, times * jnp.exp(jnp.minimum(logits - top, 0.0)), 0.0)
        total = jnp.sum(e, -1, keepdims=True)
        positive = jnp.sum(first * logits, -1, keepdims=True)
        loss_ref[...] = top + jnp.log(total) - positive
        grad = e[:, :128] * (1.0 / total) - first[:, :128]
        high = grad.astype(bf16)
        lower = (grad - high.astype(f32)).astype(bf16)
        gp[...] += (tn(high, queries) + tn(lower, queries))[:SLOT]

    @pl.when(step >= steps)
    def _():
        block = (step - steps) ^ sc_ref[0]
        places = block * piece + lax.broadcasted_iota(jnp.int32, (piece, 1), 0)
        grad = cot_ref[...].astype(f32)
        for j in range(PASS):
            grad += jnp.where(places == sc_ref[1 + j], gp[j : j + 1, :], 0.0)
        xhat = xhat_ref[...]
        back = norm_back(grad, xhat, inv_ref[...], gt_ref[...])
        gr_ref[...] = back
        down = back.astype(bf16)
        gd_ref[...] = down
        sums_ref[0:1, :] += jnp.sum(down.astype(f32), 0, keepdims=True)
        sums_ref[1:2, :] += jnp.sum(grad * xhat, 0, keepdims=True)
        sums_ref[2:3, :] += jnp.sum(grad, 0, keepdims=True)


def cube_place(owner, own, devices):
    off = owner ^ own
    z = off >> 3
    return (off & 1) * 16 + (z ^ (z >> 1)) * 4 + ((off >> 1) & 3)


def turned_place(owner, own, devices):
    off = owner - own
    return jnp.where(off < 0, off + devices, off)


def retrieval(sc, code_all, pooled, cot, xhat, inv, gain, piece, places, devices):
    count, width = code_all.shape
    length, d = cot.shape
    block = 256
    steps, pieces = count // block, length // piece
    first = lambda i: jnp.minimum(i, steps - 1)
    second = lambda i: jnp.maximum(i - steps, 0)
    part = lambda c: pl.BlockSpec((piece, c), lambda i, s: (second(i), 0))
    return call(
        functools.partial(loss_kernel, piece, steps, devices, places),
        sc,
        (code_all, pooled, cot, xhat, inv, gain),
        [
            pl.BlockSpec((block, width), lambda i, s: (first(i), 0)),
            whole(*pooled.shape), part(d), part(d), part(1), whole(1, d),
        ],
        [shape(f32, count, 1), shape(bf16, length, d), shape(f32, length, d), shape(f32, SLOT, d)],
        [
            pl.BlockSpec((block, 1), lambda i, s: (first(i), 0)), part(d), part(d), whole(SLOT, d),
        ],
        (steps + pieces,),
        [pltpu.VMEM((SLOT, d), f32)],
        "retrieval", 12,
    )


def feed_back_kernel(
    sc_ref, gd_ref, gr_ref, wd_ref, wu_ref, slope_ref, xhat_ref, inv_ref, go_ref, wo_ref,
    gug_ref, bup_ref, gr1_ref, gctx_ref, sums_ref,
    acc,
):
    step = pl.program_id(0)
    last = pl.num_programs(0) - 1

    @pl.when(step == 0)
    def _():
        acc[...] = gr_ref[...]

    @pl.when(step < last)
    def _():
        gact = nt(gd_ref[...], wd_ref[...])
        gup = (gact * slope_ref[0]).astype(bf16)
        gug_ref[0] = gup
        bup_ref[0] = jnp.sum(gup.astype(f32), 0, keepdims=True)
        acc[...] += nt(gup, wu_ref[...])

    @pl.when(step == last)
    def _():
        grad = acc[...]
        xhat = xhat_ref[...]
        back = norm_back(grad, xhat, inv_ref[...], go_ref[...])
        gr1_ref[...] = back
        gab = back.astype(bf16)
        gug_ref[0] = gab
        gctx_ref[...] = nt(gab, wo_ref[...]).astype(bf16)
        sums_ref[0:1, :] = jnp.sum(gab.astype(f32), 0, keepdims=True)
        sums_ref[1:2, :] = jnp.sum(grad * xhat, 0, keepdims=True)
        sums_ref[2:3, :] = jnp.sum(grad, 0, keepdims=True)


def feed_back(sc, gd, gr, wd, wu, slope, xhat, inv, go, wo, deps):
    length, d = gd.shape
    steps = slope.shape[0]
    at = lambda i: jnp.minimum(i, steps - 1)
    return call(
        feed_back_kernel,
        sc,
        (gd, gr, wd, wu, slope, xhat, inv, go, wo),
        [
            whole(length, d), whole(length, d),
            pl.BlockSpec((d, d), lambda i, s: (at(i), 0)),
            pl.BlockSpec((d, d), lambda i, s: (0, at(i))),
            pl.BlockSpec((1, length, d), lambda i, s: (at(i), 0, 0)),
            whole(length, d), whole(length, 1), whole(1, d), whole(d, d),
        ],
        [
            shape(bf16, steps + 1, length, d), shape(f32, steps, 1, d), shape(f32, length, d),
            shape(bf16, length, d), shape(f32, SLOT, d),
        ],
        [
            pl.BlockSpec((1, length, d), lambda i, s: (i, 0, 0)),
            pl.BlockSpec((1, 1, d), lambda i, s: (at(i), 0, 0)),
            whole(length, d), whole(length, d), whole(SLOT, d),
        ],
        (steps + 1,),
        [pltpu.VMEM((length, d), f32)],
        "feed_back", 0, deps,
    )


def attention_back_kernel(
    piece, sc_ref, q_ref, k_ref, v_ref, gctx_ref, lse_ref, wq_ref, wk_ref, wv_ref, gr_ref,
    gqkv_ref, gtok_ref, sums_ref,
    acc, bias, gkt, gvt,
):
    step = pl.program_id(0)
    length = q_ref.shape[0]

    @pl.when(step == 0)
    def _():
        bias[...] = segment_bias(sc_ref, length, piece)
        acc[...] = gr_ref[...]

    lse = lse_ref[0].T
    for h in range(GROUP):
        cols = slice(h * HEAD, (h + 1) * HEAD)
        q = q_ref[:, cols]
        k = k_ref[:, cols]
        gctx = gctx_ref[:, cols]
        scores = nt(q * jnp.asarray(SCALE, bf16), k) + bias[...]
        p = jnp.exp(scores - lse[:, h : h + 1])
        ga = nt(gctx, v_ref[:, cols])
        dots = jnp.sum(p * ga, -1, keepdims=True)
        g = (p * (ga - dots)).astype(bf16)
        gqkv_ref[0, :, cols] = (nn(g, k) * SCALE).astype(bf16)
        gkt[cols, :] = (tn(q, g) * SCALE).astype(bf16)
        gvt[cols, :] = tn(gctx, p.astype(bf16)).astype(bf16)
    gqkv_ref[1] = gkt[...].T
    gqkv_ref[2] = gvt[...].T
    gq, gk, gv = gqkv_ref[0], gqkv_ref[1], gqkv_ref[2]
    sums_ref[0:1, :] = jnp.sum(gq.astype(f32), 0, keepdims=True)
    sums_ref[1:2, :] = jnp.sum(gv.astype(f32), 0, keepdims=True)
    acc[...] += nt(gq, wq_ref[...]) + nt(gk, wk_ref[...]) + nt(gv, wv_ref[...])

    @pl.when(step == pl.num_programs(0) - 1)
    def _():
        gtok_ref[...] = acc[...].astype(bf16)


def attention_back(sc, q, k, v, gctx, lse, wq, wk, wv, gr, piece, deps):
    length, d = q.shape
    wide = GROUP * HEAD
    steps = d // wide
    cols = lambda r: pl.BlockSpec((r, wide), lambda i, s: (0, i))
    return call(
        functools.partial(attention_back_kernel, piece),
        sc,
        (q, k, v, gctx, lse, wq, wk, wv, gr),
        [
            cols(length), cols(length), cols(length), cols(length),
            pl.BlockSpec((1, SLOT, length), lambda i, s: (i, 0, 0)),
            cols(d), cols(d), cols(d), whole(length, d),
        ],
        [shape(bf16, 3, length, d), shape(bf16, length, d), shape(f32, SLOT, d)],
        [pl.BlockSpec((3, length, wide), lambda i, s: (0, 0, i)), whole(length, d), cols(SLOT)],
        (steps,),
        [
            pltpu.VMEM((length, d), f32), pltpu.VMEM((length, length), f32),
            pltpu.VMEM((wide, length), bf16), pltpu.VMEM((wide, length), bf16),
        ],
        "attention_back", 0, deps,
    )


def weight_total(two, lo_refs, lp_ref, go_ref, gp_ref):
    lo = lo_refs[0][...].reshape(lo_refs[0].shape[-2:])
    if len(lo_refs) > 1:
        lo = jnp.where(pl.program_id(0) < two, lo, lo_refs[1][...].reshape(lo.shape))
    return nn(lo, go_ref[0]) + nn(lp_ref[0, 0], gp_ref[0])


def weight_send_kernel(lefts, two, sc_ref, *refs):
    lo_refs, (lp_ref, go_ref, gp_ref, out_ref) = refs[:lefts], refs[lefts:]
    out_ref[0] = weight_total(two, lo_refs, lp_ref, go_ref, gp_ref).astype(bf16)


def weight_keep_kernel(lefts, two, sc_ref, *refs):
    lo_refs, (lp_ref, go_ref, gp_ref, recv_ref, keep_ref, send_ref) = refs[:lefts], refs[lefts:]
    total = weight_total(two, lo_refs, lp_ref, go_ref, gp_ref) + recv_ref[0].astype(f32)
    half = total.shape[0] // 2
    for h in range(2):
        rows = total[h * half : (h + 1) * half]

        @pl.when(sc_ref[2] == h)
        def _():
            keep_ref[0] = rows

        @pl.when(sc_ref[2] != h)
        def _():
            send_ref[0] = rows.astype(bf16)


def weight_specs(lefts, halves, grads, grads_p, other, steps, turn):
    x = (lambda s: 1 - s[0]) if other else (lambda s: s[0])
    specs = []
    for left in lefts:
        if left.ndim == 4:
            specs.append(
                pl.BlockSpec((1, 1) + left.shape[2:], lambda i, s: (2 * x(s) + s[1], i, 0, 0))
            )
        else:
            specs.append(pl.BlockSpec((1,) + left.shape[1:], lambda i, s: (2 * x(s) + s[1], 0, 0)))
    specs.append(pl.BlockSpec((1, 1) + halves.shape[2:], lambda i, s: (x(s), turn(i), 0, 0)))
    one = grads.shape[0] == 1
    block = pl.BlockSpec((1,) + grads.shape[1:], lambda i, s: (0 if one else i, 0, 0))
    return (*lefts, halves, grads, grads_p), specs + [block, block]


def weight_send(sc, operands, steps, two, turn, name, deps=(), micros=0):
    args, specs = weight_specs(*operands, True, steps, turn)
    rows, wide = operands[1].shape[2], operands[2].shape[2]
    return call(
        functools.partial(weight_send_kernel, len(operands[0]), two),
        sc, args, specs, shape(bf16, steps, rows, wide),
        pl.BlockSpec((1, rows, wide), lambda i, s: (i, 0, 0)), (steps,), [],
        name, micros, deps,
    )


def weight_keep(sc, operands, recv, steps, two, turn, name, deps=(), micros=0):
    args, specs = weight_specs(*operands, False, steps, turn)
    rows, wide = operands[1].shape[2], operands[2].shape[2]
    half = pl.BlockSpec((1, rows // 2, wide), lambda i, s: (i, 0, 0))
    return call(
        functools.partial(weight_keep_kernel, len(operands[0]), two),
        sc, args + (recv,), specs + [pl.BlockSpec((1, rows, wide), lambda i, s: (i, 0, 0))],
        [shape(f32, steps, rows // 2, wide), shape(bf16, steps, rows // 2, wide)],
        [half, half], (steps,), [],
        name, micros, deps,
    )


def place_kernel(spots, sc_ref, own_ref, far_ref, *out_refs):
    half = own_ref.shape[1]
    wide = own_ref.shape[2]
    for n, (out, down, left) in enumerate(spots):
        for part, side in ((own_ref, 0), (far_ref, 1)):
            h = sc_ref[2] ^ side
            top = pl.multiple_of(down * 2 * half + h * half, half)
            out_refs[out][pl.ds(top, half), left * wide : (left + 1) * wide] = part[n].astype(f32)


def place(sc, own, far, spots, dims, name):
    return call(
        functools.partial(place_kernel, spots),
        sc, (own, far), [whole(*own.shape), whole(*far.shape)],
        [shape(f32, *dim) for dim in dims], [whole(*dim) for dim in dims], (1,), [],
        name, 3,
    )


def flip(value, axis, mask):
    count = lax.axis_size(axis)
    return lax.ppermute(value, axis, [(i, i ^ mask) for i in range(count)])


def flip_both(value, row_mask, seq_mask):
    rows, seq = lax.axis_size("rows"), lax.axis_size("seq")
    pairs = [
        (r * seq + s, (r ^ row_mask) * seq + (s ^ seq_mask)) for r in range(rows) for s in range(seq)
    ]
    return lax.ppermute(value, ("rows", "seq"), pairs)


def row_flips():
    count = lax.axis_size("rows")
    assert count >= 8 and count & (count - 1) == 0
    return [2, 6] + [1 << b for b in range(3, count.bit_length() - 1)]


def over_rows(keep, send, masks):
    value = (keep + flip(send, "rows", 1).astype(f32)).astype(bf16)
    for mask in masks:
        value = (value.astype(f32) + flip(value, "rows", mask).astype(f32)).astype(bf16)
    return value, flip(value, "rows", 1)


def spread(rows):
    own = lax.axis_index("seq")
    count = lax.axis_size("seq")
    assert rows.shape[0] == count
    pieces = [
        flip(lax.dynamic_index_in_dim(rows, own ^ mask, 0, keepdims=False), "seq", mask)
        if mask
        else lax.dynamic_index_in_dim(rows, own, 0, keepdims=False)
        for mask in range(count)
    ]
    return jnp.concatenate(pieces, 0)


def gather_back(row, count):
    own = lax.axis_index("seq")
    row = row.reshape(count, -1, row.shape[-1])
    out = jnp.zeros_like(row)
    for mask in range(count):
        piece = flip(row[mask], "seq", mask) if mask else row[0]
        out = lax.dynamic_update_index_in_dim(out, piece, own ^ mask, 0)
    return out


def per_device(
    tokens,
    w_query,
    b_query,
    w_key,
    w_value,
    b_value,
    w_out,
    b_out,
    gain_one,
    shift_one,
    w_up,
    b_up,
    w_down,
    b_down,
    gain_two,
    shift_two,
    passage_starts,
    queries,
    choices,
    cotangent,
):
    seq_count = lax.axis_size("seq")
    row_count = lax.axis_size("rows")
    own_s = lax.axis_index("seq")
    own_r = lax.axis_index("rows")
    row_block, piece, d = tokens.shape
    assert row_block == seq_count == 4
    ff = w_up.shape[1]
    quarter = d // 4
    core, xside = own_s % 2, own_s // 2
    own_lin = own_r * seq_count + own_s
    devices = row_count * seq_count
    masks = row_flips()
    wsc = jnp.stack([xside, core, own_r % 2, own_r % 2]).astype(jnp.int32)
    starts = lax.dynamic_index_in_dim(passage_starts, own_s, 0, keepdims=False)
    sc = jnp.concatenate([own_s[None].astype(jnp.int32), starts, own_lin[None].astype(jnp.int32)])
    row = lambda v: v.reshape(1, -1)
    swap = lambda t: flip(t, "seq", 1)

    x = spread(tokens)

    code = jnp.concatenate(
        [queries, (choices // PASS).astype(bf16), (choices % PASS).astype(bf16)], axis=1
    )
    code_all = lax.all_gather(code, ("rows", "seq"), axis=0, tiled=True)

    cot = spread(cotangent)

    q, k, v, ctxt, lse, xt, xhat_one, inv_one, hid, hidt = attention_forward(
        sc, x, w_query, w_key, w_value, row(b_query), row(b_value), w_out, row(b_out),
        row(gain_one), row(shift_one), piece,
    )
    actt, slope, xhat_two, inv_two, mixed_row, pool = feed_forward(
        sc, hid, w_up, row(b_up), w_down, row(b_down), row(gain_two), row(shift_two), piece, (cot,)
    )

    pool = pool.astype(bf16)
    if row_count == 8:
        near = jnp.concatenate(
            [pool, flip(pool, "seq", 2), flip(pool, "rows", 1), flip_both(pool, 1, 2)], 0
        )
        mid = jnp.concatenate(
            [near, flip(near, "rows", 2), flip(near, "rows", 6), flip(near, "rows", 4)], 0
        )
        pooled = jnp.concatenate([mid, flip(mid, "seq", 1)], 0)
        places = cube_place
    else:
        pooled = lax.all_gather(pool, ("rows", "seq"), axis=0, tiled=True)
        pooled = jnp.roll(pooled, -own_lin * SLOT, 0)
        places = turned_place

    other_half = lambda t: lax.dynamic_index_in_dim(
        t.reshape(2, 2, -1, quarter, t.shape[-1]), 1 - core, 1, keepdims=False
    )
    halves = swap(
        jnp.concatenate([other_half(hidt), other_half(ctxt), other_half(xt), other_half(actt)], 1)
    )
    quarters = lambda t: t.reshape(4, -1, t.shape[-1])

    losses_all, gd, gr_two, sums_two = retrieval(
        sc, code_all, pooled, cot, xhat_two, inv_two, row(gain_two), piece, places, devices
    )
    query_losses = lax.dynamic_slice_in_dim(
        losses_all[:, 0], own_lin * queries.shape[0], queries.shape[0]
    )

    down_ops = ((actt.reshape(4, 4, quarter, -1),), halves, gd[None], swap(gd)[None])
    down_turn = lambda i: 3 + i
    down_sent = weight_send(wsc, down_ops, 4, 0, down_turn, "down_send")
    down_got = flip(down_sent, "seq", 2)

    gug, bup, gr_one, gctx, sums_one = feed_back(
        sc, gd, gr_two, w_down, w_up, slope, xhat_one, inv_one, row(gain_one), w_out, (down_sent,)
    )
    down_parts = weight_keep(wsc, down_ops, down_got, 4, 0, down_turn, "down_keep", (gug,), 100)
    up_ops = ((quarters(hidt), quarters(ctxt)), halves, gug, swap(gug))
    up_turn = lambda i: i // 4
    up_sent = weight_send(wsc, up_ops, 5, 4, up_turn, "up_send", (down_parts[0],))
    up_got = flip(up_sent, "seq", 2)

    gqkv, gtok, sums_qkv = attention_back(
        sc, q, k, v, gctx, lse, w_query, w_key, w_value, gr_one, piece, (up_sent,)
    )
    up_parts = weight_keep(wsc, up_ops, up_got, 5, 4, up_turn, "up_keep", (gqkv,), 100)
    qkv_ops = ((quarters(xt),), halves, gqkv, swap(gqkv))
    qkv_turn = lambda i: 2
    qkv_sent = weight_send(wsc, qkv_ops, 3, 0, qkv_turn, "qkv_send", (up_parts[0],))
    qkv_got = flip(qkv_sent, "seq", 2)

    down_sum = over_rows(*down_parts, masks)
    up_sum = over_rows(*up_parts, masks)
    qkv_parts = weight_keep(wsc, qkv_ops, qkv_got, 3, 0, qkv_turn, "qkv_keep", (up_parts[0],))
    qkv_sum = over_rows(*qkv_parts, masks)

    vec = jnp.concatenate([sums_qkv[:2], sums_one[:3], sums_two[:3]], 0)
    vec = vec.reshape(8, 4, quarter).transpose(1, 0, 2).reshape(4, 2, d)
    vec = jnp.concatenate([vec, bup.reshape(4, ff // 4 // d, d)], 1)
    vec = vec.reshape(2, 2, 3, d)
    vec = lax.dynamic_index_in_dim(vec, core, 1, keepdims=False) + swap(
        lax.dynamic_index_in_dim(vec, 1 - core, 1, keepdims=False)
    )
    vec = lax.dynamic_index_in_dim(vec, xside, 0, keepdims=False) + flip(
        lax.dynamic_index_in_dim(vec, 1 - xside, 0, keepdims=False), "seq", 2
    )
    for mask in [1] + masks:
        vec = vec + flip(vec, "rows", mask)

    mixed = gather_back(mixed_row, seq_count)
    grad_tokens = gather_back(gtok, seq_count)

    (grad_down,) = place(
        wsc, *down_sum, [(0, n, 0) for n in range(4)], [(4 * quarter, d)], "down_place"
    )
    grad_up, grad_o = place(
        wsc, *up_sum, [(0, 0, n) for n in range(4)] + [(1, 0, 0)],
        [(quarter, ff), (quarter, d)], "up_place",
    )
    grad_q, grad_k, grad_v = place(
        wsc, *qkv_sum, [(n, 0, 0) for n in range(3)], [(quarter, d)] * 3, "qkv_place"
    )

    eight = vec[:2].reshape(8, quarter)
    return (
        mixed,
        query_losses,
        grad_tokens,
        grad_q,
        eight[0],
        grad_k,
        grad_v,
        eight[1],
        grad_o,
        eight[2],
        eight[3],
        eight[4],
        grad_up,
        vec[2],
        grad_down,
        eight[5],
        eight[6],
        eight[7],
    )


def solution(mesh):
    weights = (P(),) * 15
    placed = (
        (P("rows", "seq", None),)
        + weights
        + (
            P("rows", None),
            P(("rows", "seq"), None),
            P(("rows", "seq"), None),
            P("rows", "seq", None),
        )
    )
    return jax.shard_map(
        per_device,
        mesh=mesh,
        in_specs=placed,
        out_specs=(
            P("rows", "seq", None),
            P(("rows", "seq")),
            P("rows", "seq", None),
            P("seq", None),
            P("seq"),
            P("seq", None),
            P("seq", None),
            P("seq"),
            P("seq", None),
            P("seq"),
            P("seq"),
            P("seq"),
            P("seq", None),
            P("seq"),
            P("seq", None),
            P("seq"),
            P("seq"),
            P("seq"),
        ),
        check_vma=False,
    )
```

time: 1020 us -> 322 us (0.32)
  the two profiles are of different devices: /device:TPU:0 before, /device:TPU:16 now
where the time goes in v2:
time: 322 us; the launch traced here: 320 us
  Pallas kernels  134 us (42%)
  waiting for transfers between devices  88.8 us (28%)
  starting transfers between devices  41.5 us (13%)
  local copies, waits for them, and re-layouts  29.8 us (9%)
  between operations  14.8 us (5%)
  other arithmetic  11.2 us (3%)
    pallas_call x14, Pallas kernels, call(): pl.pallas_call(body, grid_spec=pltpu.PrefetchScalarGridSpec(num_scalar_pr...  134 us
    ppermute x42, waiting for transfers between devices, flip(): return lax.ppermute(value, axis, [(i, i ^ mask) for i in range(count)])  88.8 us
    ppermute x42, starting transfers between devices, flip(): return lax.ppermute(value, axis, [(i, i ^ mask) for i in range(count)])  40 us
    unnamed x88, local copies, waits for them, and re-layouts  8.66 us
  transfers between devices with their start and end apart: 44, of which 15 were waited for; matrix products, arithmetic and copies ran while one was open for 10% of the time, Pallas kernels for 39%

profile of v2, /device:TPU:16, one launch (start us, length us, event | category | flops | bytes accessed | tf_op | source)
XLA Modules:
  0.0 320.1 jit_solution(17990363594674827518)
XLA Ops:
  20.9 17.8 %attention_forward.1 = (bf16[512,768]{1,0:T(8,128)(2,1)}, bf16[512,768]{1,0:T(8,128)(2,1)}, bf16[512,768]{1,0:T(8,128)(2,1)}, bf16[768,512]{1,0:T(8,128)(2,1)}, ...) custom-call(s32[8]{0:T(128)} %pad_add_fusion.sc_ref, ...), custom_call_target="tpu_custom_call" | custom-call | flops 20700000256 | tf_op jit(solution)/shard_map/attention_forward/pallas_call | solution.py:97
  39.7 17.7 %feed_forward.1 = (bf16[3072,512]{1,0:T(8,128)(2,1)}, f32[4,512,768]{2,1,0:T(8,128)}, f32[512,768]{1,0:T(8,128)}, f32[512,1]{1,0:T(8,128)}, bf16[512,768]{1,0:T(8,128)(2,1)}, /*index=5*/f32[8,768]{1,0:T(8,128)}) custom-call(s32[8]{0:T(128)} %pad_add_fusion.sc_ref, bf16[512,768]{1,0:T(8,128)(2,1)} %get-tuple-element.57.refs_0_, bf16[768,3072]{1,0:T(8,128)(2,1)} %refs_3_.5, ...), custom_call_target="tpu_custom_call" | custom-call | flops 16099999744 | tf_op jit(solution)/shard_map/feed_forward/pallas_call | solution.py:97
  66.8 2.8 collective-permute-start.14
  69.6 3.8 %collective-permute-done.13 = bf16[32,768]{1,0:T(8,128)(2,1)S(1)} collective-permute-done((bf16[32,768]{1,0:T(8,128)(2,1)S(1)}, bf16[32,768]{1,0:T(8,128)(2,1)S(1)}, u32[]{:S(2)}, u32[]{:S(2)}) %collective-permute-start.13) | collective-permute-done | bytes 49184 | tf_op jit(solution)/shard_map/ppermute | solution.py:572
  75.7 14.7 %retrieval.1 = (f32[1024,1]{1,0:T(8,128)}, bf16[512,768]{1,0:T(8,128)(2,1)}, f32[512,768]{1,0:T(8,128)}, f32[8,768]{1,0:T(8,128)}) custom-call(s32[8]{0:T(128)} %pad_add_fusion.sc_ref, bf16[1024,832]{1,0:T(8,128)(2,1)} %all-gather.2.cloned.1.call-done.refs_0_, bf16[256,768]{1,0:T(8,128)(2,1)} %copy-done.35, ...), custom_call_target="tpu_custom_call" | custom-call | flops 13799999488 | tf_op jit(solution)/shard_map/retrieval/pallas_call | solution.py:97
  93.9 5.9 %down_send.1.refs_9_ = bf16[4,192,768]{2,1,0:T(8,128)(2,1)} custom-call(s32[4]{0:T(128)} %pad_add_fusion.1.sc_ref, bf16[4,4,192,512]{3,2,1,0:T(8,128)(2,1)} %bitcast.89, bf16[2,7,192,512]{3,2,1,0:T(8,128)(2,1)} %copy-done.2, bf16[1,512,768]{2,1,0:T(8,128)(2,1)} %bitcast.94, bf16[1,512,768]{2,1,0:T(8,128)(2,1)} %bitcast.102), custom_call_target="tpu_custom_call" | custom-call | tf_op jit(solution)/shard_map/down_send/pallas_call | solution.py:97
  101.2 15.5 %feed_back.1 = (bf16[5,512,768]{2,1,0:T(8,128)(2,1)}, f32[4,1,768]{2,1,0:T(1,128)}, f32[512,768]{1,0:T(8,128)}, bf16[512,768]{1,0:T(8,128)(2,1)}, f32[8,768]{1,0:T(8,128)}) custom-call(s32[8]{0:T(128)} %pad_add_fusion.sc_ref, bf16[512,768]{1,0:T(8,128)(2,1)} %get-tuple-element.66.refs_0_, f32[512,768]{1,0:T(8,128)} %get-tuple-element.67.refs_1_, ...), custom_call_target="tpu_custom_call" | custom-call | tf_op jit(solution)/shard_map/feed_back/pallas_call | solution.py:97
  116.8 11.2 %collective-permute-done.19.refs_4_ = bf16[4,192,768]{2,1,0:T(8,128)(2,1)S(1)} collective-permute-done((bf16[4,192,768]{2,1,0:T(8,128)(2,1)}, bf16[4,192,768]{2,1,0:T(8,128)(2,1)S(1)}, u32[]{:S(2)}, u32[]{:S(2)}) %collective-permute-start.19) | collective-permute-done | bytes 1179680 | tf_op jit(solution)/shard_map/ppermute | solution.py:572
  129.0 6.1 %down_keep.1 = (f32[4,96,768]{2,1,0:T(8,128)}, bf16[4,96,768]{2,1,0:T(8,128)(2,1)}) custom-call(s32[4]{0:T(128)} %pad_add_fusion.1.sc_ref, bf16[4,4,192,512]{3,2,1,0:T(8,128)(2,1)} %bitcast.90, bf16[2,7,192,512]{3,2,1,0:T(8,128)(2,1)} %copy-done.2, bf16[1,512,768]{2,1,0:T(8,128)(2,1)} %bitcast.95, bf16[1,512,768]{2,1,0:T(8,128)(2,1)} %bitcast.103, ...), custom_call_target="tpu_custom_call" | custom-call | flops 115000000512 | tf_op jit(solution)/shard_map/down_keep/pallas_call | solution.py:97
  138.6 7.9 %up_send.1.refs_9_ = bf16[5,192,768]{2,1,0:T(8,128)(2,1)} custom-call(s32[4]{0:T(128)} %pad_add_fusion.1.sc_ref, bf16[4,192,512]{2,1,0:T(8,128)(2,1)} %bitcast.99, bf16[4,192,512]{2,1,0:T(8,128)(2,1)} %bitcast.96, bf16[2,7,192,512]{3,2,1,0:T(8,128)(2,1)} %copy-done.2, bf16[5,512,768]{2,1,0:T(8,128)(2,1)} %get-tuple-element.78.refs_5_.refs_3_, ...), custom_call_target="tpu_custom_call" | custom-call | tf_op jit(solution)/shard_map/up_send/pallas_call | solution.py:97
  153.7 10.4 %collective-permute-done.40 = bf16[4,96,768]{2,1,0:T(8,128)(2,1)S(1)} collective-permute-done((bf16[4,96,768]{2,1,0:T(8,128)(2,1)S(1)}, bf16[4,96,768]{2,1,0:T(8,128)(2,1)S(1)}, u32[]{:S(2)}, u32[]{:S(2)}) %collective-permute-start.40) | collective-permute-done | bytes 589856 | tf_op jit(solution)/shard_map/ppermute | solution.py:572
  164.4 17.9 %attention_back.1 = (bf16[3,512,768]{2,1,0:T(8,128)(2,1)}, bf16[512,768]{1,0:T(8,128)(2,1)}, f32[8,768]{1,0:T(8,128)}) custom-call(s32[8]{0:T(128)} %pad_add_fusion.sc_ref, bf16[512,768]{1,0:T(8,128)(2,1)} %get-tuple-element.63.refs_0_, bf16[512,768]{1,0:T(8,128)(2,1)} %get-tuple-element.64.refs_1_, bf16[512,768]{1,0:T(8,128)(2,1)} %get-tuple-element.65.refs_2_, ...), custom_call_target="tpu_custom_call" | custom-call | tf_op jit(solution)/shard_map/attention_back/pallas_call | solution.py:97
  184.1 8.5 %up_keep.1 = (f32[5,96,768]{2,1,0:T(8,128)}, bf16[5,96,768]{2,1,0:T(8,128)(2,1)}) custom-call(s32[4]{0:T(128)} %pad_add_fusion.1.sc_ref, bf16[4,192,512]{2,1,0:T(8,128)(2,1)} %bitcast.100, bf16[4,192,512]{2,1,0:T(8,128)(2,1)} %bitcast.97, bf16[2,7,192,512]{3,2,1,0:T(8,128)(2,1)} %copy-done.2, bf16[5,512,768]{2,1,0:T(8,128)(2,1)} %get-tuple-element.78.refs_5_.refs_3_, ...), custom_call_target="tpu_custom_call" | custom-call | flops 115000000512 | tf_op jit(solution)/shard_map/up_keep/pallas_call | solution.py:97
  204.1 5.6 %qkv_send.1 = bf16[3,192,768]{2,1,0:T(8,128)(2,1)} custom-call(s32[4]{0:T(128)} %pad_add_fusion.1.sc_ref, bf16[4,192,512]{2,1,0:T(8,128)(2,1)} %bitcast.91, bf16[2,7,192,512]{3,2,1,0:T(8,128)(2,1)} %copy-done.2, bf16[3,512,768]{2,1,0:T(8,128)(2,1)} %get-tuple-element.81.refs_6_.refs_2_, bf16[3,512,768]{2,1,0:T(8,128)(2,1)} %copy-done.4, ...), custom_call_target="tpu_custom_call" | custom-call | tf_op jit(solution)/shard_map/qkv_send/pallas_call | solution.py:97
  213.5 2.7 collective-permute-start.36
  217.9 6.6 %collective-permute-done.42.refs_1_ = bf16[4,96,768]{2,1,0:T(8,128)(2,1)S(1)} collective-permute-done((bf16[4,96,768]{2,1,0:T(8,128)(2,1)S(1)}, bf16[4,96,768]{2,1,0:T(8,128)(2,1)S(1)}, u32[]{:S(2)}, u32[]{:S(2)}) %collective-permute-start.42) | collective-permute-done | bytes 589856 | tf_op jit(solution)/shard_map/ppermute | solution.py:572
  225.3 3.5 %down_place.1 = f32[768,768]{1,0:T(8,128)} custom-call(s32[4]{0:T(128)} %pad_add_fusion.1.sc_ref, bf16[4,96,768]{2,1,0:T(8,128)(2,1)} %copy-done.18, bf16[4,96,768]{2,1,0:T(8,128)(2,1)} %copy-done.39), custom_call_target="tpu_custom_call" | custom-call | flops 3449999872 | tf_op jit(solution)/shard_map/down_place/pallas_call | solution.py:97
  236.0 6.0 %qkv_keep.1 = (f32[3,96,768]{2,1,0:T(8,128)}, bf16[3,96,768]{2,1,0:T(8,128)(2,1)}) custom-call(s32[4]{0:T(128)} %pad_add_fusion.1.sc_ref, bf16[4,192,512]{2,1,0:T(8,128)(2,1)} %bitcast.92, bf16[2,7,192,512]{3,2,1,0:T(8,128)(2,1)} %copy-done.2, bf16[3,512,768]{2,1,0:T(8,128)(2,1)} %get-tuple-element.81.refs_6_.refs_2_, bf16[3,512,768]{2,1,0:T(8,128)(2,1)} %copy-done.4, ...), custom_call_target="tpu_custom_call" | custom-call | tf_op jit(solution)/shard_map/qkv_keep/pallas_call | solution.py:97
  247.7 6.1 %collective-permute-done.26 = bf16[3,96,768]{2,1,0:T(8,128)(2,1)} collective-permute-done((bf16[3,96,768]{2,1,0:T(8,128)(2,1)}, bf16[3,96,768]{2,1,0:T(8,128)(2,1)}, u32[]{:S(2)}, u32[]{:S(2)}) %collective-permute-start.26) | collective-permute-done | bytes 442400 | tf_op jit(solution)/shard_map/ppermute | solution.py:572
  258.4 18.7 %collective-permute-done.37 = bf16[5,96,768]{2,1,0:T(8,128)(2,1)S(1)} collective-permute-done((bf16[5,96,768]{2,1,0:T(8,128)(2,1)S(1)}, bf16[5,96,768]{2,1,0:T(8,128)(2,1)S(1)}, u32[]{:S(2)}, u32[]{:S(2)}) %collective-permute-start.37) | collective-permute-done | bytes 737312 | tf_op jit(solution)/shard_map/ppermute | solution.py:572
  280.2 16.8 %collective-permute-done.28 = bf16[3,96,768]{2,1,0:T(8,128)(2,1)S(1)} collective-permute-done((bf16[3,96,768]{2,1,0:T(8,128)(2,1)S(1)}, bf16[3,96,768]{2,1,0:T(8,128)(2,1)S(1)}, u32[]{:S(2)}, u32[]{:S(2)}) %collective-permute-start.28) | collective-permute-done | bytes 442400 | tf_op jit(solution)/shard_map/ppermute | solution.py:572
  299.6 3.8 %up_place.1 = (f32[192,3072]{1,0:T(8,128)}, f32[192,768]{1,0:T(8,128)}) custom-call(s32[4]{0:T(128)} %pad_add_fusion.1.sc_ref, bf16[5,96,768]{2,1,0:T(8,128)(2,1)} %copy-done.17, bf16[5,96,768]{2,1,0:T(8,128)(2,1)} %copy-done.38), custom_call_target="tpu_custom_call" | custom-call | flops 3449999872 | tf_op jit(solution)/shard_map/up_place/pallas_call | solution.py:97
  303.3 6.0 %collective-permute-done.29.refs_1_ = bf16[3,96,768]{2,1,0:T(8,128)(2,1)S(1)} collective-permute-done((bf16[3,96,768]{2,1,0:T(8,128)(2,1)S(1)}, bf16[3,96,768]{2,1,0:T(8,128)(2,1)S(1)}, u32[]{:S(2)}, u32[]{:S(2)}) %collective-permute-start.29) | collective-permute-done | bytes 442400 | tf_op jit(solution)/shard_map/ppermute | solution.py:572
  310.0 3.2 %qkv_place.1 = (f32[192,768]{1,0:T(8,128)}, f32[192,768]{1,0:T(8,128)}, f32[192,768]{1,0:T(8,128)}) custom-call(s32[4]{0:T(128)} %pad_add_fusion.1.sc_ref, bf16[3,96,768]{2,1,0:T(8,128)(2,1)} %copy-done.19, bf16[3,96,768]{2,1,0:T(8,128)(2,1)} %copy-done.40), custom_call_target="tpu_custom_call" | custom-call | flops 3449999872 | tf_op jit(solution)/shard_map/qkv_place/pallas_call | solution.py:97
  (232 shorter events, 86.4 us)
Async XLA Ops:
  7.2 67.7 %all-gather.2.cloned.1.call-start = ((), (), s32[]{:S(2)}) async-start(), calls=%async_computation | async-start | bytes 1892352 | tf_op jit(solution)/shard_map/all_gather | solution.py:664
  10.8 27.9 %collective-permute-start.3 = (bf16[128,768]{1,0:T(8,128)(2,1)S(1)}, bf16[128,768]{1,0:T(8,128)(2,1)S(1)}, u32[]{:S(2)}, u32[]{:S(2)}) collective-permute-start(bf16[128,768]{1,0:T(8,128)(2,1)S(1)} %get-tuple-element.105), channel_id=1, source_target_pairs={{0,1},{1,0},{2,3},{3,2},{4,5},{5,4},{6,7},{7,6},{8,9},{9,8},{10,11... | collective-permute-start | bytes 589832 | tf_op jit(solution)/shard_map/ppermute | solution.py:572
  11.3 27.5 %collective-permute-start.4 = (bf16[128,768]{1,0:T(8,128)(2,1)S(1)}, bf16[128,768]{1,0:T(8,128)(2,1)S(1)}, u32[]{:S(2)}, u32[]{:S(2)}) collective-permute-start(bf16[128,768]{1,0:T(8,128)(2,1)S(1)} %get-tuple-element.107), channel_id=1, source_target_pairs={{0,2},{1,3},{2,0},{3,1},{4,6},{5,7},{6,4},{7,5},{8,10},{9,11},{10,... | collective-permute-start | bytes 589832 | tf_op jit(solution)/shard_map/ppermute | solution.py:572
  18.8 20.0 %collective-permute-start.5 = (bf16[128,768]{1,0:T(8,128)(2,1)S(1)}, bf16[128,768]{1,0:T(8,128)(2,1)S(1)}, u32[]{:S(2)}, u32[]{:S(2)}) collective-permute-start(bf16[128,768]{1,0:T(8,128)(2,1)S(1)} %get-tuple-element.106), channel_id=1, source_target_pairs={{0,3},{1,2},{2,1},{3,0},{4,7},{5,6},{6,5},{7,4},{8,11},{9,10},{10,... | collective-permute-start | bytes 589832 | tf_op jit(solution)/shard_map/ppermute | solution.py:572
  65.1 26.2 %collective-permute-start.16 = (bf16[2,7,192,512]{3,2,1,0:T(8,128)(2,1)}, bf16[2,7,192,512]{3,2,1,0:T(8,128)(2,1)S(1)}, u32[]{:S(2)}, u32[]{:S(2)}) collective-permute-start(bf16[2,7,192,512]{3,2,1,0:T(8,128)(2,1)} %pad_maximum_fusion), channel_id=1, source_target_pairs={{0,1},{1,0},{2,3},{3,2},{4,5},{5,4},{6,7},{7,6},{8,9},{9,8},{10,11... | collective-permute-start | bytes 8257544 | tf_op jit(solution)/shard_map/ppermute | solution.py:572
  99.8 28.2 %collective-permute-start.19 = (bf16[4,192,768]{2,1,0:T(8,128)(2,1)}, bf16[4,192,768]{2,1,0:T(8,128)(2,1)S(1)}, u32[]{:S(2)}, u32[]{:S(2)}) collective-permute-start(bf16[4,192,768]{2,1,0:T(8,128)(2,1)} %down_send.1.refs_9_), channel_id=1, source_target_pairs={{0,2},{1,3},{2,0},{3,1},{4,6},{5,7},{6,4},{7,5},{8,10},{9,11},{10,... | collective-permute-start | bytes 3538952 | tf_op jit(solution)/shard_map/ppermute | solution.py:572
  116.7 21.9 %collective-permute-start.18 = (bf16[5,512,768]{2,1,0:T(8,128)(2,1)}, bf16[5,512,768]{2,1,0:T(8,128)(2,1)}, u32[]{:S(2)}, u32[]{:S(2)}) collective-permute-start(bf16[5,512,768]{2,1,0:T(8,128)(2,1)} %get-tuple-element.78.refs_5_.refs_3_), channel_id=1, source_target_pairs={{0,1},{1,0},{2,3},{3,2},{4,5},{5,4},{6,7},{7,6},{8,9},{9,8},{10,11... | collective-permute-start | bytes 11796488 | tf_op jit(solution)/shard_map/ppermute | solution.py:572
  136.7 15.4 %collective-permute-start.6 = (bf16[128,768]{1,0:T(8,128)(2,1)S(1)}, bf16[128,768]{1,0:T(8,128)(2,1)S(1)}, u32[]{:S(2)}, u32[]{:S(2)}) collective-permute-start(bf16[128,768]{1,0:T(8,128)(2,1)S(1)} %get-tuple-element.103), channel_id=1, source_target_pairs={{0,1},{1,0},{2,3},{3,2},{4,5},{5,4},{6,7},{7,6},{8,9},{9,8},{10,11... | collective-permute-start | bytes 589832 | tf_op jit(solution)/shard_map/ppermute | solution.py:572
  136.8 15.4 %collective-permute-start.7 = (bf16[128,768]{1,0:T(8,128)(2,1)S(1)}, bf16[128,768]{1,0:T(8,128)(2,1)S(1)}, u32[]{:S(2)}, u32[]{:S(2)}) collective-permute-start(bf16[128,768]{1,0:T(8,128)(2,1)S(1)} %get-tuple-element.102), channel_id=1, source_target_pairs={{0,2},{1,3},{2,0},{3,1},{4,6},{5,7},{6,4},{7,5},{8,10},{9,11},{10,... | collective-permute-start | bytes 589832 | tf_op jit(solution)/shard_map/ppermute | solution.py:572
  146.5 36.5 %collective-permute-start.24 = (bf16[5,192,768]{2,1,0:T(8,128)(2,1)}, bf16[5,192,768]{2,1,0:T(8,128)(2,1)S(1)}, u32[]{:S(2)}, u32[]{:S(2)}) collective-permute-start(bf16[5,192,768]{2,1,0:T(8,128)(2,1)} %up_send.1.refs_9_), channel_id=1, source_target_pairs={{0,2},{1,3},{2,0},{3,1},{4,6},{5,7},{6,4},{7,5},{8,10},{9,11},{10,... | collective-permute-start | bytes 4423688 | tf_op jit(solution)/shard_map/ppermute | solution.py:572
  164.2 36.0 %collective-permute-start.41 = (bf16[4,96,768]{2,1,0:T(8,128)(2,1)S(1)}, bf16[4,96,768]{2,1,0:T(8,128)(2,1)S(1)}, u32[]{:S(2)}, u32[]{:S(2)}) collective-permute-start(bf16[4,96,768]{2,1,0:T(8,128)(2,1)S(1)} %add_convert_fusion.4), channel_id=1, source_target_pairs={{0,24},{4,28},{8,16},{12,20},{16,8},{20,12},{24,0},{28,4},{1,25},{... | collective-permute-start | bytes 1769480 | tf_op jit(solution)/shard_map/ppermute | solution.py:572
  183.0 19.7 %collective-permute-start.23 = (bf16[3,512,768]{2,1,0:T(8,128)(2,1)}, bf16[3,512,768]{2,1,0:T(8,128)(2,1)S(1)}, u32[]{:S(2)}, u32[]{:S(2)}) collective-permute-start(bf16[3,512,768]{2,1,0:T(8,128)(2,1)} %get-tuple-element.81.refs_6_.refs_2_), channel_id=1, source_target_pairs={{0,1},{1,0},{2,3},{3,2},{4,5},{5,4},{6,7},{7,6},{8,9},{9,8},{10,11... | collective-permute-start | bytes 7077896 | tf_op jit(solution)/shard_map/ppermute | solution.py:572
  192.6 19.6 %collective-permute-start.35 = (bf16[5,96,768]{2,1,0:T(8,128)(2,1)}, bf16[5,96,768]{2,1,0:T(8,128)(2,1)}, u32[]{:S(2)}, u32[]{:S(2)}) collective-permute-start(bf16[5,96,768]{2,1,0:T(8,128)(2,1)} %get-tuple-element.92), channel_id=1, source_target_pairs={{0,4},{4,0},{8,12},{12,8},{16,20},{20,16},{24,28},{28,24},{1,5},{5... | collective-permute-start | bytes 2211848 | tf_op jit(solution)/shard_map/ppermute | solution.py:572
  200.3 24.2 %collective-permute-start.42 = (bf16[4,96,768]{2,1,0:T(8,128)(2,1)S(1)}, bf16[4,96,768]{2,1,0:T(8,128)(2,1)S(1)}, u32[]{:S(2)}, u32[]{:S(2)}) collective-permute-start(bf16[4,96,768]{2,1,0:T(8,128)(2,1)S(1)} %add_convert_fusion.3.refs_0_), channel_id=1, source_target_pairs={{0,4},{4,0},{8,12},{12,8},{16,20},{20,16},{24,28},{28,24},{1,5},{5... | collective-permute-start | bytes 1769480 | tf_op jit(solution)/shard_map/ppermute | solution.py:572
  201.2 15.1 %collective-permute-start.31 = (f32[3,768]{1,0:T(4,128)S(1)}, f32[3,768]{1,0:T(4,128)S(1)}, u32[]{:S(2)}, u32[]{:S(2)}) collective-permute-start(f32[3,768]{1,0:T(4,128)S(1)} %dynamic-slice_bitcast_fusion.12), channel_id=1, source_target_pairs={{0,2},{1,3},{2,0},{3,1},{4,6},{5,7},{6,4},{7,5},{8,10},{9,11},{10,... | collective-permute-start | bytes 27656 | tf_op jit(solution)/shard_map/ppermute | solution.py:572
  209.7 25.3 %collective-permute-start.25 = (bf16[3,192,768]{2,1,0:T(8,128)(2,1)}, bf16[3,192,768]{2,1,0:T(8,128)(2,1)S(1)}, u32[]{:S(2)}, u32[]{:S(2)}) collective-permute-start(bf16[3,192,768]{2,1,0:T(8,128)(2,1)} %qkv_send.1), channel_id=1, source_target_pairs={{0,2},{1,3},{2,0},{3,1},{4,6},{5,7},{6,4},{7,5},{8,10},{9,11},{10,... | collective-permute-start | bytes 2654216 | tf_op jit(solution)/shard_map/ppermute | solution.py:572
  213.5 30.1 %collective-permute-start.36 = (bf16[5,96,768]{2,1,0:T(8,128)(2,1)S(1)}, bf16[5,96,768]{2,1,0:T(8,128)(2,1)S(1)}, u32[]{:S(2)}, u32[]{:S(2)}) collective-permute-start(bf16[5,96,768]{2,1,0:T(8,128)(2,1)S(1)} %add_convert_fusion.2), channel_id=1, source_target_pairs={{0,8},{4,12},{8,0},{12,4},{16,24},{20,28},{24,16},{28,20},{1,9},{5... | collective-permute-start | bytes 2211848 | tf_op jit(solution)/shard_map/ppermute | solution.py:572
  232.2 46.1 %collective-permute-start.20 = (bf16[128,768]{1,0:T(8,128)(2,1)}, bf16[128,768]{1,0:T(8,128)(2,1)}, u32[]{:S(2)}, u32[]{:S(2)}) collective-permute-start(bf16[128,768]{1,0:T(8,128)(2,1)} %get-tuple-element.100), channel_id=1, source_target_pairs={{0,1},{1,0},{2,3},{3,2},{4,5},{5,4},{6,7},{7,6},{8,9},{9,8},{10,11... | collective-permute-start | bytes 589832 | tf_op jit(solution)/shard_map/ppermute | solution.py:572
  243.8 33.3 %collective-permute-start.37 = (bf16[5,96,768]{2,1,0:T(8,128)(2,1)S(1)}, bf16[5,96,768]{2,1,0:T(8,128)(2,1)S(1)}, u32[]{:S(2)}, u32[]{:S(2)}) collective-permute-start(bf16[5,96,768]{2,1,0:T(8,128)(2,1)S(1)} %add_convert_fusion.1), channel_id=1, source_target_pairs={{0,24},{4,28},{8,16},{12,20},{16,8},{20,12},{24,0},{28,4},{1,25},{... | collective-permute-start | bytes 2211848 | tf_op jit(solution)/shard_map/ppermute | solution.py:572
  244.1 35.2 %collective-permute-start.21 = (bf16[128,768]{1,0:T(8,128)(2,1)S(1)}, bf16[128,768]{1,0:T(8,128)(2,1)}, u32[]{:S(2)}, u32[]{:S(2)}) collective-permute-start(bf16[128,768]{1,0:T(8,128)(2,1)S(1)} %get-tuple-element.99), channel_id=1, source_target_pairs={{0,2},{1,3},{2,0},{3,1},{4,6},{5,7},{6,4},{7,5},{8,10},{9,11},{10,... | collective-permute-start | bytes 589832 | tf_op jit(solution)/shard_map/ppermute | solution.py:572
  245.7 52.0 %collective-permute-start.22 = (bf16[128,768]{1,0:T(8,128)(2,1)S(1)}, bf16[128,768]{1,0:T(8,128)(2,1)}, u32[]{:S(2)}, u32[]{:S(2)}) collective-permute-start(bf16[128,768]{1,0:T(8,128)(2,1)S(1)} %get-tuple-element.98), channel_id=1, source_target_pairs={{0,3},{1,2},{2,1},{3,0},{4,7},{5,6},{6,5},{7,4},{8,11},{9,10},{10,... | collective-permute-start | bytes 589832 | tf_op jit(solution)/shard_map/ppermute | solution.py:572
  254.9 22.9 %collective-permute-start.27 = (bf16[3,96,768]{2,1,0:T(8,128)(2,1)S(1)}, bf16[3,96,768]{2,1,0:T(8,128)(2,1)S(1)}, u32[]{:S(2)}, u32[]{:S(2)}) collective-permute-start(bf16[3,96,768]{2,1,0:T(8,128)(2,1)S(1)} %add_convert_fusion.8), channel_id=1, source_target_pairs={{0,8},{4,12},{8,0},{12,4},{16,24},{20,28},{24,16},{28,20},{1,9},{5... | collective-permute-start | bytes 1327112 | tf_op jit(solution)/shard_map/ppermute | solution.py:572
  277.3 21.3 %collective-permute-start.38 = (bf16[5,96,768]{2,1,0:T(8,128)(2,1)S(1)}, bf16[5,96,768]{2,1,0:T(8,128)(2,1)S(1)}, u32[]{:S(2)}, u32[]{:S(2)}) collective-permute-start(bf16[5,96,768]{2,1,0:T(8,128)(2,1)S(1)} %add_convert_fusion.refs_0_), channel_id=1, source_target_pairs={{0,4},{4,0},{8,12},{12,8},{16,20},{20,16},{24,28},{28,24},{1,5},{5... | collective-permute-start | bytes 2211848 | tf_op jit(solution)/shard_map/ppermute | solution.py:572
  277.9 19.1 %collective-permute-start.28 = (bf16[3,96,768]{2,1,0:T(8,128)(2,1)S(1)}, bf16[3,96,768]{2,1,0:T(8,128)(2,1)S(1)}, u32[]{:S(2)}, u32[]{:S(2)}) collective-permute-start(bf16[3,96,768]{2,1,0:T(8,128)(2,1)S(1)} %add_convert_fusion.7), channel_id=1, source_target_pairs={{0,24},{4,28},{8,16},{12,20},{16,8},{20,12},{24,0},{28,4},{1,25},{... | collective-permute-start | bytes 1327112 | tf_op jit(solution)/shard_map/ppermute | solution.py:572
  (61 other events, 483.4 us)
Sparse Core Ops, SparseCore 0:
  13.6 54.5 all-gather.1

commit v3 on v2

--- a/solution.py
+++ b/solution.py
@@ -13,17 +13,16 @@
 CH = 32
 SLOT = 8
 GROUP = 4
-SUB = 256
-TAIL = (
-    0.0925346463, 0.0902475115, 0.103641987, 0.0105003931,
-    0.230693277, -0.20728912, 0.250823127, -0.0711517759,
-)
+SUB = 384
 SCALE = HEAD ** (-0.5)
 
 norm_eps = 1e-05
 f32 = jnp.float32
 bf16 = jnp.bfloat16
-VMEM_BYTES = 56 * 1024 * 1024
+VMEM_BYTES = 28 * 1024 * 1024
+PIN = 100
+EXTRA = 16
+SMALL = 128
 
 
 def params():
@@ -77,14 +76,6 @@
     col = segments(sc_ref, true_places(sc_ref[0], length, piece, 0))
     row = segments(sc_ref, true_places(sc_ref[0], length, piece, 1))
     return jnp.where(col == row, 0.0, -1e30)
-
-
-def normal_tail(size):
-    t = 1.0 / (1.0 + 0.2316419 * size)
-    total = jnp.full_like(t, TAIL[-1])
-    for term in TAIL[-2::-1]:
-        total = total * t + term
-    return total * t
 
 
 def call(kernel, sc, args, specs, outs, out_specs, grid, scratch, name, micros, deps=()):
@@ -114,6 +105,14 @@
     return jax.ShapeDtypeStruct(dims, t)
 
 
+def kept(t, *dims):
+    return pltpu.HBM(dims, t)
+
+
+def far(*values):
+    return tuple(pltpu.with_memory_space_constraint(v, pltpu.HBM) for v in values)
+
+
 def whole(*dims):
     return pl.BlockSpec(dims, lambda i, s: (0,) * len(dims))
 
@@ -173,16 +172,16 @@
     return call(
         functools.partial(attention_kernel, piece),
         sc,
-        (x, wq, wk, wv, bq, bv, wo, bo, go, so),
+        (x, *far(wq, wk, wv), bq, bv, *far(wo), bo, go, so),
         [
             whole(length, d), cols(d), cols(d), cols(d), cols(1), cols(1), rows(d),
             whole(1, d), whole(1, d), whole(1, d),
         ],
         [
-            shape(bf16, length, d), shape(bf16, length, d), shape(bf16, length, d),
-            shape(bf16, d, length), shape(f32, steps, SLOT, length), shape(bf16, d, length),
-            shape(f32, length, d), shape(f32, length, 1), shape(bf16, length, d),
-            shape(bf16, d, length),
+            kept(bf16, length, d), kept(bf16, length, d), kept(bf16, length, d),
+            kept(bf16, d, length), kept(f32, steps, SLOT, length), kept(bf16, d, length),
+            kept(f32, length, d), kept(f32, length, 1), shape(bf16, length, d),
+            kept(bf16, d, length),
         ],
         [
             cols(length), cols(length), cols(length), rows(length),
@@ -191,7 +190,7 @@
         ],
         (steps,),
         [pltpu.VMEM((length, d), f32), pltpu.VMEM((length, length), f32)],
-        "attention_forward", 18,
+        "attention_forward", 0,
     )
 
 
@@ -211,9 +210,8 @@
         cols = slice(c, c + SUB)
         up = nn(hid_ref[...], wu_ref[:, cols]) + bu_ref[:, cols]
         e = jnp.exp(-0.5 * up * up)
-        tail = normal_tail(jnp.abs(up)) * e
-        cum = jnp.where(up < 0.0, tail, 1.0 - tail)
-        slope_ref[0, :, cols] = cum + up * (e * 0.3989422804014327)
+        cum = 0.5 + 0.5 * lax.erf(up * (2.0 ** -0.5))
+        slope_ref[0, :, cols] = (cum + up * (e * 0.3989422804014327)).astype(bf16)
         act = (up * cum).astype(bf16)
         actt_ref[cols, :] = act.T
         acc[...] += nn(act, wd_ref[cols, :])
@@ -240,7 +238,7 @@
     return call(
         functools.partial(feed_kernel, piece),
         sc,
-        (hid, wu, bu, wd, bd, gt, st),
+        (hid, *far(wu), bu, *far(wd), bd, gt, st),
         [
             whole(length, d),
             pl.BlockSpec((d, d), lambda i, s: (0, i)),
@@ -249,8 +247,8 @@
             whole(1, d), whole(1, d), whole(1, d),
         ],
         [
-            shape(bf16, ff, length), shape(f32, steps, length, d), shape(f32, length, d),
-            shape(f32, length, 1), shape(bf16, length, d), shape(f32, SLOT, d),
+            kept(bf16, ff, length), kept(bf16, steps, length, d), kept(f32, length, d),
+            kept(f32, length, 1), kept(bf16, length, d), shape(f32, SLOT, d),
         ],
         [
             pl.BlockSpec((d, length), lambda i, s: (i, 0)),
@@ -259,7 +257,7 @@
         ],
         (steps,),
         [pltpu.VMEM((length, d), f32)],
-        "feed_forward", 14, deps,
+        "feed_forward", 0, deps,
     )
 
 
@@ -326,7 +324,7 @@
     return jnp.where(off < 0, off + devices, off)
 
 
-def retrieval(sc, code_all, pooled, cot, xhat, inv, gain, piece, places, devices):
+def retrieval(sc, code_all, pooled, cot, xhat, inv, gain, piece, places, devices, deps):
     count, width = code_all.shape
     length, d = cot.shape
     block = 256
@@ -337,7 +335,7 @@
     return call(
         functools.partial(loss_kernel, piece, steps, devices, places),
         sc,
-        (code_all, pooled, cot, xhat, inv, gain),
+        (*far(code_all), pooled, *far(cot, xhat, inv), gain),
         [
             pl.BlockSpec((block, width), lambda i, s: (first(i), 0)),
             whole(*pooled.shape), part(d), part(d), part(1), whole(1, d),
@@ -348,7 +346,7 @@
         ],
         (steps + pieces,),
         [pltpu.VMEM((SLOT, d), f32)],
-        "retrieval", 12,
+        "retrieval", 0, deps,
     )
 
 
@@ -367,7 +365,7 @@
     @pl.when(step < last)
     def _():
         gact = nt(gd_ref[...], wd_ref[...])
-        gup = (gact * slope_ref[0]).astype(bf16)
+        gup = (gact * slope_ref[0].astype(f32)).astype(bf16)
         gug_ref[0] = gup
         bup_ref[0] = jnp.sum(gup.astype(f32), 0, keepdims=True)
         acc[...] += nt(gup, wu_ref[...])
@@ -393,7 +391,7 @@
     return call(
         feed_back_kernel,
         sc,
-        (gd, gr, wd, wu, slope, xhat, inv, go, wo),
+        (gd, gr, *far(wd, wu, slope, xhat, inv), go, *far(wo)),
         [
             whole(length, d), whole(length, d),
             pl.BlockSpec((d, d), lambda i, s: (at(i), 0)),
@@ -418,7 +416,7 @@
 
 def attention_back_kernel(
     piece, sc_ref, q_ref, k_ref, v_ref, gctx_ref, lse_ref, wq_ref, wk_ref, wv_ref, gr_ref,
-    gqkv_ref, gtok_ref, sums_ref,
+    gq_ref, gk_ref, gv_ref, gtok_ref, sums_ref,
     acc, bias, gkt, gvt,
 ):
     step = pl.program_id(0)
@@ -440,12 +438,12 @@
         ga = nt(gctx, v_ref[:, cols])
         dots = jnp.sum(p * ga, -1, keepdims=True)
         g = (p * (ga - dots)).astype(bf16)
-        gqkv_ref[0, :, cols] = (nn(g, k) * SCALE).astype(bf16)
+        gq_ref[:, cols] = (nn(g, k) * SCALE).astype(bf16)
         gkt[cols, :] = (tn(q, g) * SCALE).astype(bf16)
         gvt[cols, :] = tn(gctx, p.astype(bf16)).astype(bf16)
-    gqkv_ref[1] = gkt[...].T
-    gqkv_ref[2] = gvt[...].T
-    gq, gk, gv = gqkv_ref[0], gqkv_ref[1], gqkv_ref[2]
+    gk_ref[...] = gkt[...].T
+    gv_ref[...] = gvt[...].T
+    gq, gk, gv = gq_ref[...], gk_ref[...], gv_ref[...]
     sums_ref[0:1, :] = jnp.sum(gq.astype(f32), 0, keepdims=True)
     sums_ref[1:2, :] = jnp.sum(gv.astype(f32), 0, keepdims=True)
     acc[...] += nt(gq, wq_ref[...]) + nt(gk, wk_ref[...]) + nt(gv, wv_ref[...])
@@ -463,14 +461,14 @@
     return call(
         functools.partial(attention_back_kernel, piece),
         sc,
-        (q, k, v, gctx, lse, wq, wk, wv, gr),
+        (*far(q, k, v), gctx, *far(lse, wq, wk, wv), gr),
         [
             cols(length), cols(length), cols(length), cols(length),
             pl.BlockSpec((1, SLOT, length), lambda i, s: (i, 0, 0)),
             cols(d), cols(d), cols(d), whole(length, d),
         ],
-        [shape(bf16, 3, length, d), shape(bf16, length, d), shape(f32, SLOT, d)],
-        [pl.BlockSpec((3, length, wide), lambda i, s: (0, 0, i)), whole(length, d), cols(SLOT)],
+        [shape(bf16, length, d)] * 4 + [shape(f32, SLOT, d)],
+        [cols(length), cols(length), cols(length), whole(length, d), cols(SLOT)],
         (steps,),
         [
             pltpu.VMEM((length, d), f32), pltpu.VMEM((length, length), f32),
@@ -492,20 +490,124 @@
     out_ref[0] = weight_total(two, lo_refs, lp_ref, go_ref, gp_ref).astype(bf16)
 
 
+def deal(sc_ref, total, step, keep_ref, send_ref):
+    rows = total.shape[0] // 4
+    spot = pl.ds(step * rows if isinstance(step, int) else pl.multiple_of(step * rows, rows), rows)
+    for h in range(2):
+        for z in range(2):
+            part = total[(2 * h + z) * rows : (2 * h + z + 1) * rows].astype(bf16)
+
+            @pl.when(sc_ref[2] == h)
+            def _():
+                keep_ref[sc_ref[3] ^ z, spot, :] = part
+
+            @pl.when(sc_ref[2] != h)
+            def _():
+                send_ref[sc_ref[3] ^ z, spot, :] = part
+
+
 def weight_keep_kernel(lefts, two, sc_ref, *refs):
     lo_refs, (lp_ref, go_ref, gp_ref, recv_ref, keep_ref, send_ref) = refs[:lefts], refs[lefts:]
     total = weight_total(two, lo_refs, lp_ref, go_ref, gp_ref) + recv_ref[0].astype(f32)
-    half = total.shape[0] // 2
-    for h in range(2):
-        rows = total[h * half : (h + 1) * half]
-
-        @pl.when(sc_ref[2] == h)
-        def _():
-            keep_ref[0] = rows
-
-        @pl.when(sc_ref[2] != h)
-        def _():
-            send_ref[0] = rows.astype(bf16)
+    deal(sc_ref, total, pl.program_id(0), keep_ref, send_ref)
+
+
+def pack_kernel(sc_ref, qkv_ref, one_ref, two_ref, bup_ref, own_ref, far_ref):
+    rows = jnp.concatenate([qkv_ref[0:2], one_ref[0:3], two_ref[0:3]], 0)
+    quarter = rows.shape[1] // 4
+    own_ref[...] = jnp.zeros_like(own_ref)
+    far_ref[...] = jnp.zeros_like(far_ref)
+    for x in range(2):
+        for c in range(2):
+            q = 2 * x + c
+            left = rows[:, q * quarter : (q + 1) * quarter]
+
+            def put(ref):
+                ref[x, 0:8, :quarter] = left
+                for j in range(4):
+                    ref[x, 8 + j : 9 + j, :quarter] = bup_ref[q, :, j * quarter : (j + 1) * quarter]
+
+            @pl.when(sc_ref[1] == c)
+            def _():
+                put(own_ref)
+
+            @pl.when(sc_ref[1] != c)
+            def _():
+                put(far_ref)
+
+
+def pack(sc, qkv, one, two, bup):
+    out = shape(f32, 2, EXTRA, 2 * SMALL)
+    return call(
+        pack_kernel, sc, (qkv, one, two, bup), [whole(*t.shape) for t in (qkv, one, two, bup)],
+        [out, out], [whole(*out.shape)] * 2, (1,), [], "pack", 0,
+    )
+
+
+def qkv_totals(lo_ref, lp_ref, own, par):
+    return [nn(lo_ref[0], o[...]) + nn(lp_ref[0, 0], p[...]) for o, p in zip(own, par)]
+
+
+def qkv_send_kernel(sc_ref, lo_ref, lp_ref, own_ref, par_ref, *refs):
+    out_ref = refs[6]
+    rows = lo_ref.shape[1]
+    for n, total in enumerate(qkv_totals(lo_ref, lp_ref, refs[:3], refs[3:6])):
+        out_ref[n * rows : (n + 1) * rows, :] = total.astype(bf16)
+    vec = own_ref[1 - sc_ref[0]] + par_ref[1 - sc_ref[0]]
+    out_ref[3 * rows :, :] = jnp.zeros((EXTRA, out_ref.shape[1]), bf16)
+    out_ref[3 * rows :, : vec.shape[1]] = vec.astype(bf16)
+
+
+def qkv_keep_kernel(sc_ref, lo_ref, lp_ref, own_ref, par_ref, *refs):
+    recv_ref, keep_ref, send_ref = refs[6:]
+    rows = lo_ref.shape[1]
+    for n, total in enumerate(qkv_totals(lo_ref, lp_ref, refs[:3], refs[3:6])):
+        total += recv_ref[n * rows : (n + 1) * rows, :].astype(f32)
+        deal(sc_ref, total, n, keep_ref, send_ref)
+    base = keep_ref.shape[1] - EXTRA
+    vec = own_ref[sc_ref[0]] + par_ref[sc_ref[0]]
+    wide = vec.shape[1]
+    vec += recv_ref[3 * rows :, :wide].astype(f32)
+    blank = jnp.zeros((EXTRA, keep_ref.shape[2]), bf16)
+    for ref in (keep_ref, send_ref):
+        for z in range(2):
+            ref[z, base:, :] = blank
+            ref[z, base:, :wide] = vec.astype(bf16)
+
+
+def qkv_specs(xt, halves, own, other):
+    x = (lambda s: 1 - s[0]) if other else (lambda s: s[0])
+    return [
+        pl.BlockSpec((1,) + xt.shape[1:], lambda i, s: (2 * x(s) + s[1], 0, 0)),
+        pl.BlockSpec((1, 1) + halves.shape[2:], lambda i, s: (x(s), 2, 0, 0)),
+    ] + [whole(2, EXTRA, 2 * SMALL)] * 2 + [whole(*own.shape)] * 6
+
+
+def qkv_send(sc, operands, deps):
+    xt, halves, _, _, own = operands[:5]
+    rows, wide = xt.shape[1], own.shape[1]
+    out = shape(bf16, 3 * rows + EXTRA, wide)
+    return call(
+        qkv_send_kernel, sc, far(xt, halves) + operands[2:], qkv_specs(xt, halves, own, True), out, whole(*out.shape),
+        (1,), [], "qkv_send", 0, deps,
+    )
+
+
+def qkv_keep(sc, operands, recv, deps):
+    xt, halves, _, _, own = operands[:5]
+    rows, wide = xt.shape[1], own.shape[1]
+    out = shape(bf16, 2, 3 * rows // 4 + EXTRA, wide)
+    return call(
+        qkv_keep_kernel, sc, far(xt, halves) + operands[2:] + (recv,),
+        qkv_specs(xt, halves, own, False) + [whole(*recv.shape)],
+        [out, out], [whole(*out.shape)] * 2, (1,), [], "qkv_keep", 0, deps,
+    )
+
+
+def order_kernel(sc_ref, *refs):
+    out_ref = refs[-1]
+    for mask, piece in enumerate(refs[:-1]):
+        out_ref[sc_ref[0] ^ mask] = piece[...]
 
 
 def weight_specs(lefts, halves, grads, grads_p, other, steps, turn):
@@ -521,7 +623,7 @@
     specs.append(pl.BlockSpec((1, 1) + halves.shape[2:], lambda i, s: (x(s), turn(i), 0, 0)))
     one = grads.shape[0] == 1
     block = pl.BlockSpec((1,) + grads.shape[1:], lambda i, s: (0 if one else i, 0, 0))
-    return (*lefts, halves, grads, grads_p), specs + [block, block]
+    return (*far(*lefts), *far(halves), grads, grads_p), specs + [block, block]
 
 
 def weight_send(sc, operands, steps, two, turn, name, deps=(), micros=0):
@@ -538,32 +640,37 @@
 def weight_keep(sc, operands, recv, steps, two, turn, name, deps=(), micros=0):
     args, specs = weight_specs(*operands, False, steps, turn)
     rows, wide = operands[1].shape[2], operands[2].shape[2]
-    half = pl.BlockSpec((1, rows // 2, wide), lambda i, s: (i, 0, 0))
+    out = shape(bf16, 2, steps * rows // 4, wide)
     return call(
         functools.partial(weight_keep_kernel, len(operands[0]), two),
         sc, args + (recv,), specs + [pl.BlockSpec((1, rows, wide), lambda i, s: (i, 0, 0))],
-        [shape(f32, steps, rows // 2, wide), shape(bf16, steps, rows // 2, wide)],
-        [half, half], (steps,), [],
+        [out, out], [whole(*out.shape)] * 2, (steps,), [],
         name, micros, deps,
     )
 
 
-def place_kernel(spots, sc_ref, own_ref, far_ref, *out_refs):
-    half = own_ref.shape[1]
-    wide = own_ref.shape[2]
-    for n, (out, down, left) in enumerate(spots):
-        for part, side in ((own_ref, 0), (far_ref, 1)):
-            h = sc_ref[2] ^ side
-            top = pl.multiple_of(down * 2 * half + h * half, half)
-            out_refs[out][pl.ds(top, half), left * wide : (left + 1) * wide] = part[n].astype(f32)
-
-
-def place(sc, own, far, spots, dims, name):
-    return call(
-        functools.partial(place_kernel, spots),
-        sc, (own, far), [whole(*own.shape), whole(*far.shape)],
+def place_kernel(spots, extra, sc_ref, *refs):
+    parts, out_refs = refs[:4], refs[4:]
+    rows = (parts[0].shape[0] - extra) // len(spots)
+    wide = parts[0].shape[1]
+    for side, part in enumerate(parts):
+        slot = 2 * (sc_ref[2] ^ (side // 2)) + (sc_ref[3] ^ (side % 2))
+        for n, (out, down, left) in enumerate(spots):
+            top = pl.multiple_of((4 * down + slot) * rows, rows)
+            out_refs[out][pl.ds(top, rows), left * wide : (left + 1) * wide] = part[
+                n * rows : (n + 1) * rows, :
+            ].astype(f32)
+    if extra:
+        small = out_refs[-1]
+        small[...] = parts[0][len(spots) * rows :, : small.shape[1]].astype(f32)
+
+
+def place(sc, parts, spots, dims, extra, name):
+    return call(
+        functools.partial(place_kernel, spots, extra),
+        sc, parts, [whole(*parts[0].shape)] * 4,
         [shape(f32, *dim) for dim in dims], [whole(*dim) for dim in dims], (1,), [],
-        name, 3,
+        name, 0,
     )
 
 
@@ -586,11 +693,33 @@
     return [2, 6] + [1 << b for b in range(3, count.bit_length() - 1)]
 
 
-def over_rows(keep, send, masks):
-    value = (keep + flip(send, "rows", 1).astype(f32)).astype(bf16)
-    for mask in masks:
-        value = (value.astype(f32) + flip(value, "rows", mask).astype(f32)).astype(bf16)
-    return value, flip(value, "rows", 1)
+def join_kernel(sc_ref, left_ref, right_ref, out_ref):
+    out_ref[...] = (left_ref[...].astype(f32) + right_ref[...].astype(f32)).astype(bf16)
+
+
+def join(sc, left, right, deps):
+    block = whole(*left.shape)
+    return call(
+        join_kernel, sc, (left, right), [block, block], shape(bf16, *left.shape), block, (1,), [],
+        "join", 0, deps,
+    )
+
+
+def over_rows(sc, keep, send, masks, deps=(), later=()):
+    near, *rest = masks
+    value = keep
+    if send is not None:
+        got = flip(send, "rows", 1)
+        value = join(sc, keep, got, deps) if deps else add(keep, got)
+    got = flip(value[1], "rows", near)
+    value = join(sc, value[0], got, later) if later else add(value[0], got)
+    for mask in rest:
+        value = add(value, flip(value, "rows", mask))
+    return tuple([value] + [flip(value, "rows", mask) for mask in (near, 1, near ^ 1)])
+
+
+def add(left, right):
+    return (left.astype(f32) + right.astype(f32)).astype(bf16)
 
 
 def spread(rows):
@@ -606,14 +735,13 @@
     return jnp.concatenate(pieces, 0)
 
 
-def gather_back(row, count):
-    own = lax.axis_index("seq")
+def gather_back(sc, row, count, name, deps=()):
     row = row.reshape(count, -1, row.shape[-1])
-    out = jnp.zeros_like(row)
-    for mask in range(count):
-        piece = flip(row[mask], "seq", mask) if mask else row[0]
-        out = lax.dynamic_update_index_in_dim(out, piece, own ^ mask, 0)
-    return out
+    pieces = tuple(flip(row[mask], "seq", mask) if mask else row[0] for mask in range(count))
+    return call(
+        order_kernel, sc, pieces, [whole(*row.shape[1:])] * count, shape(row.dtype, *row.shape),
+        whole(*row.shape), (1,), [], name, 0, deps,
+    )
 
 
 def per_device(
@@ -650,7 +778,7 @@
     own_lin = own_r * seq_count + own_s
     devices = row_count * seq_count
     masks = row_flips()
-    wsc = jnp.stack([xside, core, own_r % 2, own_r % 2]).astype(jnp.int32)
+    wsc = jnp.stack([xside, core, own_r % 2, (own_r // 2 ^ own_r // 4) % 2]).astype(jnp.int32)
     starts = lax.dynamic_index_in_dim(passage_starts, own_s, 0, keepdims=False)
     sc = jnp.concatenate([own_s[None].astype(jnp.int32), starts, own_lin[None].astype(jnp.int32)])
     row = lambda v: v.reshape(1, -1)
@@ -697,68 +825,63 @@
     quarters = lambda t: t.reshape(4, -1, t.shape[-1])
 
     losses_all, gd, gr_two, sums_two = retrieval(
-        sc, code_all, pooled, cot, xhat_two, inv_two, row(gain_two), piece, places, devices
+        sc, code_all, pooled, cot, xhat_two, inv_two, row(gain_two), piece, places, devices,
+        (halves,),
     )
     query_losses = lax.dynamic_slice_in_dim(
         losses_all[:, 0], own_lin * queries.shape[0], queries.shape[0]
     )
 
-    down_ops = ((actt.reshape(4, 4, quarter, -1),), halves, gd[None], swap(gd)[None])
+    gd_p = swap(gd)
+    gug, bup, gr_one, gctx, sums_one = feed_back(
+        sc, gd, gr_two, w_down, w_up, slope, xhat_one, inv_one, row(gain_one), w_out, (gd_p,)
+    )
+    down_ops = ((actt.reshape(4, 4, quarter, -1),), halves, gd[None], gd_p[None])
     down_turn = lambda i: 3 + i
-    down_sent = weight_send(wsc, down_ops, 4, 0, down_turn, "down_send")
+    down_sent = weight_send(wsc, down_ops, 4, 0, down_turn, "down_send", (gug,))
     down_got = flip(down_sent, "seq", 2)
 
-    gug, bup, gr_one, gctx, sums_one = feed_back(
-        sc, gd, gr_two, w_down, w_up, slope, xhat_one, inv_one, row(gain_one), w_out, (down_sent,)
-    )
-    down_parts = weight_keep(wsc, down_ops, down_got, 4, 0, down_turn, "down_keep", (gug,), 100)
     up_ops = ((quarters(hidt), quarters(ctxt)), halves, gug, swap(gug))
     up_turn = lambda i: i // 4
-    up_sent = weight_send(wsc, up_ops, 5, 4, up_turn, "up_send", (down_parts[0],))
+    up_sent = weight_send(wsc, up_ops, 5, 4, up_turn, "up_send", (down_sent,))
     up_got = flip(up_sent, "seq", 2)
 
-    gqkv, gtok, sums_qkv = attention_back(
+    gq, gk, gv, gtok, sums_qkv = attention_back(
         sc, q, k, v, gctx, lse, w_query, w_key, w_value, gr_one, piece, (up_sent,)
     )
-    up_parts = weight_keep(wsc, up_ops, up_got, 5, 4, up_turn, "up_keep", (gqkv,), 100)
-    qkv_ops = ((quarters(xt),), halves, gqkv, swap(gqkv))
-    qkv_turn = lambda i: 2
-    qkv_sent = weight_send(wsc, qkv_ops, 3, 0, qkv_turn, "qkv_send", (up_parts[0],))
+    vec, vec_far = pack(wsc, sums_qkv, sums_one, sums_two, bup)
+    qkv_ops = (
+        quarters(xt), halves, vec, swap(vec_far), gq, gk, gv, swap(gq), swap(gk), swap(gv)
+    )
+    up_parts = weight_keep(wsc, up_ops, up_got, 5, 4, up_turn, "up_keep", (vec,))
+    qkv_sent = qkv_send(wsc, qkv_ops, (up_parts[0],))
     qkv_got = flip(qkv_sent, "seq", 2)
-
-    down_sum = over_rows(*down_parts, masks)
-    up_sum = over_rows(*up_parts, masks)
-    qkv_parts = weight_keep(wsc, qkv_ops, qkv_got, 3, 0, qkv_turn, "qkv_keep", (up_parts[0],))
-    qkv_sum = over_rows(*qkv_parts, masks)
-
-    vec = jnp.concatenate([sums_qkv[:2], sums_one[:3], sums_two[:3]], 0)
-    vec = vec.reshape(8, 4, quarter).transpose(1, 0, 2).reshape(4, 2, d)
-    vec = jnp.concatenate([vec, bup.reshape(4, ff // 4 // d, d)], 1)
-    vec = vec.reshape(2, 2, 3, d)
-    vec = lax.dynamic_index_in_dim(vec, core, 1, keepdims=False) + swap(
-        lax.dynamic_index_in_dim(vec, 1 - core, 1, keepdims=False)
-    )
-    vec = lax.dynamic_index_in_dim(vec, xside, 0, keepdims=False) + flip(
-        lax.dynamic_index_in_dim(vec, 1 - xside, 0, keepdims=False), "seq", 2
-    )
-    for mask in [1] + masks:
-        vec = vec + flip(vec, "rows", mask)
-
-    mixed = gather_back(mixed_row, seq_count)
-    grad_tokens = gather_back(gtok, seq_count)
+    up_got_rows = flip(up_parts[1], "rows", 1)
+    up_first = join(wsc, up_parts[0], up_got_rows, (qkv_sent,))
+    down_parts = weight_keep(
+        wsc, down_ops, down_got, 4, 0, down_turn, "down_keep", (up_first,), PIN
+    )
+    qkv_parts = qkv_keep(wsc, qkv_ops, qkv_got, (down_parts[0],))
+    up_sum = over_rows(wsc, up_first, None, masks, later=(qkv_parts[0],))
+    down_sum = over_rows(wsc, *down_parts, masks, (qkv_parts[0],))
+    qkv_sum = over_rows(wsc, *qkv_parts, masks)
+
+    mixed = gather_back(sc, mixed_row, seq_count, "mixed_order", (qkv_sent,))
+    grad_tokens = gather_back(sc, gtok, seq_count, "tokens_order", (qkv_parts[0],))
 
     (grad_down,) = place(
-        wsc, *down_sum, [(0, n, 0) for n in range(4)], [(4 * quarter, d)], "down_place"
+        wsc, down_sum, [(0, n, 0) for n in range(4)], [(4 * quarter, d)], 0, "down_place"
     )
     grad_up, grad_o = place(
-        wsc, *up_sum, [(0, 0, n) for n in range(4)] + [(1, 0, 0)],
-        [(quarter, ff), (quarter, d)], "up_place",
-    )
-    grad_q, grad_k, grad_v = place(
-        wsc, *qkv_sum, [(n, 0, 0) for n in range(3)], [(quarter, d)] * 3, "qkv_place"
-    )
-
-    eight = vec[:2].reshape(8, quarter)
+        wsc, up_sum, [(0, 0, n) for n in range(4)] + [(1, 0, 0)],
+        [(quarter, ff), (quarter, d)], 0, "up_place",
+    )
+    grad_q, grad_k, grad_v, small = place(
+        wsc, qkv_sum, [(n, 0, 0) for n in range(3)], [(quarter, d)] * 3 + [(EXTRA, 2 * SMALL)],
+        EXTRA, "qkv_place",
+    )
+
+    eight = small[:, :quarter]
     return (
         mixed,
         query_losses,
@@ -773,7 +896,7 @@
         eight[3],
         eight[4],
         grad_up,
-        vec[2],
+        eight[8:12].reshape(-1),
         grad_down,
         eight[5],
         eight[6],

time: 322 us -> 303 us (0.941)
  the two profiles are of different devices: /device:TPU:16 before, /device:TPU:0 now
where the time goes in v3:
time: 303 us; the launch traced here: 302 us
  Pallas kernels  116 us (38%)
  waiting for transfers between devices  103 us (34%)
  starting transfers between devices  47.4 us (16%)
  local copies, waits for them, and re-layouts  18 us (6%)
  between operations  14.9 us (5%)
  other arithmetic  3.38 us (1%)
    pallas_call x20, Pallas kernels, call(): pl.pallas_call(body, grid_spec=pltpu.PrefetchScalarGridSpec(num_scalar_pr...  116 us
    ppermute x46, waiting for transfers between devices, flip(): return lax.ppermute(value, axis, [(i, i ^ mask) for i in range(count)])  102 us
    ppermute x46, starting transfers between devices, flip(): return lax.ppermute(value, axis, [(i, i ^ mask) for i in range(count)])  43.8 us
    unnamed x88, local copies, waits for them, and re-layouts  11.5 us
  transfers between devices with their start and end apart: 48, of which 22 were waited for; matrix products, arithmetic and copies ran while one was open for 3% of the time, Pallas kernels for 26%

profile of v3, /device:TPU:0, one launch (start us, length us, event | category | flops | bytes accessed | tf_op | source)
XLA Modules:
  0.0 302.5 jit_solution(4070692414243862154)
XLA Ops:
  20.0 4.6 %collective-permute-done.1 = bf16[128,768]{1,0:T(8,128)(2,1)S(1)} collective-permute-done((bf16[128,768]{1,0:T(8,128)(2,1)S(1)}, bf16[128,768]{1,0:T(8,128)(2,1)S(1)}, u32[]{:S(2)}, u32[]{:S(2)}) %collective-permute-start.1) | collective-permute-done | bytes 196640 | tf_op jit(solution)/shard_map/ppermute | solution.py:679
  24.7 17.0 %attention_forward.1 = (bf16[512,768]{1,0:T(8,128)(2,1)}, bf16[512,768]{1,0:T(8,128)(2,1)}, bf16[512,768]{1,0:T(8,128)(2,1)}, bf16[768,512]{1,0:T(8,128)(2,1)}, ...) custom-call(s32[8]{0:T(128)S(1)} %pad_add_fusion.sc_ref, ...), custom_call_target="tpu_custom_call" | custom-call | tf_op jit(solution)/shard_map/attention_forward/pallas_call | solution.py:88
  43.1 14.3 %feed_forward.1 = (bf16[3072,512]{1,0:T(8,128)(2,1)}, bf16[4,512,768]{2,1,0:T(8,128)(2,1)}, f32[512,768]{1,0:T(8,128)}, f32[512,1]{1,0:T(8,128)}, bf16[512,768]{1,0:T(8,128)(2,1)}, /*index=5*/f32[8,768]{1,0:T(8,128)S(1)}) custom-call(s32[8]{0:T(128)S(1)} %pad_add_fusion.sc_ref, bf16[512,768]{1,0:T(8,128)(2,1)S(1)} %get-tuple-element.62.refs_0_, ...), custom_call_target="tpu_custom_call" | custom-call | tf_op jit(solution)/shard_map/feed_forward/pallas_call | solution.py:88
  59.4 3.5 %collective-permute-start.12 = (bf16[8,768]{1,0:T(8,128)(2,1)S(1)}, bf16[8,768]{1,0:T(8,128)(2,1)S(1)}, u32[]{:S(2)}, u32[]{:S(2)}) collective-permute-start(bf16[8,768]{1,0:T(8,128)(2,1)S(1)} %get-tuple-element.107), channel_id=1, source_target_pairs={{0,6},{1,7},{2,4},{3,5},{4,2},{5,3},{6,0},{7,1},{8,14},{9,15},{10,... | collective-permute-start | bytes 36872 | tf_op jit(solution)/shard_map/ppermute | solution.py:687
  71.4 3.8 %collective-permute-done.13 = bf16[32,768]{1,0:T(8,128)(2,1)S(1)} collective-permute-done((bf16[32,768]{1,0:T(8,128)(2,1)S(1)}, bf16[32,768]{1,0:T(8,128)(2,1)S(1)}, u32[]{:S(2)}, u32[]{:S(2)}) %collective-permute-start.13) | collective-permute-done | bytes 49184 | tf_op jit(solution)/shard_map/ppermute | solution.py:679
  79.3 13.3 %retrieval.1 = (f32[1024,1]{1,0:T(8,128)S(1)}, bf16[512,768]{1,0:T(8,128)(2,1)S(1)}, f32[512,768]{1,0:T(8,128)S(1)}, f32[8,768]{1,0:T(8,128)S(1)}) custom-call(s32[8]{0:T(128)S(1)} %pad_add_fusion.sc_ref, bf16[1024,832]{1,0:T(8,128)(2,1)} %all-gather.2.cloned.1.call-done.refs_0_, bf16[256,768]{1,0:T(8,128)(2,1)S(1)} %copy-done.7, ...), custom_call_target="tpu_custom_call" | custom-call | tf_op jit(solution)/shard_map/retrieval/pallas_call | solution.py:88
  95.0 13.5 %feed_back.1 = (bf16[5,512,768]{2,1,0:T(8,128)(2,1)}, f32[4,1,768]{2,1,0:T(1,128)S(1)}, f32[512,768]{1,0:T(8,128)S(1)}, bf16[512,768]{1,0:T(8,128)(2,1)S(1)}, f32[8,768]{1,0:T(8,128)S(1)}) custom-call(s32[8]{0:T(128)S(1)} %pad_add_fusion.sc_ref, bf16[512,768]{1,0:T(8,128)(2,1)S(1)} %get-tuple-element.74.refs_0_, f32[512,768]{1,0:T(8,128)S(1)} %get-tuple-element.75.refs_1_, ...), custom_call_target="tpu_custom_call" | custom-call | tf_op jit(solution)/shard_map/feed_back/pallas_call | solution.py:88
  109.8 4.1 %down_send.1.refs_5_ = bf16[4,192,768]{2,1,0:T(8,128)(2,1)S(1)} custom-call(s32[4]{0:T(128)S(1)} %pad_add_fusion.1.sc_ref, bf16[4,4,192,512]{3,2,1,0:T(8,128)(2,1)} %bitcast.83, bf16[2,7,192,512]{3,2,1,0:T(8,128)(2,1)} %copy-done.2, bf16[1,512,768]{2,1,0:T(8,128)(2,1)S(1)} %bitcast.77, bf16[1,512,768]{2,1,0:T(8,128)(2,1)S(1)} %bitcast.79, ...), custom_call_target="tpu_custom_call" | custom-call | tf_op jit(solution)/shard_map/down_send/pallas_call | solution.py:88
  116.8 6.7 %up_send.1.refs_9_ = bf16[5,192,768]{2,1,0:T(8,128)(2,1)S(1)} custom-call(s32[4]{0:T(128)S(1)} %pad_add_fusion.1.sc_ref, bf16[4,192,512]{2,1,0:T(8,128)(2,1)} %bitcast.91, bf16[4,192,512]{2,1,0:T(8,128)(2,1)} %bitcast.88, bf16[2,7,192,512]{3,2,1,0:T(8,128)(2,1)} %copy-done.2, bf16[5,512,768]{2,1,0:T(8,128)(2,1)} %get-tuple-element.82.refs_4_.refs_3_, ...), custom_call_target="tpu_custom_call" | custom-call | tf_op jit(solution)/shard_map/up_send/pallas_call | solution.py:88
  125.5 15.8 %attention_back.1 = (bf16[512,768]{1,0:T(8,128)(2,1)S(1)}, bf16[512,768]{1,0:T(8,128)(2,1)S(1)}, bf16[512,768]{1,0:T(8,128)(2,1)S(1)}, bf16[512,768]{1,0:T(8,128)(2,1)S(1)}, f32[8,768]{1,0:T(8,128)S(1)}) custom-call(s32[8]{0:T(128)S(1)} %pad_add_fusion.sc_ref, bf16[512,768]{1,0:T(8,128)(2,1)} %get-tuple-element.68.refs_0_, ...), custom_call_target="tpu_custom_call" | custom-call | tf_op jit(solution)/shard_map/attention_back/pallas_call | solution.py:88
  142.8 15.8 %collective-permute-done.23.refs_5_ = bf16[5,192,768]{2,1,0:T(8,128)(2,1)S(1)} collective-permute-done((bf16[5,192,768]{2,1,0:T(8,128)(2,1)S(1)}, bf16[5,192,768]{2,1,0:T(8,128)(2,1)S(1)}, u32[]{:S(2)}, u32[]{:S(2)}) %collective-permute-start.23) | collective-permute-done | bytes 1474592 | tf_op jit(solution)/shard_map/ppermute | solution.py:679
  158.6 6.9 %up_keep.1 = (bf16[2,240,768]{2,1,0:T(8,128)(2,1)S(1)}, bf16[2,240,768]{2,1,0:T(8,128)(2,1)S(1)}) custom-call(s32[4]{0:T(128)S(1)} %pad_add_fusion.1.sc_ref, bf16[4,192,512]{2,1,0:T(8,128)(2,1)} %bitcast.92, bf16[4,192,512]{2,1,0:T(8,128)(2,1)} %bitcast.89, bf16[2,7,192,512]{3,2,1,0:T(8,128)(2,1)} %copy-done.2, ...), custom_call_target="tpu_custom_call" | custom-call | tf_op jit(solution)/shard_map/up_keep/pallas_call | solution.py:88
  170.0 14.5 %collective-permute-done.29.refs_1_ = bf16[2,240,768]{2,1,0:T(8,128)(2,1)S(1)} collective-permute-done((bf16[2,240,768]{2,1,0:T(8,128)(2,1)S(1)}, bf16[2,240,768]{2,1,0:T(8,128)(2,1)S(1)}, u32[]{:S(2)}, u32[]{:S(2)}) %collective-permute-start.29) | collective-permute-done | bytes 737312 | tf_op jit(solution)/shard_map/ppermute | solution.py:679
  185.3 4.4 %down_keep.1 = (bf16[2,192,768]{2,1,0:T(8,128)(2,1)S(1)}, bf16[2,192,768]{2,1,0:T(8,128)(2,1)S(1)}) custom-call(s32[4]{0:T(128)S(1)} %pad_add_fusion.1.sc_ref, bf16[4,4,192,512]{3,2,1,0:T(8,128)(2,1)} %bitcast.84, bf16[2,7,192,512]{3,2,1,0:T(8,128)(2,1)} %copy-done.2, bf16[1,512,768]{2,1,0:T(8,128)(2,1)S(1)} %bitcast.78, bf16[1,512,768]{2,1,0:T(8,128)(2,1)S(1)} %bitcast.80, ...), custom_call_target="tpu_custom_call" | custom-call | flops 115000000512 | tf_op jit(solution)/shard_map/down_keep/pallas_call | solution.py:88
  191.4 11.2 %collective-permute-done.27.refs_10_ = bf16[592,768]{1,0:T(8,128)(2,1)S(1)} collective-permute-done((bf16[592,768]{1,0:T(8,128)(2,1)S(1)}, bf16[592,768]{1,0:T(8,128)(2,1)S(1)}, u32[]{:S(2)}, u32[]{:S(2)}) %collective-permute-start.27) | collective-permute-done | bytes 909344 | tf_op jit(solution)/shard_map/ppermute | solution.py:679
  202.6 3.3 %qkv_keep.1 = (bf16[2,160,768]{2,1,0:T(8,128)(2,1)S(1)}, bf16[2,160,768]{2,1,0:T(8,128)(2,1)S(1)}) custom-call(s32[4]{0:T(128)S(1)} %pad_add_fusion.1.sc_ref, bf16[4,192,512]{2,1,0:T(8,128)(2,1)} %bitcast.86, bf16[2,7,192,512]{3,2,1,0:T(8,128)(2,1)} %copy-done.2, f32[2,16,256]{2,1,0:T(8,128)S(1)} %get-tuple-element.87.refs_6_.refs_2_, ...), custom_call_target="tpu_custom_call" | custom-call | tf_op jit(solution)/shard_map/qkv_keep/pallas_call | solution.py:88
  213.0 5.4 %collective-permute-done.30 = bf16[2,160,768]{2,1,0:T(8,128)(2,1)S(1)} collective-permute-done((bf16[2,160,768]{2,1,0:T(8,128)(2,1)S(1)}, bf16[2,160,768]{2,1,0:T(8,128)(2,1)S(1)}, u32[]{:S(2)}, u32[]{:S(2)}) %collective-permute-start.30) | collective-permute-done | bytes 491552 | tf_op jit(solution)/shard_map/ppermute | solution.py:679
  218.5 5.0 %collective-permute-done.37 = bf16[240,768]{1,0:T(8,128)(2,1)S(1)} collective-permute-done((bf16[240,768]{1,0:T(8,128)(2,1)S(1)}, bf16[240,768]{1,0:T(8,128)(2,1)S(1)}, u32[]{:S(2)}, u32[]{:S(2)}) %collective-permute-start.37) | collective-permute-done | bytes 368672 | tf_op jit(solution)/shard_map/ppermute | solution.py:679
  223.6 5.1 %collective-permute-start.31 = (bf16[160,768]{1,0:T(8,128)(2,1)S(1)}, bf16[160,768]{1,0:T(8,128)(2,1)S(1)}, u32[]{:S(2)}, u32[]{:S(2)}) collective-permute-start(bf16[160,768]{1,0:T(8,128)(2,1)S(1)} %slice_bitcast_fusion.4), channel_id=1, source_target_pairs={{0,8},{4,12},{8,0},{12,4},{16,24},{20,28},{24,16},{28,20},{1,9},{5... | collective-permute-start | bytes 737288 | tf_op jit(solution)/shard_map/ppermute | solution.py:679
  228.8 5.5 %collective-permute-done.31 = bf16[160,768]{1,0:T(8,128)(2,1)S(1)} collective-permute-done((bf16[160,768]{1,0:T(8,128)(2,1)S(1)}, bf16[160,768]{1,0:T(8,128)(2,1)S(1)}, u32[]{:S(2)}, u32[]{:S(2)}) %collective-permute-start.31) | collective-permute-done | bytes 245792 | tf_op jit(solution)/shard_map/ppermute | solution.py:679
  246.1 9.1 %collective-permute-done.32 = bf16[160,768]{1,0:T(8,128)(2,1)S(1)} collective-permute-done((bf16[160,768]{1,0:T(8,128)(2,1)S(1)}, bf16[160,768]{1,0:T(8,128)(2,1)S(1)}, u32[]{:S(2)}, u32[]{:S(2)}) %collective-permute-start.32) | collective-permute-done | bytes 245792 | tf_op jit(solution)/shard_map/ppermute | solution.py:679
  265.5 3.6 %collective-permute-done.38.refs_1_ = bf16[240,768]{1,0:T(8,128)(2,1)S(1)} collective-permute-done((bf16[240,768]{1,0:T(8,128)(2,1)S(1)}, bf16[240,768]{1,0:T(8,128)(2,1)S(1)}, u32[]{:S(2)}, u32[]{:S(2)}) %collective-permute-start.38) | collective-permute-done | bytes 368672 | tf_op jit(solution)/shard_map/ppermute | solution.py:679
  271.4 4.0 %collective-permute-done.35.refs_3_ = bf16[160,768]{1,0:T(8,128)(2,1)S(1)} collective-permute-done((bf16[160,768]{1,0:T(8,128)(2,1)S(1)}, bf16[160,768]{1,0:T(8,128)(2,1)S(1)}, u32[]{:S(2)}, u32[]{:S(2)}) %collective-permute-start.35) | collective-permute-done | bytes 245792 | tf_op jit(solution)/shard_map/ppermute | solution.py:679
  292.4 3.2 %down_place.1 = f32[768,768]{1,0:T(8,128)} custom-call(s32[4]{0:T(128)S(1)} %pad_add_fusion.1.sc_ref, bf16[192,768]{1,0:T(8,128)(2,1)S(1)} %add_convert_fusion.2.refs_0_, bf16[192,768]{1,0:T(8,128)(2,1)} %collective-permute-done.44.refs_1_, bf16[192,768]{1,0:T(8,128)(2,1)} %collective-permute-done.45.refs_2_, bf16[192,768]{1,0:T(8,128)(2,1)} %collective-permute-done.46.refs_3_), custom_call_target="tpu_custom_call" | custom-call | tf_op jit(solution)/shard_map/down_place/pallas_call | solution.py:88
  (221 shorter events, 94.0 us)
Async XLA Ops:
  7.2 70.8 %all-gather.2.cloned.1.call-start = ((), (), s32[]{:S(2)}) async-start(), calls=%async_computation | async-start | bytes 1892352 | tf_op jit(solution)/shard_map/all_gather | solution.py:792
  14.8 26.9 %collective-permute-start.3 = (bf16[128,768]{1,0:T(8,128)(2,1)S(1)}, bf16[128,768]{1,0:T(8,128)(2,1)S(1)}, u32[]{:S(2)}, u32[]{:S(2)}) collective-permute-start(bf16[128,768]{1,0:T(8,128)(2,1)S(1)} %get-tuple-element.117), channel_id=1, source_target_pairs={{0,1},{1,0},{2,3},{3,2},{4,5},{5,4},{6,7},{7,6},{8,9},{9,8},{10,11... | collective-permute-start | bytes 589832 | tf_op jit(solution)/shard_map/ppermute | solution.py:679
  15.0 26.7 %collective-permute-start.5 = (bf16[128,768]{1,0:T(8,128)(2,1)S(1)}, bf16[128,768]{1,0:T(8,128)(2,1)S(1)}, u32[]{:S(2)}, u32[]{:S(2)}) collective-permute-start(bf16[128,768]{1,0:T(8,128)(2,1)S(1)} %get-tuple-element.118), channel_id=1, source_target_pairs={{0,3},{1,2},{2,1},{3,0},{4,7},{5,6},{6,5},{7,4},{8,11},{9,10},{10,... | collective-permute-start | bytes 589832 | tf_op jit(solution)/shard_map/ppermute | solution.py:679
  17.2 24.5 %collective-permute-start.4 = (bf16[128,768]{1,0:T(8,128)(2,1)S(1)}, bf16[128,768]{1,0:T(8,128)(2,1)S(1)}, u32[]{:S(2)}, u32[]{:S(2)}) collective-permute-start(bf16[128,768]{1,0:T(8,128)(2,1)S(1)} %get-tuple-element.119), channel_id=1, source_target_pairs={{0,2},{1,3},{2,0},{3,1},{4,6},{5,7},{6,4},{7,5},{8,10},{9,11},{10,... | collective-permute-start | bytes 589832 | tf_op jit(solution)/shard_map/ppermute | solution.py:679
  123.4 35.2 %collective-permute-start.23 = (bf16[5,192,768]{2,1,0:T(8,128)(2,1)S(1)}, bf16[5,192,768]{2,1,0:T(8,128)(2,1)S(1)}, u32[]{:S(2)}, u32[]{:S(2)}) collective-permute-start(bf16[5,192,768]{2,1,0:T(8,128)(2,1)S(1)} %up_send.1.refs_9_), channel_id=1, source_target_pairs={{0,2},{1,3},{2,0},{3,1},{4,6},{5,7},{6,4},{7,5},{8,10},{9,11},{10,... | collective-permute-start | bytes 4423688 | tf_op jit(solution)/shard_map/ppermute | solution.py:679
  123.6 61.6 %collective-permute-start.28 = (bf16[4,192,768]{2,1,0:T(8,128)(2,1)S(1)}, bf16[4,192,768]{2,1,0:T(8,128)(2,1)S(1)}, u32[]{:S(2)}, u32[]{:S(2)}) collective-permute-start(bf16[4,192,768]{2,1,0:T(8,128)(2,1)S(1)} %down_send.1.refs_5_), channel_id=1, source_target_pairs={{0,2},{1,3},{2,0},{3,1},{4,6},{5,7},{6,4},{7,5},{8,10},{9,11},{10,... | collective-permute-start | bytes 3538952 | tf_op jit(solution)/shard_map/ppermute | solution.py:679
  141.3 25.9 %collective-permute-start.20 = (bf16[512,768]{1,0:T(8,128)(2,1)S(1)}, bf16[512,768]{1,0:T(8,128)(2,1)S(1)}, u32[]{:S(2)}, u32[]{:S(2)}) collective-permute-start(bf16[512,768]{1,0:T(8,128)(2,1)S(1)} %get-tuple-element.89.refs_4_), channel_id=1, source_target_pairs={{0,1},{1,0},{2,3},{3,2},{4,5},{5,4},{6,7},{7,6},{8,9},{9,8},{10,11... | collective-permute-start | bytes 2359304 | tf_op jit(solution)/shard_map/ppermute | solution.py:679
  141.4 25.8 %collective-permute-start.21 = (bf16[512,768]{1,0:T(8,128)(2,1)S(1)}, bf16[512,768]{1,0:T(8,128)(2,1)S(1)}, u32[]{:S(2)}, u32[]{:S(2)}) collective-permute-start(bf16[512,768]{1,0:T(8,128)(2,1)S(1)} %get-tuple-element.90.refs_5_), channel_id=1, source_target_pairs={{0,1},{1,0},{2,3},{3,2},{4,5},{5,4},{6,7},{7,6},{8,9},{9,8},{10,11... | collective-permute-start | bytes 2359304 | tf_op jit(solution)/shard_map/ppermute | solution.py:679
  141.9 25.3 %collective-permute-start.22 = (bf16[512,768]{1,0:T(8,128)(2,1)S(1)}, bf16[512,768]{1,0:T(8,128)(2,1)S(1)}, u32[]{:S(2)}, u32[]{:S(2)}) collective-permute-start(bf16[512,768]{1,0:T(8,128)(2,1)S(1)} %get-tuple-element.91.refs_6_), channel_id=1, source_target_pairs={{0,1},{1,0},{2,3},{3,2},{4,5},{5,4},{6,7},{7,6},{8,9},{9,8},{10,11... | collective-permute-start | bytes 2359304 | tf_op jit(solution)/shard_map/ppermute | solution.py:679
  165.6 19.0 %collective-permute-start.29 = (bf16[2,240,768]{2,1,0:T(8,128)(2,1)S(1)}, bf16[2,240,768]{2,1,0:T(8,128)(2,1)S(1)}, u32[]{:S(2)}, u32[]{:S(2)}) collective-permute-start(bf16[2,240,768]{2,1,0:T(8,128)(2,1)S(1)} %get-tuple-element.95), channel_id=1, source_target_pairs={{0,4},{4,0},{8,12},{12,8},{16,20},{20,16},{24,28},{28,24},{1,5},{5... | collective-permute-start | bytes 2211848 | tf_op jit(solution)/shard_map/ppermute | solution.py:679
  169.9 32.7 %collective-permute-start.27 = (bf16[592,768]{1,0:T(8,128)(2,1)S(1)}, bf16[592,768]{1,0:T(8,128)(2,1)S(1)}, u32[]{:S(2)}, u32[]{:S(2)}) collective-permute-start(bf16[592,768]{1,0:T(8,128)(2,1)S(1)} %qkv_send.1.refs_4_.refs_2_), channel_id=1, source_target_pairs={{0,2},{1,3},{2,0},{3,1},{4,6},{5,7},{6,4},{7,5},{8,10},{9,11},{10,... | collective-permute-start | bytes 2727944 | tf_op jit(solution)/shard_map/ppermute | solution.py:679
  189.7 20.5 %collective-permute-start.41 = (bf16[2,192,768]{2,1,0:T(8,128)(2,1)S(1)}, bf16[2,192,768]{2,1,0:T(8,128)(2,1)S(1)}, u32[]{:S(2)}, u32[]{:S(2)}) collective-permute-start(bf16[2,192,768]{2,1,0:T(8,128)(2,1)S(1)} %get-tuple-element.105), channel_id=1, source_target_pairs={{0,4},{4,0},{8,12},{12,8},{16,20},{20,16},{24,28},{28,24},{1,5},{5... | collective-permute-start | bytes 1769480 | tf_op jit(solution)/shard_map/ppermute | solution.py:679
  207.5 26.8 %collective-permute-start.8 = (bf16[128,768]{1,0:T(8,128)(2,1)S(1)}, bf16[128,768]{1,0:T(8,128)(2,1)S(1)}, u32[]{:S(2)}, u32[]{:S(2)}) collective-permute-start(bf16[128,768]{1,0:T(8,128)(2,1)S(1)} %get-tuple-element.112), channel_id=1, source_target_pairs={{0,3},{1,2},{2,1},{3,0},{4,7},{5,6},{6,5},{7,4},{8,11},{9,10},{10,... | collective-permute-start | bytes 589832 | tf_op jit(solution)/shard_map/ppermute | solution.py:679
  207.6 28.4 %collective-permute-start.7 = (bf16[128,768]{1,0:T(8,128)(2,1)S(1)}, bf16[128,768]{1,0:T(8,128)(2,1)S(1)}, u32[]{:S(2)}, u32[]{:S(2)}) collective-permute-start(bf16[128,768]{1,0:T(8,128)(2,1)S(1)} %get-tuple-element.113), channel_id=1, source_target_pairs={{0,2},{1,3},{2,0},{3,1},{4,6},{5,7},{6,4},{7,5},{8,10},{9,11},{10,... | collective-permute-start | bytes 589832 | tf_op jit(solution)/shard_map/ppermute | solution.py:679
  208.3 32.1 %collective-permute-start.6 = (bf16[128,768]{1,0:T(8,128)(2,1)S(1)}, bf16[128,768]{1,0:T(8,128)(2,1)S(1)}, u32[]{:S(2)}, u32[]{:S(2)}) collective-permute-start(bf16[128,768]{1,0:T(8,128)(2,1)S(1)} %get-tuple-element.114), channel_id=1, source_target_pairs={{0,1},{1,0},{2,3},{3,2},{4,5},{5,4},{6,7},{7,6},{8,9},{9,8},{10,11... | collective-permute-start | bytes 589832 | tf_op jit(solution)/shard_map/ppermute | solution.py:679
  218.4 19.4 %collective-permute-start.42 = (bf16[192,768]{1,0:T(8,128)(2,1)S(1)}, bf16[192,768]{1,0:T(8,128)(2,1)S(1)}, u32[]{:S(2)}, u32[]{:S(2)}) collective-permute-start(bf16[192,768]{1,0:T(8,128)(2,1)S(1)} %slice_bitcast_fusion.2), channel_id=1, source_target_pairs={{0,8},{4,12},{8,0},{12,4},{16,24},{20,28},{24,16},{28,20},{1,9},{5... | collective-permute-start | bytes 884744 | tf_op jit(solution)/shard_map/ppermute | solution.py:679
  236.0 22.9 %collective-permute-start.40 = (bf16[240,768]{1,0:T(8,128)(2,1)S(1)}, bf16[240,768]{1,0:T(8,128)(2,1)S(1)}, u32[]{:S(2)}, u32[]{:S(2)}) collective-permute-start(bf16[240,768]{1,0:T(8,128)(2,1)S(1)} %add_convert_fusion.1.refs_0_), channel_id=1, source_target_pairs={{0,12},{4,8},{8,4},{12,0},{16,28},{20,24},{24,20},{28,16},{1,13},{... | collective-permute-start | bytes 1105928 | tf_op jit(solution)/shard_map/ppermute | solution.py:679
  241.1 20.3 %collective-permute-start.43 = (bf16[192,768]{1,0:T(8,128)(2,1)S(1)}, bf16[192,768]{1,0:T(8,128)(2,1)S(1)}, u32[]{:S(2)}, u32[]{:S(2)}) collective-permute-start(bf16[192,768]{1,0:T(8,128)(2,1)S(1)} %fusion), channel_id=1, source_target_pairs={{0,24},{4,28},{8,16},{12,20},{16,8},{20,12},{24,0},{28,4},{1,25},{... | collective-permute-start | bytes 884744 | tf_op jit(solution)/shard_map/ppermute | solution.py:679
  245.4 19.0 %collective-permute-start.39 = (bf16[240,768]{1,0:T(8,128)(2,1)S(1)}, bf16[240,768]{1,0:T(8,128)(2,1)S(1)}, u32[]{:S(2)}, u32[]{:S(2)}) collective-permute-start(bf16[240,768]{1,0:T(8,128)(2,1)S(1)} %add_convert_fusion.1.refs_0_), channel_id=1, source_target_pairs={{0,4},{4,0},{8,12},{12,8},{16,20},{20,16},{24,28},{28,24},{1,5},{5... | collective-permute-start | bytes 1105928 | tf_op jit(solution)/shard_map/ppermute | solution.py:679
  255.9 19.5 %collective-permute-start.35 = (bf16[160,768]{1,0:T(8,128)(2,1)S(1)}, bf16[160,768]{1,0:T(8,128)(2,1)S(1)}, u32[]{:S(2)}, u32[]{:S(2)}) collective-permute-start(bf16[160,768]{1,0:T(8,128)(2,1)S(1)} %add_convert_fusion.3.refs_0_), channel_id=1, source_target_pairs={{0,12},{4,8},{8,4},{12,0},{16,28},{20,24},{24,20},{28,16},{1,13},{... | collective-permute-start | bytes 737288 | tf_op jit(solution)/shard_map/ppermute | solution.py:679
  258.9 26.7 %collective-permute-start.34 = (bf16[160,768]{1,0:T(8,128)(2,1)S(1)}, bf16[160,768]{1,0:T(8,128)(2,1)}, u32[]{:S(2)}, u32[]{:S(2)}) collective-permute-start(bf16[160,768]{1,0:T(8,128)(2,1)S(1)} %add_convert_fusion.3.refs_0_), channel_id=1, source_target_pairs={{0,4},{4,0},{8,12},{12,8},{16,20},{20,16},{24,28},{28,24},{1,5},{5... | collective-permute-start | bytes 737288 | tf_op jit(solution)/shard_map/ppermute | solution.py:679
  261.5 24.1 %collective-permute-start.33 = (bf16[160,768]{1,0:T(8,128)(2,1)S(1)}, bf16[160,768]{1,0:T(8,128)(2,1)}, u32[]{:S(2)}, u32[]{:S(2)}) collective-permute-start(bf16[160,768]{1,0:T(8,128)(2,1)S(1)} %add_convert_fusion.3.refs_0_), channel_id=1, source_target_pairs={{0,8},{4,12},{8,0},{12,4},{16,24},{20,28},{24,16},{28,20},{1,9},{5... | collective-permute-start | bytes 737288 | tf_op jit(solution)/shard_map/ppermute | solution.py:679
  264.4 25.3 %collective-permute-start.46 = (bf16[192,768]{1,0:T(8,128)(2,1)S(1)}, bf16[192,768]{1,0:T(8,128)(2,1)}, u32[]{:S(2)}, u32[]{:S(2)}) collective-permute-start(bf16[192,768]{1,0:T(8,128)(2,1)S(1)} %add_convert_fusion.2.refs_0_), channel_id=1, source_target_pairs={{0,12},{4,8},{8,4},{12,0},{16,28},{20,24},{24,20},{28,16},{1,13},{... | collective-permute-start | bytes 884744 | tf_op jit(solution)/shard_map/ppermute | solution.py:679
  269.9 19.9 %collective-permute-start.45 = (bf16[192,768]{1,0:T(8,128)(2,1)S(1)}, bf16[192,768]{1,0:T(8,128)(2,1)}, u32[]{:S(2)}, u32[]{:S(2)}) collective-permute-start(bf16[192,768]{1,0:T(8,128)(2,1)S(1)} %add_convert_fusion.2.refs_0_), channel_id=1, source_target_pairs={{0,4},{4,0},{8,12},{12,8},{16,20},{20,16},{24,28},{28,24},{1,5},{5... | collective-permute-start | bytes 884744 | tf_op jit(solution)/shard_map/ppermute | solution.py:679
  (65 other events, 520.8 us)
Sparse Core Ops, SparseCore 0:
  11.5 58.4 all-gather.1

commit v4 on v3

--- a/solution.py
+++ b/solution.py
@@ -490,6 +490,44 @@
     out_ref[0] = weight_total(two, lo_refs, lp_ref, go_ref, gp_ref).astype(bf16)
 
 
+def down_total(lo_ref, lp_ref, go_ref, gp_ref):
+    return nn(lo_ref[0, 0], go_ref[...]) + nn(lp_ref[0], gp_ref[...])
+
+
+def down_send_kernel(sc_ref, lo_ref, lp_ref, go_ref, gp_ref, out_ref):
+    out_ref[0] = down_total(lo_ref, lp_ref, go_ref, gp_ref).astype(bf16)
+
+
+def down_mid_kernel(sc_ref, lo_ref, lp_ref, go_ref, gp_ref, got_ref, near_ref, far_ref):
+    total = down_total(lo_ref, lp_ref, go_ref, gp_ref) + got_ref[pl.program_id(0)].astype(f32)
+    half = total.shape[0] // 2
+    for z in range(2):
+        part = total[z * half : (z + 1) * half].astype(bf16)
+
+        @pl.when(sc_ref[3] == z)
+        def _():
+            near_ref[0] = part
+
+        @pl.when(sc_ref[3] != z)
+        def _():
+            far_ref[0] = part
+
+
+def down_stage(kernel, sc, operands, got, outs, out_specs, steps, x, h, name, deps, micros=0):
+    lo, lp, go, gp = operands
+    rows = lo.shape[2]
+    return call(
+        kernel, sc, far(lo, lp) + (go, gp) + got,
+        [
+            pl.BlockSpec((1, 1) + lo.shape[2:], lambda i, s: (2 * x(i, s) + s[1], h(s), 0, 0)),
+            pl.BlockSpec((1, rows, lp.shape[2]), lambda i, s: (x(i, s), h(s), 0)),
+            whole(*go.shape), whole(*gp.shape),
+        ]
+        + [whole(*g.shape) for g in got],
+        outs, out_specs, (steps,), [], name, micros, deps,
+    )
+
+
 def deal(sc_ref, total, step, keep_ref, send_ref):
     rows = total.shape[0] // 4
     spot = pl.ds(step * rows if isinstance(step, int) else pl.multiple_of(step * rows, rows), rows)
@@ -579,7 +617,7 @@
     x = (lambda s: 1 - s[0]) if other else (lambda s: s[0])
     return [
         pl.BlockSpec((1,) + xt.shape[1:], lambda i, s: (2 * x(s) + s[1], 0, 0)),
-        pl.BlockSpec((1, 1) + halves.shape[2:], lambda i, s: (x(s), 2, 0, 0)),
+        pl.BlockSpec((1, 1) + halves.shape[2:], lambda i, s: (x(s), 6, 0, 0)),
     ] + [whole(2, EXTRA, 2 * SMALL)] * 2 + [whole(*own.shape)] * 6
 
 
@@ -665,12 +703,12 @@
         small[...] = parts[0][len(spots) * rows :, : small.shape[1]].astype(f32)
 
 
-def place(sc, parts, spots, dims, extra, name):
+def place(sc, parts, spots, dims, extra, name, deps=()):
     return call(
         functools.partial(place_kernel, spots, extra),
         sc, parts, [whole(*parts[0].shape)] * 4,
         [shape(f32, *dim) for dim in dims], [whole(*dim) for dim in dims], (1,), [],
-        name, 0,
+        name, 0, deps,
     )
 
 
@@ -694,28 +732,42 @@
 
 
 def join_kernel(sc_ref, left_ref, right_ref, out_ref):
-    out_ref[...] = (left_ref[...].astype(f32) + right_ref[...].astype(f32)).astype(bf16)
-
-
-def join(sc, left, right, deps):
+    out_ref[...] = add(left_ref[...], right_ref[...])
+
+
+def join(sc, left, right, deps, name, micros=0):
     block = whole(*left.shape)
     return call(
         join_kernel, sc, (left, right), [block, block], shape(bf16, *left.shape), block, (1,), [],
-        "join", 0, deps,
-    )
-
-
-def over_rows(sc, keep, send, masks, deps=(), later=()):
-    near, *rest = masks
-    value = keep
-    if send is not None:
-        got = flip(send, "rows", 1)
-        value = join(sc, keep, got, deps) if deps else add(keep, got)
-    got = flip(value[1], "rows", near)
-    value = join(sc, value[0], got, later) if later else add(value[0], got)
+        name, micros, deps,
+    )
+
+
+def join_two_kernel(slot, sc_ref, left_ref, right_ref, near_ref, far_ref):
+    own = 0 if slot is None else sc_ref[slot]
+    near_ref[...] = add(left_ref[own], right_ref[own])
+    far_ref[...] = add(left_ref[1 - own], right_ref[1 - own])
+
+
+def join_two(sc, left, right, deps, name, slot=None):
+    block, half = whole(*left.shape), whole(*left.shape[1:])
+    out = shape(bf16, *left.shape[1:])
+    return call(
+        functools.partial(join_two_kernel, slot), sc, (left, right), [block, block], [out, out],
+        [half, half], (1,), [], name, 0, deps,
+    )
+
+
+def across(sc, value, masks, deps, name):
+    first, *rest = masks
+    value = join(sc, value, flip(value, "rows", first), deps, name)
     for mask in rest:
         value = add(value, flip(value, "rows", mask))
-    return tuple([value] + [flip(value, "rows", mask) for mask in (near, 1, near ^ 1)])
+    return value
+
+
+def gathered(value, near):
+    return (value,) + tuple(flip(value, "rows", mask) for mask in (near, 1, near ^ 1))
 
 
 def add(left, right):
@@ -820,7 +872,7 @@
         t.reshape(2, 2, -1, quarter, t.shape[-1]), 1 - core, 1, keepdims=False
     )
     halves = swap(
-        jnp.concatenate([other_half(hidt), other_half(ctxt), other_half(xt), other_half(actt)], 1)
+        jnp.concatenate([other_half(actt), other_half(hidt), other_half(ctxt), other_half(xt)], 1)
     )
     quarters = lambda t: t.reshape(4, -1, t.shape[-1])
 
@@ -836,13 +888,19 @@
     gug, bup, gr_one, gctx, sums_one = feed_back(
         sc, gd, gr_two, w_down, w_up, slope, xhat_one, inv_one, row(gain_one), w_out, (gd_p,)
     )
-    down_ops = ((actt.reshape(4, 4, quarter, -1),), halves, gd[None], gd_p[None])
-    down_turn = lambda i: 3 + i
-    down_sent = weight_send(wsc, down_ops, 4, 0, down_turn, "down_send", (gug,))
-    down_got = flip(down_sent, "seq", 2)
+
+    near, *rest = masks
+    part = ff // 8
+    down_ops = (actt.reshape(4, 2, part, -1), halves.reshape(2, -1, piece * seq_count), gd, gd_p)
+    down_sent = down_stage(
+        down_send_kernel, wsc, down_ops, (), shape(bf16, 2, part, d),
+        pl.BlockSpec((1, part, d), lambda i, s: (i, 0, 0)), 2,
+        lambda i, s: i, lambda s: 1 - s[2], "down_send", (gug,),
+    )
+    down_got = flip(down_sent, "rows", 1)
 
     up_ops = ((quarters(hidt), quarters(ctxt)), halves, gug, swap(gug))
-    up_turn = lambda i: i // 4
+    up_turn = lambda i: 4 + i // 4
     up_sent = weight_send(wsc, up_ops, 5, 4, up_turn, "up_send", (down_sent,))
     up_got = flip(up_sent, "seq", 2)
 
@@ -853,31 +911,47 @@
     qkv_ops = (
         quarters(xt), halves, vec, swap(vec_far), gq, gk, gv, swap(gq), swap(gk), swap(gv)
     )
-    up_parts = weight_keep(wsc, up_ops, up_got, 5, 4, up_turn, "up_keep", (vec,))
-    qkv_sent = qkv_send(wsc, qkv_ops, (up_parts[0],))
+    qkv_sent = qkv_send(wsc, qkv_ops, ())
     qkv_got = flip(qkv_sent, "seq", 2)
-    up_got_rows = flip(up_parts[1], "rows", 1)
-    up_first = join(wsc, up_parts[0], up_got_rows, (qkv_sent,))
-    down_parts = weight_keep(
-        wsc, down_ops, down_got, 4, 0, down_turn, "down_keep", (up_first,), PIN
-    )
-    qkv_parts = qkv_keep(wsc, qkv_ops, qkv_got, (down_parts[0],))
-    up_sum = over_rows(wsc, up_first, None, masks, later=(qkv_parts[0],))
-    down_sum = over_rows(wsc, *down_parts, masks, (qkv_parts[0],))
-    qkv_sum = over_rows(wsc, *qkv_parts, masks)
-
-    mixed = gather_back(sc, mixed_row, seq_count, "mixed_order", (qkv_sent,))
-    grad_tokens = gather_back(sc, gtok, seq_count, "tokens_order", (qkv_parts[0],))
-
-    (grad_down,) = place(
-        wsc, down_sum, [(0, n, 0) for n in range(4)], [(4 * quarter, d)], 0, "down_place"
-    )
+    pair = shape(bf16, 2, part // 2, d)
+    each = pl.BlockSpec((1, part // 2, d), lambda i, s: (i, 0, 0))
+    down_near, down_far = down_stage(
+        down_mid_kernel, wsc, down_ops, (down_got,), [pair, pair], [each, each], 2,
+        lambda i, s: i, lambda s: s[2], "down_mid", (qkv_sent,), 3,
+    )
+    up_parts = weight_keep(
+        wsc, up_ops, up_got, 5, 4, up_turn, "up_keep", (vec, down_near), PIN
+    )
+    down_sum = join(wsc, down_near, flip(down_far, "rows", near), (up_parts[0],), "down_join_a", 3)
+    for mask in rest[1:]:
+        down_sum = add(down_sum, flip(down_sum, "rows", mask))
+    qkv_parts = qkv_keep(wsc, qkv_ops, qkv_got, (down_sum,))
+    up_near, up_far = join_two(
+        wsc, up_parts[0], flip(up_parts[1], "rows", 1), (qkv_parts[0],), "up_join_y"
+    )
+    qkv_near, qkv_far = join_two(
+        wsc, qkv_parts[0], flip(qkv_parts[1], "rows", 1), (up_near,), "qkv_join_y"
+    )
+    up_sum = join(wsc, up_near, flip(up_far, "rows", near), (qkv_near,), "up_join_a")
+    down_own, down_other = join_two(
+        wsc, down_sum, flip(down_sum, "rows", rest[0]), (up_sum,), "down_join_b", 0
+    )
+    qkv_sum = join(wsc, qkv_near, flip(qkv_far, "rows", near), (down_own,), "qkv_join_a")
+    down_sum = join(wsc, down_own, flip(down_other, "seq", 2), (qkv_sum,), "down_join_x")
+    down_all = gathered(down_sum, near)
+    up_sum = across(wsc, up_sum, rest, (down_sum,), "up_join_b")
+    up_all = gathered(up_sum, near)
+    (grad_down,) = place(wsc, down_all, [(0, 0, 0)], [(4 * quarter, d)], 0, "down_place", (up_sum,))
+    qkv_sum = across(wsc, qkv_sum, rest, (grad_down,), "qkv_join_b")
+    qkv_all = gathered(qkv_sum, near)
+    mixed = gather_back(sc, mixed_row, seq_count, "mixed_order", (down_sum,))
+    grad_tokens = gather_back(sc, gtok, seq_count, "tokens_order", (qkv_sum,))
     grad_up, grad_o = place(
-        wsc, up_sum, [(0, 0, n) for n in range(4)] + [(1, 0, 0)],
-        [(quarter, ff), (quarter, d)], 0, "up_place",
+        wsc, up_all, [(0, 0, n) for n in range(4)] + [(1, 0, 0)],
+        [(quarter, ff), (quarter, d)], 0, "up_place", (qkv_sum,),
     )
     grad_q, grad_k, grad_v, small = place(
-        wsc, qkv_sum, [(n, 0, 0) for n in range(3)], [(quarter, d)] * 3 + [(EXTRA, 2 * SMALL)],
+        wsc, qkv_all, [(n, 0, 0) for n in range(3)], [(quarter, d)] * 3 + [(EXTRA, 2 * SMALL)],
         EXTRA, "qkv_place",
     )
 

time: 303 us -> 269 us (0.89)
  waiting for transfers between devices: 103 us -> 72.5 us
    ppermute x46, waiting for transfers between devices: 102 us -> 71.6 us  [flip(): return lax.ppermute(value, axis, [(i, i ^ mask) for i in range(count)])]
    pallas_call x20 -> x26, Pallas kernels: 116 us -> 116 us  [call(): pl.pallas_call(body, grid_spec=pltpu.PrefetchScalarGridSpec(num_scalar_pr...]
    unnamed x88 -> x78, local copies, waits for them, and re-layouts: 11.5 us -> 11.5 us
  transfers between devices with their start and end apart: 48 -> 48, of which waited for: 22 -> 30; matrix products, arithmetic and copies ran while one was open for 3% -> 2% of each run, Pallas kernels for 26% -> 33%
where the time goes in v4:
time: 269 us; the launch traced here: 268 us
  Pallas kernels  116 us (43%)
  waiting for transfers between devices  72.5 us (27%)
  starting transfers between devices  44.8 us (17%)
  local copies, waits for them, and re-layouts  17.2 us (6%)
  between operations  14.8 us (6%)
  other arithmetic  3.03 us (1%)
    pallas_call x26, Pallas kernels, call(): pl.pallas_call(body, grid_spec=pltpu.PrefetchScalarGridSpec(num_scalar_pr...  116 us
    ppermute x46, waiting for transfers between devices, flip(): return lax.ppermute(value, axis, [(i, i ^ mask) for i in range(count)])  71.6 us
    ppermute x46, starting transfers between devices, flip(): return lax.ppermute(value, axis, [(i, i ^ mask) for i in range(count)])  41.7 us
    unnamed x78, local copies, waits for them, and re-layouts  11.5 us
  transfers between devices with their start and end apart: 48, of which 30 were waited for; matrix products, arithmetic and copies ran while one was open for 2% of the time, Pallas kernels for 33%

profile of v4, /device:TPU:0, one launch (start us, length us, event | category | flops | bytes accessed | tf_op | source)
XLA Modules:
  0.0 268.5 jit_solution(2638226536945947112)
XLA Ops:
  19.4 4.7 %collective-permute-done.1 = bf16[128,768]{1,0:T(8,128)(2,1)S(1)} collective-permute-done((bf16[128,768]{1,0:T(8,128)(2,1)S(1)}, bf16[128,768]{1,0:T(8,128)(2,1)S(1)}, u32[]{:S(2)}, u32[]{:S(2)}) %collective-permute-start.1) | collective-permute-done | bytes 196640 | tf_op jit(solution)/shard_map/ppermute | solution.py:717
  24.1 16.9 %attention_forward.1 = (bf16[512,768]{1,0:T(8,128)(2,1)}, bf16[512,768]{1,0:T(8,128)(2,1)}, bf16[512,768]{1,0:T(8,128)(2,1)}, bf16[768,512]{1,0:T(8,128)(2,1)}, ...) custom-call(s32[8]{0:T(128)S(1)} %pad_add_fusion.sc_ref, ...), custom_call_target="tpu_custom_call" | custom-call | tf_op jit(solution)/shard_map/attention_forward/pallas_call | solution.py:88
  42.5 14.3 %feed_forward.1 = (bf16[3072,512]{1,0:T(8,128)(2,1)}, bf16[4,512,768]{2,1,0:T(8,128)(2,1)}, f32[512,768]{1,0:T(8,128)}, f32[512,1]{1,0:T(8,128)}, bf16[512,768]{1,0:T(8,128)(2,1)}, /*index=5*/f32[8,768]{1,0:T(8,128)S(1)}) custom-call(s32[8]{0:T(128)S(1)} %pad_add_fusion.sc_ref, bf16[512,768]{1,0:T(8,128)(2,1)S(1)} %get-tuple-element.68.refs_0_, ...), custom_call_target="tpu_custom_call" | custom-call | tf_op jit(solution)/shard_map/feed_forward/pallas_call | solution.py:88
  59.0 3.1 %collective-permute-start.12 = (bf16[8,768]{1,0:T(8,128)(2,1)S(1)}, bf16[8,768]{1,0:T(8,128)(2,1)S(1)}, u32[]{:S(2)}, u32[]{:S(2)}) collective-permute-start(bf16[8,768]{1,0:T(8,128)(2,1)S(1)} %get-tuple-element.119), channel_id=1, source_target_pairs={{0,6},{1,7},{2,4},{3,5},{4,2},{5,3},{6,0},{7,1},{8,14},{9,15},{10,... | collective-permute-start | bytes 36872 | tf_op jit(solution)/shard_map/ppermute | solution.py:725
  70.7 3.6 %collective-permute-done.13 = bf16[32,768]{1,0:T(8,128)(2,1)S(1)} collective-permute-done((bf16[32,768]{1,0:T(8,128)(2,1)S(1)}, bf16[32,768]{1,0:T(8,128)(2,1)S(1)}, u32[]{:S(2)}, u32[]{:S(2)}) %collective-permute-start.13) | collective-permute-done | bytes 49184 | tf_op jit(solution)/shard_map/ppermute | solution.py:717
  78.5 13.3 %retrieval.1 = (f32[1024,1]{1,0:T(8,128)S(1)}, bf16[512,768]{1,0:T(8,128)(2,1)S(1)}, f32[512,768]{1,0:T(8,128)S(1)}, f32[8,768]{1,0:T(8,128)S(1)}) custom-call(s32[8]{0:T(128)S(1)} %pad_add_fusion.sc_ref, bf16[1024,832]{1,0:T(8,128)(2,1)} %all-gather.2.cloned.1.call-done.refs_0_, bf16[256,768]{1,0:T(8,128)(2,1)S(1)} %copy-done.10, ...), custom_call_target="tpu_custom_call" | custom-call | tf_op jit(solution)/shard_map/retrieval/pallas_call | solution.py:88
  94.9 13.5 %feed_back.1 = (bf16[5,512,768]{2,1,0:T(8,128)(2,1)}, f32[4,1,768]{2,1,0:T(1,128)S(1)}, f32[512,768]{1,0:T(8,128)S(1)}, bf16[512,768]{1,0:T(8,128)(2,1)S(1)}, f32[8,768]{1,0:T(8,128)S(1)}) custom-call(s32[8]{0:T(128)S(1)} %pad_add_fusion.sc_ref, bf16[512,768]{1,0:T(8,128)(2,1)S(1)} %get-tuple-element.77.refs_0_.refs_2_, ...), custom_call_target="tpu_custom_call" | custom-call | tf_op jit(solution)/shard_map/feed_back/pallas_call | solution.py:88
  110.6 3.3 %down_send.1.refs_5_ = bf16[2,384,768]{2,1,0:T(8,128)(2,1)S(1)} custom-call(s32[4]{0:T(128)S(1)} %pad_add_fusion.1.sc_ref, bf16[4,2,384,512]{3,2,1,0:T(8,128)(2,1)} %bitcast.62, bf16[2,1344,512]{2,1,0:T(8,128)(2,1)} %bitcast.58, bf16[512,768]{1,0:T(8,128)(2,1)S(1)} %get-tuple-element.77.refs_0_.refs_2_, ...), custom_call_target="tpu_custom_call" | custom-call | tf_op jit(solution)/shard_map/down_send/pallas_call | solution.py:88
  117.5 6.8 %up_send.1.refs_9_ = bf16[5,192,768]{2,1,0:T(8,128)(2,1)S(1)} custom-call(s32[4]{0:T(128)S(1)} %pad_add_fusion.1.sc_ref, bf16[4,192,512]{2,1,0:T(8,128)(2,1)} %bitcast.70, bf16[4,192,512]{2,1,0:T(8,128)(2,1)} %bitcast.67, bf16[2,7,192,512]{3,2,1,0:T(8,128)(2,1)} %copy-done.2, bf16[5,512,768]{2,1,0:T(8,128)(2,1)} %get-tuple-element.82.refs_4_.refs_3_, ...), custom_call_target="tpu_custom_call" | custom-call | tf_op jit(solution)/shard_map/up_send/pallas_call | solution.py:88
  124.9 15.8 %attention_back.1 = (bf16[512,768]{1,0:T(8,128)(2,1)S(1)}, bf16[512,768]{1,0:T(8,128)(2,1)S(1)}, bf16[512,768]{1,0:T(8,128)(2,1)S(1)}, bf16[512,768]{1,0:T(8,128)(2,1)S(1)}, f32[8,768]{1,0:T(8,128)S(1)}) custom-call(s32[8]{0:T(128)S(1)} %pad_add_fusion.sc_ref, bf16[512,768]{1,0:T(8,128)(2,1)} %get-tuple-element.83.refs_0_, ...), custom_call_target="tpu_custom_call" | custom-call | tf_op jit(solution)/shard_map/attention_back/pallas_call | solution.py:88
  146.2 2.7 qkv_send.1.refs_5_
  150.5 3.7 %down_mid.1 = (bf16[2,192,768]{2,1,0:T(8,128)(2,1)S(1)}, bf16[2,192,768]{2,1,0:T(8,128)(2,1)S(1)}) custom-call(s32[4]{0:T(128)S(1)} %pad_add_fusion.1.sc_ref, bf16[4,2,384,512]{3,2,1,0:T(8,128)(2,1)} %bitcast.63, bf16[2,1344,512]{2,1,0:T(8,128)(2,1)} %bitcast.59, bf16[512,768]{1,0:T(8,128)(2,1)S(1)} %get-tuple-element.77.refs_0_.refs_2_, ...), custom_call_target="tpu_custom_call" | custom-call | flops 3449999872 | tf_op jit(solution)/shard_map/down_mid/pallas_call | solution.py:88
  154.2 5.3 %collective-permute-done.25.refs_5_ = bf16[5,192,768]{2,1,0:T(8,128)(2,1)S(1)} collective-permute-done((bf16[5,192,768]{2,1,0:T(8,128)(2,1)S(1)}, bf16[5,192,768]{2,1,0:T(8,128)(2,1)S(1)}, u32[]{:S(2)}, u32[]{:S(2)}) %collective-permute-start.25) | collective-permute-done | bytes 1474592 | tf_op jit(solution)/shard_map/ppermute | solution.py:717
  159.5 6.9 %up_keep.1 = (bf16[2,240,768]{2,1,0:T(8,128)(2,1)S(1)}, bf16[2,240,768]{2,1,0:T(8,128)(2,1)S(1)}) custom-call(s32[4]{0:T(128)S(1)} %pad_add_fusion.1.sc_ref, bf16[4,192,512]{2,1,0:T(8,128)(2,1)} %bitcast.71, bf16[4,192,512]{2,1,0:T(8,128)(2,1)} %bitcast.68, bf16[2,7,192,512]{3,2,1,0:T(8,128)(2,1)} %copy-done.2, ...), custom_call_target="tpu_custom_call" | custom-call | flops 115000000512 | tf_op jit(solution)/shard_map/up_keep/pallas_call | solution.py:88
  172.3 5.9 %collective-permute-done.28.refs_10_ = bf16[592,768]{1,0:T(8,128)(2,1)S(1)} collective-permute-done((bf16[592,768]{1,0:T(8,128)(2,1)S(1)}, bf16[592,768]{1,0:T(8,128)(2,1)S(1)}, u32[]{:S(2)}, u32[]{:S(2)}) %collective-permute-start.28) | collective-permute-done | bytes 909344 | tf_op jit(solution)/shard_map/ppermute | solution.py:717
  178.2 3.0 %qkv_keep.1 = (bf16[2,160,768]{2,1,0:T(8,128)(2,1)S(1)}, bf16[2,160,768]{2,1,0:T(8,128)(2,1)S(1)}) custom-call(s32[4]{0:T(128)S(1)} %pad_add_fusion.1.sc_ref, bf16[4,192,512]{2,1,0:T(8,128)(2,1)} %bitcast.65, bf16[2,7,192,512]{3,2,1,0:T(8,128)(2,1)} %copy-done.2, f32[2,16,256]{2,1,0:T(8,128)S(1)} %get-tuple-element.93.refs_2_.refs_6_, ...), custom_call_target="tpu_custom_call" | custom-call | tf_op jit(solution)/shard_map/qkv_keep/pallas_call | solution.py:88
  184.3 9.6 %collective-permute-done.30.refs_1_ = bf16[2,160,768]{2,1,0:T(8,128)(2,1)S(1)} collective-permute-done((bf16[2,160,768]{2,1,0:T(8,128)(2,1)S(1)}, bf16[2,160,768]{2,1,0:T(8,128)(2,1)S(1)}, u32[]{:S(2)}, u32[]{:S(2)}) %collective-permute-start.30) | collective-permute-done | bytes 491552 | tf_op jit(solution)/shard_map/ppermute | solution.py:717
  203.2 2.8 %collective-permute-done.31.refs_1_ = bf16[192,768]{1,0:T(8,128)(2,1)S(1)} collective-permute-done((bf16[192,768]{1,0:T(8,128)(2,1)S(1)}, bf16[192,768]{1,0:T(8,128)(2,1)S(1)}, u32[]{:S(2)}, u32[]{:S(2)}) %collective-permute-start.31) | collective-permute-done | bytes 294944 | tf_op jit(solution)/shard_map/ppermute | solution.py:717
  208.3 3.6 %collective-permute-start.39 = (bf16[192,768]{1,0:T(8,128)(2,1)S(1)}, bf16[192,768]{1,0:T(8,128)(2,1)S(1)}, u32[]{:S(2)}, u32[]{:S(2)}) collective-permute-start(bf16[192,768]{1,0:T(8,128)(2,1)S(1)} %down_join_x.1.refs_4_.refs_2_.refs_0_), channel_id=1, source_target_pairs={{0,12},{4,8},{8,4},{12,0},{16,28},{20,24},{24,20},{28,16},{1,13},{... | collective-permute-start | bytes 884744 | tf_op jit(solution)/shard_map/ppermute | solution.py:717
  222.2 3.9 %collective-permute-done.36.refs_1_ = bf16[160,768]{1,0:T(8,128)(2,1)S(1)} collective-permute-done((bf16[160,768]{1,0:T(8,128)(2,1)S(1)}, bf16[160,768]{1,0:T(8,128)(2,1)S(1)}, u32[]{:S(2)}, u32[]{:S(2)}) %collective-permute-start.36) | collective-permute-done | bytes 245792 | tf_op jit(solution)/shard_map/ppermute | solution.py:717
  226.1 2.9 %collective-permute-start.34 = (bf16[128,768]{1,0:T(8,128)(2,1)S(1)}, bf16[128,768]{1,0:T(8,128)(2,1)S(1)}, u32[]{:S(2)}, u32[]{:S(2)}) collective-permute-start(bf16[128,768]{1,0:T(8,128)(2,1)S(1)} %get-tuple-element.121), channel_id=1, source_target_pairs={{0,2},{1,3},{2,0},{3,1},{4,6},{5,7},{6,4},{7,5},{8,10},{9,11},{10,... | collective-permute-start | bytes 589832 | tf_op jit(solution)/shard_map/ppermute | solution.py:717
  229.3 3.9 %collective-permute-done.37.refs_1_ = bf16[192,768]{1,0:T(8,128)(2,1)S(1)} collective-permute-done((bf16[192,768]{1,0:T(8,128)(2,1)S(1)}, bf16[192,768]{1,0:T(8,128)(2,1)S(1)}, u32[]{:S(2)}, u32[]{:S(2)}) %collective-permute-start.37) | collective-permute-done | bytes 294944 | tf_op jit(solution)/shard_map/ppermute | solution.py:717
  251.4 2.8 %collective-permute-done.43.refs_3_ = bf16[160,768]{1,0:T(8,128)(2,1)S(1)} collective-permute-done((bf16[160,768]{1,0:T(8,128)(2,1)S(1)}, bf16[160,768]{1,0:T(8,128)(2,1)S(1)}, u32[]{:S(2)}, u32[]{:S(2)}) %collective-permute-start.43) | collective-permute-done | bytes 245792 | tf_op jit(solution)/shard_map/ppermute | solution.py:717
  254.2 4.2 %collective-permute-done.42.refs_2_ = bf16[160,768]{1,0:T(8,128)(2,1)S(1)} collective-permute-done((bf16[160,768]{1,0:T(8,128)(2,1)S(1)}, bf16[160,768]{1,0:T(8,128)(2,1)S(1)}, u32[]{:S(2)}, u32[]{:S(2)}) %collective-permute-start.42) | collective-permute-done | bytes 245792 | tf_op jit(solution)/shard_map/ppermute | solution.py:717
  (208 shorter events, 97.0 us)
Async XLA Ops:
  7.2 70.0 %all-gather.2.cloned.1.call-start = ((), (), s32[]{:S(2)}) async-start(), calls=%async_computation | async-start | bytes 1892352 | tf_op jit(solution)/shard_map/all_gather | solution.py:844
  14.3 26.8 %collective-permute-start.3 = (bf16[128,768]{1,0:T(8,128)(2,1)S(1)}, bf16[128,768]{1,0:T(8,128)(2,1)S(1)}, u32[]{:S(2)}, u32[]{:S(2)}) collective-permute-start(bf16[128,768]{1,0:T(8,128)(2,1)S(1)} %get-tuple-element.129), channel_id=1, source_target_pairs={{0,1},{1,0},{2,3},{3,2},{4,5},{5,4},{6,7},{7,6},{8,9},{9,8},{10,11... | collective-permute-start | bytes 589832 | tf_op jit(solution)/shard_map/ppermute | solution.py:717
  14.4 26.7 %collective-permute-start.5 = (bf16[128,768]{1,0:T(8,128)(2,1)S(1)}, bf16[128,768]{1,0:T(8,128)(2,1)S(1)}, u32[]{:S(2)}, u32[]{:S(2)}) collective-permute-start(bf16[128,768]{1,0:T(8,128)(2,1)S(1)} %get-tuple-element.130), channel_id=1, source_target_pairs={{0,3},{1,2},{2,1},{3,0},{4,7},{5,6},{6,5},{7,4},{8,11},{9,10},{10,... | collective-permute-start | bytes 589832 | tf_op jit(solution)/shard_map/ppermute | solution.py:717
  16.6 24.5 %collective-permute-start.4 = (bf16[128,768]{1,0:T(8,128)(2,1)S(1)}, bf16[128,768]{1,0:T(8,128)(2,1)S(1)}, u32[]{:S(2)}, u32[]{:S(2)}) collective-permute-start(bf16[128,768]{1,0:T(8,128)(2,1)S(1)} %get-tuple-element.131), channel_id=1, source_target_pairs={{0,2},{1,3},{2,0},{3,1},{4,6},{5,7},{6,4},{7,5},{8,10},{9,11},{10,... | collective-permute-start | bytes 589832 | tf_op jit(solution)/shard_map/ppermute | solution.py:717
  58.9 18.3 %collective-permute-start.9 = (bf16[2,7,192,512]{3,2,1,0:T(8,128)(2,1)S(1)}, bf16[2,7,192,512]{3,2,1,0:T(8,128)(2,1)S(1)}, u32[]{:S(2)}, u32[]{:S(2)}) collective-permute-start(bf16[2,7,192,512]{3,2,1,0:T(8,128)(2,1)S(1)} %pad_maximum_fusion), channel_id=1, source_target_pairs={{0,1},{1,0},{2,3},{3,2},{4,5},{5,4},{6,7},{7,6},{8,9},{9,8},{10,11... | collective-permute-start | bytes 8257544 | tf_op jit(solution)/shard_map/ppermute | solution.py:717
  113.9 36.6 %collective-permute-start.18 = (bf16[2,384,768]{2,1,0:T(8,128)(2,1)S(1)}, bf16[2,384,768]{2,1,0:T(8,128)(2,1)S(1)}, u32[]{:S(2)}, u32[]{:S(2)}) collective-permute-start(bf16[2,384,768]{2,1,0:T(8,128)(2,1)S(1)} %down_send.1.refs_5_), channel_id=1, source_target_pairs={{0,4},{4,0},{8,12},{12,8},{16,20},{20,16},{24,28},{28,24},{1,5},{5... | collective-permute-start | bytes 3538952 | tf_op jit(solution)/shard_map/ppermute | solution.py:717
  124.3 35.2 %collective-permute-start.25 = (bf16[5,192,768]{2,1,0:T(8,128)(2,1)S(1)}, bf16[5,192,768]{2,1,0:T(8,128)(2,1)S(1)}, u32[]{:S(2)}, u32[]{:S(2)}) collective-permute-start(bf16[5,192,768]{2,1,0:T(8,128)(2,1)S(1)} %up_send.1.refs_9_), channel_id=1, source_target_pairs={{0,2},{1,3},{2,0},{3,1},{4,6},{5,7},{6,4},{7,5},{8,10},{9,11},{10,... | collective-permute-start | bytes 4423688 | tf_op jit(solution)/shard_map/ppermute | solution.py:717
  148.9 29.4 %collective-permute-start.28 = (bf16[592,768]{1,0:T(8,128)(2,1)S(1)}, bf16[592,768]{1,0:T(8,128)(2,1)S(1)}, u32[]{:S(2)}, u32[]{:S(2)}) collective-permute-start(bf16[592,768]{1,0:T(8,128)(2,1)S(1)} %qkv_send.1.refs_5_), channel_id=1, source_target_pairs={{0,2},{1,3},{2,0},{3,1},{4,6},{5,7},{6,4},{7,5},{8,10},{9,11},{10,... | collective-permute-start | bytes 2727944 | tf_op jit(solution)/shard_map/ppermute | solution.py:717
  154.1 15.4 %collective-permute-start.24 = (bf16[2,192,768]{2,1,0:T(8,128)(2,1)S(1)}, bf16[2,192,768]{2,1,0:T(8,128)(2,1)S(1)}, u32[]{:S(2)}, u32[]{:S(2)}) collective-permute-start(bf16[2,192,768]{2,1,0:T(8,128)(2,1)S(1)} %get-tuple-element.99), channel_id=1, source_target_pairs={{0,8},{4,12},{8,0},{12,4},{16,24},{20,28},{24,16},{28,20},{1,9},{5... | collective-permute-start | bytes 1769480 | tf_op jit(solution)/shard_map/ppermute | solution.py:717
  166.5 17.1 %collective-permute-start.27 = (bf16[2,240,768]{2,1,0:T(8,128)(2,1)S(1)}, bf16[2,240,768]{2,1,0:T(8,128)(2,1)S(1)}, u32[]{:S(2)}, u32[]{:S(2)}) collective-permute-start(bf16[2,240,768]{2,1,0:T(8,128)(2,1)S(1)} %get-tuple-element.101), channel_id=1, source_target_pairs={{0,4},{4,0},{8,12},{12,8},{16,20},{20,16},{24,28},{28,24},{1,5},{5... | collective-permute-start | bytes 2211848 | tf_op jit(solution)/shard_map/ppermute | solution.py:717
  170.2 25.2 %collective-permute-start.26 = (bf16[2,192,768]{2,1,0:T(8,128)(2,1)S(1)}, bf16[2,192,768]{2,1,0:T(8,128)(2,1)S(1)}, u32[]{:S(2)}, u32[]{:S(2)}) collective-permute-start(bf16[2,192,768]{2,1,0:T(8,128)(2,1)S(1)} %down_join_a.1.refs_11_.refs_0_), channel_id=1, source_target_pairs={{0,24},{4,28},{8,16},{12,20},{16,8},{20,12},{24,0},{28,4},{1,25},{... | collective-permute-start | bytes 1769480 | tf_op jit(solution)/shard_map/ppermute | solution.py:717
  181.3 12.7 %collective-permute-start.30 = (bf16[2,160,768]{2,1,0:T(8,128)(2,1)S(1)}, bf16[2,160,768]{2,1,0:T(8,128)(2,1)S(1)}, u32[]{:S(2)}, u32[]{:S(2)}) collective-permute-start(bf16[2,160,768]{2,1,0:T(8,128)(2,1)S(1)} %get-tuple-element.105), channel_id=1, source_target_pairs={{0,4},{4,0},{8,12},{12,8},{16,20},{20,16},{24,28},{28,24},{1,5},{5... | collective-permute-start | bytes 1474568 | tf_op jit(solution)/shard_map/ppermute | solution.py:717
  196.7 17.4 %collective-permute-start.7 = (bf16[128,768]{1,0:T(8,128)(2,1)S(1)}, bf16[128,768]{1,0:T(8,128)(2,1)S(1)}, u32[]{:S(2)}, u32[]{:S(2)}) collective-permute-start(bf16[128,768]{1,0:T(8,128)(2,1)S(1)} %get-tuple-element.125), channel_id=1, source_target_pairs={{0,2},{1,3},{2,0},{3,1},{4,6},{5,7},{6,4},{7,5},{8,10},{9,11},{10,... | collective-permute-start | bytes 589832 | tf_op jit(solution)/shard_map/ppermute | solution.py:717
  198.4 18.3 %collective-permute-start.6 = (bf16[128,768]{1,0:T(8,128)(2,1)S(1)}, bf16[128,768]{1,0:T(8,128)(2,1)S(1)}, u32[]{:S(2)}, u32[]{:S(2)}) collective-permute-start(bf16[128,768]{1,0:T(8,128)(2,1)S(1)} %get-tuple-element.126), channel_id=1, source_target_pairs={{0,1},{1,0},{2,3},{3,2},{4,5},{5,4},{6,7},{7,6},{8,9},{9,8},{10,11... | collective-permute-start | bytes 589832 | tf_op jit(solution)/shard_map/ppermute | solution.py:717
  201.1 17.8 %collective-permute-start.40 = (bf16[240,768]{1,0:T(8,128)(2,1)S(1)}, bf16[240,768]{1,0:T(8,128)(2,1)S(1)}, u32[]{:S(2)}, u32[]{:S(2)}) collective-permute-start(bf16[240,768]{1,0:T(8,128)(2,1)S(1)} %up_join_a.1.refs_2_.refs_0_), channel_id=1, source_target_pairs={{0,24},{4,28},{8,16},{12,20},{16,8},{20,12},{24,0},{28,4},{1,25},{... | collective-permute-start | bytes 1105928 | tf_op jit(solution)/shard_map/ppermute | solution.py:717
  206.1 14.8 %collective-permute-start.35 = (bf16[128,768]{1,0:T(8,128)(2,1)S(1)}, bf16[128,768]{1,0:T(8,128)(2,1)S(1)}, u32[]{:S(2)}, u32[]{:S(2)}) collective-permute-start(bf16[128,768]{1,0:T(8,128)(2,1)S(1)} %get-tuple-element.120), channel_id=1, source_target_pairs={{0,3},{1,2},{2,1},{3,0},{4,7},{5,6},{6,5},{7,4},{8,11},{9,10},{10,... | collective-permute-start | bytes 589832 | tf_op jit(solution)/shard_map/ppermute | solution.py:717
  208.3 20.7 %collective-permute-start.39 = (bf16[192,768]{1,0:T(8,128)(2,1)S(1)}, bf16[192,768]{1,0:T(8,128)(2,1)S(1)}, u32[]{:S(2)}, u32[]{:S(2)}) collective-permute-start(bf16[192,768]{1,0:T(8,128)(2,1)S(1)} %down_join_x.1.refs_4_.refs_2_.refs_0_), channel_id=1, source_target_pairs={{0,12},{4,8},{8,4},{12,0},{16,28},{20,24},{24,20},{28,16},{1,13},{... | collective-permute-start | bytes 884744 | tf_op jit(solution)/shard_map/ppermute | solution.py:717
  219.0 14.3 %collective-permute-start.37 = (bf16[192,768]{1,0:T(8,128)(2,1)S(1)}, bf16[192,768]{1,0:T(8,128)(2,1)S(1)}, u32[]{:S(2)}, u32[]{:S(2)}) collective-permute-start(bf16[192,768]{1,0:T(8,128)(2,1)S(1)} %down_join_x.1.refs_4_.refs_2_.refs_0_), channel_id=1, source_target_pairs={{0,8},{4,12},{8,0},{12,4},{16,24},{20,28},{24,16},{28,20},{1,9},{5... | collective-permute-start | bytes 884744 | tf_op jit(solution)/shard_map/ppermute | solution.py:717
  221.5 21.0 %collective-permute-start.46 = (bf16[240,768]{1,0:T(8,128)(2,1)S(1)}, bf16[240,768]{1,0:T(8,128)(2,1)S(1)}, u32[]{:S(2)}, u32[]{:S(2)}) collective-permute-start(bf16[240,768]{1,0:T(8,128)(2,1)S(1)} %up_join_b.1.refs_4_.refs_0_), channel_id=1, source_target_pairs={{0,12},{4,8},{8,4},{12,0},{16,28},{20,24},{24,20},{28,16},{1,13},{... | collective-permute-start | bytes 1105928 | tf_op jit(solution)/shard_map/ppermute | solution.py:717
  229.0 19.4 %collective-permute-start.45 = (bf16[240,768]{1,0:T(8,128)(2,1)S(1)}, bf16[240,768]{1,0:T(8,128)(2,1)S(1)}, u32[]{:S(2)}, u32[]{:S(2)}) collective-permute-start(bf16[240,768]{1,0:T(8,128)(2,1)S(1)} %up_join_b.1.refs_4_.refs_0_), channel_id=1, source_target_pairs={{0,4},{4,0},{8,12},{12,8},{16,20},{20,16},{24,28},{28,24},{1,5},{5... | collective-permute-start | bytes 1105928 | tf_op jit(solution)/shard_map/ppermute | solution.py:717
  233.3 15.8 %collective-permute-start.44 = (bf16[240,768]{1,0:T(8,128)(2,1)S(1)}, bf16[240,768]{1,0:T(8,128)(2,1)S(1)}, u32[]{:S(2)}, u32[]{:S(2)}) collective-permute-start(bf16[240,768]{1,0:T(8,128)(2,1)S(1)} %up_join_b.1.refs_4_.refs_0_), channel_id=1, source_target_pairs={{0,8},{4,12},{8,0},{12,4},{16,24},{20,28},{24,16},{28,20},{1,9},{5... | collective-permute-start | bytes 1105928 | tf_op jit(solution)/shard_map/ppermute | solution.py:717
  238.3 15.9 %collective-permute-start.43 = (bf16[160,768]{1,0:T(8,128)(2,1)S(1)}, bf16[160,768]{1,0:T(8,128)(2,1)S(1)}, u32[]{:S(2)}, u32[]{:S(2)}) collective-permute-start(bf16[160,768]{1,0:T(8,128)(2,1)S(1)} %qkv_join_b.1.refs_4_.refs_0_), channel_id=1, source_target_pairs={{0,12},{4,8},{8,4},{12,0},{16,28},{20,24},{24,20},{28,16},{1,13},{... | collective-permute-start | bytes 737288 | tf_op jit(solution)/shard_map/ppermute | solution.py:717
  240.8 17.6 %collective-permute-start.42 = (bf16[160,768]{1,0:T(8,128)(2,1)S(1)}, bf16[160,768]{1,0:T(8,128)(2,1)S(1)}, u32[]{:S(2)}, u32[]{:S(2)}) collective-permute-start(bf16[160,768]{1,0:T(8,128)(2,1)S(1)} %qkv_join_b.1.refs_4_.refs_0_), channel_id=1, source_target_pairs={{0,4},{4,0},{8,12},{12,8},{16,20},{20,16},{24,28},{28,24},{1,5},{5... | collective-permute-start | bytes 737288 | tf_op jit(solution)/shard_map/ppermute | solution.py:717
  242.5 16.0 %collective-permute-start.41 = (bf16[160,768]{1,0:T(8,128)(2,1)S(1)}, bf16[160,768]{1,0:T(8,128)(2,1)S(1)}, u32[]{:S(2)}, u32[]{:S(2)}) collective-permute-start(bf16[160,768]{1,0:T(8,128)(2,1)S(1)} %qkv_join_b.1.refs_4_.refs_0_), channel_id=1, source_target_pairs={{0,8},{4,12},{8,0},{12,4},{16,24},{20,28},{24,16},{28,20},{1,9},{5... | collective-permute-start | bytes 737288 | tf_op jit(solution)/shard_map/ppermute | solution.py:717
  (60 other events, 370.7 us)
Sparse Core Ops, SparseCore 0:
  11.5 58.5 all-gather.1

commit v5 on v4

--- a/solution.py
+++ b/solution.py
@@ -258,6 +258,60 @@
         (steps,),
         [pltpu.VMEM((length, d), f32)],
         "feed_forward", 0, deps,
+    )
+
+
+def begin_kernel(sc_ref, tokens_ref, queries_ref, choices_ref, code_ref, *piece_refs):
+    for mask, piece_ref in enumerate(piece_refs):
+        piece_ref[...] = tokens_ref[sc_ref[0] ^ mask]
+    d = queries_ref.shape[1]
+    choices = choices_ref[...]
+    owner = choices // PASS
+    code_ref[:, :d] = queries_ref[...]
+    code_ref[:, d : d + CH] = owner.astype(f32).astype(bf16)
+    code_ref[:, d + CH :] = (choices - owner * PASS).astype(f32).astype(bf16)
+
+
+def begin(sc, tokens, queries, choices):
+    count, d = queries.shape
+    outs = [shape(bf16, count, d + 2 * CH)] + [shape(bf16, *tokens.shape[1:])] * tokens.shape[0]
+    code, *pieces = call(
+        begin_kernel, sc, far(tokens, queries, choices), [whole(*tokens.shape), whole(count, d), whole(count, CH)],
+        outs, [whole(*o.shape) for o in outs], (1,), [], "begin", 0,
+    )
+    return pieces, code
+
+
+def pick_kernel(sc_ref, rows_ref, *piece_refs):
+    for mask, piece_ref in enumerate(piece_refs):
+        piece_ref[...] = rows_ref[sc_ref[0] ^ mask]
+
+
+def pick(sc, rows, deps):
+    outs = [shape(bf16, *rows.shape[1:])] * rows.shape[0]
+    return call(
+        pick_kernel, sc, far(rows), [whole(*rows.shape)], outs, [whole(*o.shape) for o in outs],
+        (1,), [], "pick", 0, deps,
+    )
+
+
+def halves_kernel(sc_ref, act_ref, hid_ref, ctx_ref, x_ref, out_ref):
+    rows = hid_ref.shape[1]
+    for n in range(act_ref.shape[1] // rows):
+        out_ref[0, n] = act_ref[0, n * rows : (n + 1) * rows, :]
+    for n, ref in enumerate((hid_ref, ctx_ref, x_ref)):
+        out_ref[0, act_ref.shape[1] // rows + n] = ref[0]
+
+
+def core_halves(sc, act, rest, deps):
+    block = lambda t: pl.BlockSpec((1,) + t.shape[1:], lambda i, s: (2 * i + 1 - s[1], 0, 0))
+    rows, length = rest[0].shape[1:]
+    blocks = act.shape[1] // rows + len(rest)
+    return call(
+        halves_kernel, sc, far(act, *rest), [block(t) for t in (act, *rest)],
+        shape(bf16, 2, blocks, rows, length),
+        pl.BlockSpec((1, blocks, rows, length), lambda i, s: (i, 0, 0, 0)), (2,), [],
+        "core_halves", 0, deps,
     )
 
 
@@ -351,12 +405,21 @@
 
 
 def feed_back_kernel(
-    sc_ref, gd_ref, gr_ref, wd_ref, wu_ref, slope_ref, xhat_ref, inv_ref, go_ref, wo_ref,
+    sc_ref, gd_ref, gr_ref, wd_ref, wu_ref, slope_ref, xhat_far, inv_ref, go_ref, wo_far,
     gug_ref, bup_ref, gr1_ref, gctx_ref, sums_ref,
-    acc,
+    acc, xhat_ref, wo_ref, arrived,
 ):
     step = pl.program_id(0)
     last = pl.num_programs(0) - 1
+    late = [
+        pltpu.make_async_copy(xhat_far, xhat_ref, arrived.at[0]),
+        pltpu.make_async_copy(wo_far, wo_ref, arrived.at[1]),
+    ]
+
+    @pl.when(step == 1)
+    def _():
+        for copy in late:
+            copy.start()
 
     @pl.when(step == 0)
     def _():
@@ -372,6 +435,8 @@
 
     @pl.when(step == last)
     def _():
+        for copy in late:
+            copy.wait()
         grad = acc[...]
         xhat = xhat_ref[...]
         back = norm_back(grad, xhat, inv_ref[...], go_ref[...])
@@ -397,7 +462,8 @@
             pl.BlockSpec((d, d), lambda i, s: (at(i), 0)),
             pl.BlockSpec((d, d), lambda i, s: (0, at(i))),
             pl.BlockSpec((1, length, d), lambda i, s: (at(i), 0, 0)),
-            whole(length, d), whole(length, 1), whole(1, d), whole(d, d),
+            pl.BlockSpec(memory_space=pl.ANY), whole(length, 1), whole(1, d),
+            pl.BlockSpec(memory_space=pl.ANY),
         ],
         [
             shape(bf16, steps + 1, length, d), shape(f32, steps, 1, d), shape(f32, length, d),
@@ -409,7 +475,10 @@
             whole(length, d), whole(length, d), whole(SLOT, d),
         ],
         (steps + 1,),
-        [pltpu.VMEM((length, d), f32)],
+        [
+            pltpu.VMEM((length, d), f32), pltpu.VMEM((length, d), f32), pltpu.VMEM((d, d), bf16),
+            pltpu.SemaphoreType.DMA((2,)),
+        ],
         "feed_back", 0, deps,
     )
 
@@ -698,9 +767,6 @@
             out_refs[out][pl.ds(top, rows), left * wide : (left + 1) * wide] = part[
                 n * rows : (n + 1) * rows, :
             ].astype(f32)
-    if extra:
-        small = out_refs[-1]
-        small[...] = parts[0][len(spots) * rows :, : small.shape[1]].astype(f32)
 
 
 def place(sc, parts, spots, dims, extra, name, deps=()):
@@ -774,17 +840,8 @@
     return (left.astype(f32) + right.astype(f32)).astype(bf16)
 
 
-def spread(rows):
-    own = lax.axis_index("seq")
-    count = lax.axis_size("seq")
-    assert rows.shape[0] == count
-    pieces = [
-        flip(lax.dynamic_index_in_dim(rows, own ^ mask, 0, keepdims=False), "seq", mask)
-        if mask
-        else lax.dynamic_index_in_dim(rows, own, 0, keepdims=False)
-        for mask in range(count)
-    ]
-    return jnp.concatenate(pieces, 0)
+def moved(pieces):
+    return [flip(piece, "seq", mask) if mask else piece for mask, piece in enumerate(pieces)]
 
 
 def gather_back(sc, row, count, name, deps=()):
@@ -836,14 +893,13 @@
     row = lambda v: v.reshape(1, -1)
     swap = lambda t: flip(t, "seq", 1)
 
-    x = spread(tokens)
-
-    code = jnp.concatenate(
-        [queries, (choices // PASS).astype(bf16), (choices % PASS).astype(bf16)], axis=1
-    )
+    own = own_s[None].astype(jnp.int32)
+    pieces, code = begin(own, tokens, queries, choices)
+    pieces = moved(pieces)
+    x = jnp.concatenate(pieces, 0)
     code_all = lax.all_gather(code, ("rows", "seq"), axis=0, tiled=True)
 
-    cot = spread(cotangent)
+    cot = jnp.concatenate(moved(pick(own, cotangent, (pieces[1],))), 0)
 
     q, k, v, ctxt, lse, xt, xhat_one, inv_one, hid, hidt = attention_forward(
         sc, x, w_query, w_key, w_value, row(b_query), row(b_value), w_out, row(b_out),
@@ -864,17 +920,15 @@
         pooled = jnp.concatenate([mid, flip(mid, "seq", 1)], 0)
         places = cube_place
     else:
+        near = pool
         pooled = lax.all_gather(pool, ("rows", "seq"), axis=0, tiled=True)
         pooled = jnp.roll(pooled, -own_lin * SLOT, 0)
         places = turned_place
 
-    other_half = lambda t: lax.dynamic_index_in_dim(
-        t.reshape(2, 2, -1, quarter, t.shape[-1]), 1 - core, 1, keepdims=False
-    )
+    quarters = lambda t: t.reshape(4, -1, t.shape[-1])
     halves = swap(
-        jnp.concatenate([other_half(actt), other_half(hidt), other_half(ctxt), other_half(xt)], 1)
-    )
-    quarters = lambda t: t.reshape(4, -1, t.shape[-1])
+        core_halves(wsc, quarters(actt), [quarters(t) for t in (hidt, ctxt, xt)], (near,))
+    )
 
     losses_all, gd, gr_two, sums_two = retrieval(
         sc, code_all, pooled, cot, xhat_two, inv_two, row(gain_two), piece, places, devices,
@@ -950,12 +1004,11 @@
         wsc, up_all, [(0, 0, n) for n in range(4)] + [(1, 0, 0)],
         [(quarter, ff), (quarter, d)], 0, "up_place", (qkv_sum,),
     )
-    grad_q, grad_k, grad_v, small = place(
-        wsc, qkv_all, [(n, 0, 0) for n in range(3)], [(quarter, d)] * 3 + [(EXTRA, 2 * SMALL)],
-        EXTRA, "qkv_place",
-    )
-
-    eight = small[:, :quarter]
+    grad_q, grad_k, grad_v = place(
+        wsc, qkv_all, [(n, 0, 0) for n in range(3)], [(quarter, d)] * 3, EXTRA, "qkv_place"
+    )
+
+    eight = qkv_sum[3 * quarter // 4 :, :quarter].astype(f32)
     return (
         mixed,
         query_losses,

time: 269 us -> 258 us (0.959); the launches traced: 268 us -> 254 us
  local copies, waits for them, and re-layouts: 17.2 us -> 11.4 us
  waiting for transfers between devices: 72.5 us -> 67.3 us
  other arithmetic: 3.03 us -> 0.22 us
    unnamed x78 -> x25, local copies, waits for them, and re-layouts: 11.5 us -> 2.34 us
    ppermute x46, waiting for transfers between devices: 71.6 us -> 66.1 us  [flip(): return lax.ppermute(value, axis, [(i, i ^ mask) for i in range(count)])]
    reshape x8, local copies, waits for them, and re-layouts: 0.03 us -> 5.51 us  [per_device(): row = lambda v: v.reshape(1, -1)]
    squeeze x5 -> x0, local copies, waits for them, and re-layouts: 2.96 us -> none  [the longest x3 1.61 us: per_device(): lax.dynamic_index_in_dim(t.reshape(2, 2, -1, quarter, t.shape[-1]), 1 - c...]
    pallas_call x26 -> x29, Pallas kernels: 116 us -> 117 us  [call(): pl.pallas_call(body, grid_spec=pltpu.PrefetchScalarGridSpec(num_scalar_pr...]
  transfers between devices with their start and end apart: 48 -> 48, of which waited for: 30 -> 26; matrix products, arithmetic and copies ran while one was open for 2% -> 4% of each run, Pallas kernels for 33% -> 35%
where the time goes in v5:
time: 258 us; the launch traced here: 254 us
  Pallas kernels  117 us (45%)
  waiting for transfers between devices  67.3 us (26%)
  starting transfers between devices  43.4 us (17%)
  between operations  14.5 us (6%)
  local copies, waits for them, and re-layouts  11.4 us (4%)
    pallas_call x29, Pallas kernels, call(): pl.pallas_call(body, grid_spec=pltpu.PrefetchScalarGridSpec(num_scalar_pr...  117 us
    ppermute x46, waiting for transfers between devices, flip(): return lax.ppermute(value, axis, [(i, i ^ mask) for i in range(count)])  66.1 us
    ppermute x46, starting transfers between devices, flip(): return lax.ppermute(value, axis, [(i, i ^ mask) for i in range(count)])  40.7 us
    reshape x8, local copies, waits for them, and re-layouts, per_device(): row = lambda v: v.reshape(1, -1)  5.51 us
  transfers between devices with their start and end apart: 48, of which 26 were waited for; matrix products, arithmetic and copies ran while one was open for 4% of the time, Pallas kernels for 35%

profile of v5, /device:TPU:0, one launch (start us, length us, event | category | flops | bytes accessed | tf_op | source)
XLA Modules:
  0.0 253.9 jit_solution(7065633633628129283)
XLA Ops:
  21.8 16.9 %attention_forward.1 = (bf16[512,768]{1,0:T(8,128)(2,1)}, bf16[512,768]{1,0:T(8,128)(2,1)}, bf16[512,768]{1,0:T(8,128)(2,1)}, bf16[768,512]{1,0:T(8,128)(2,1)}, ...) custom-call(s32[8]{0:T(128)S(1)} %pad_add_fusion.sc_ref, ...), custom_call_target="tpu_custom_call" | custom-call | tf_op jit(solution)/shard_map/attention_forward/pallas_call | solution.py:88
  39.5 14.3 %feed_forward.1 = (bf16[3072,512]{1,0:T(8,128)(2,1)}, bf16[4,512,768]{2,1,0:T(8,128)(2,1)}, f32[512,768]{1,0:T(8,128)}, f32[512,1]{1,0:T(8,128)}, bf16[512,768]{1,0:T(8,128)(2,1)}, /*index=5*/f32[8,768]{1,0:T(8,128)S(1)}) custom-call(s32[8]{0:T(128)S(1)} %pad_add_fusion.sc_ref, bf16[512,768]{1,0:T(8,128)(2,1)S(1)} %get-tuple-element.80.refs_0_, ...), custom_call_target="tpu_custom_call" | custom-call | tf_op jit(solution)/shard_map/feed_forward/pallas_call | solution.py:88
  63.3 2.7 %collective-permute-start.15 = (bf16[32,768]{1,0:T(8,128)(2,1)S(1)}, bf16[32,768]{1,0:T(8,128)(2,1)S(1)}, u32[]{:S(2)}, u32[]{:S(2)}) collective-permute-start(bf16[32,768]{1,0:T(8,128)(2,1)S(1)} %pad_maximum_fusion.1.refs_4_), channel_id=1, source_target_pairs={{0,16},{4,20},{8,24},{12,28},{16,0},{20,4},{24,8},{28,12},{1,17},{... | collective-permute-start | bytes 147464 | tf_op jit(solution)/shard_map/ppermute | solution.py:783
  67.6 4.6 %collective-permute-done.13 = bf16[32,768]{1,0:T(8,128)(2,1)S(1)} collective-permute-done((bf16[32,768]{1,0:T(8,128)(2,1)S(1)}, bf16[32,768]{1,0:T(8,128)(2,1)S(1)}, u32[]{:S(2)}, u32[]{:S(2)}) %collective-permute-start.13) | collective-permute-done | bytes 49184 | tf_op jit(solution)/shard_map/ppermute | solution.py:783
  73.8 13.7 %retrieval.1 = (f32[1024,1]{1,0:T(8,128)S(1)}, bf16[512,768]{1,0:T(8,128)(2,1)S(1)}, f32[512,768]{1,0:T(8,128)S(1)}, f32[8,768]{1,0:T(8,128)S(1)}) custom-call(s32[8]{0:T(128)S(1)} %pad_add_fusion.sc_ref, bf16[1024,832]{1,0:T(8,128)(2,1)} %all-gather.2.cloned.1.call-done.refs_0_, bf16[256,768]{1,0:T(8,128)(2,1)S(1)} %constant_dynamic-update-slice_fusion.11.refs_1_, ...), custom_call_target="tpu_custom_call" | custom-call | tf_op jit(solution)/shard_map/retrieval/pallas_call | solution.py:88
  89.8 11.7 %feed_back.1 = (bf16[5,512,768]{2,1,0:T(8,128)(2,1)S(1)}, f32[4,1,768]{2,1,0:T(1,128)S(1)}, f32[512,768]{1,0:T(8,128)S(1)}, bf16[512,768]{1,0:T(8,128)(2,1)S(1)}, f32[8,768]{1,0:T(8,128)S(1)}) custom-call(s32[8]{0:T(128)S(1)} %pad_add_fusion.sc_ref, bf16[512,768]{1,0:T(8,128)(2,1)S(1)} %get-tuple-element.94.refs_0_.refs_2_, ...), custom_call_target="tpu_custom_call" | custom-call | tf_op jit(solution)/shard_map/feed_back/pallas_call | solution.py:88
  101.7 3.3 %down_send.1.refs_5_ = bf16[2,384,768]{2,1,0:T(8,128)(2,1)S(1)} custom-call(s32[4]{0:T(128)S(1)} %pad_add_fusion.1.sc_ref, bf16[4,2,384,512]{3,2,1,0:T(8,128)(2,1)} %bitcast.27, bf16[2,1344,512]{2,1,0:T(8,128)(2,1)} %bitcast.23, bf16[512,768]{1,0:T(8,128)(2,1)S(1)} %get-tuple-element.94.refs_0_.refs_2_, ...), custom_call_target="tpu_custom_call" | custom-call | tf_op jit(solution)/shard_map/down_send/pallas_call | solution.py:88
  108.4 4.7 %up_send.1.refs_9_ = bf16[5,192,768]{2,1,0:T(8,128)(2,1)S(1)} custom-call(s32[4]{0:T(128)S(1)} %pad_add_fusion.1.sc_ref, bf16[4,192,512]{2,1,0:T(8,128)(2,1)} %bitcast.36, bf16[4,192,512]{2,1,0:T(8,128)(2,1)} %bitcast.33, bf16[2,7,192,512]{3,2,1,0:T(8,128)(2,1)} %copy-done.2, bf16[5,512,768]{2,1,0:T(8,128)(2,1)S(1)} %get-tuple-element.99.refs_4_.refs_3_, ...), custom_call_target="tpu_custom_call" | custom-call | tf_op jit(solution)/shard_map/up_send/pallas_call | solution.py:88
  114.0 15.8 %attention_back.1 = (bf16[512,768]{1,0:T(8,128)(2,1)S(1)}, bf16[512,768]{1,0:T(8,128)(2,1)S(1)}, bf16[512,768]{1,0:T(8,128)(2,1)S(1)}, bf16[512,768]{1,0:T(8,128)(2,1)S(1)}, f32[8,768]{1,0:T(8,128)S(1)}) custom-call(s32[8]{0:T(128)S(1)} %pad_add_fusion.sc_ref, bf16[512,768]{1,0:T(8,128)(2,1)} %get-tuple-element.100.refs_0_, ...), custom_call_target="tpu_custom_call" | custom-call | tf_op jit(solution)/shard_map/attention_back/pallas_call | solution.py:88
  135.3 2.7 %qkv_send.1.refs_5_ = bf16[592,768]{1,0:T(8,128)(2,1)S(1)} custom-call(s32[4]{0:T(128)S(1)} %pad_add_fusion.1.sc_ref, bf16[4,192,512]{2,1,0:T(8,128)(2,1)} %bitcast.30, bf16[2,7,192,512]{3,2,1,0:T(8,128)(2,1)} %copy-done.2, f32[2,16,256]{2,1,0:T(8,128)S(1)} %get-tuple-element.110.refs_2_.refs_6_, f32[2,16,256]{2,1,0:T(8,128)S(1)} %collective-permute-done.20.refs_3_, ...), custom_call_target="tpu_custom_call" | custom-call | tf_op jit(solution)/shard_map/qkv_send/pallas_call | solution.py:88
  139.2 3.7 %down_mid.1 = (bf16[2,192,768]{2,1,0:T(8,128)(2,1)S(1)}, bf16[2,192,768]{2,1,0:T(8,128)(2,1)S(1)}) custom-call(s32[4]{0:T(128)S(1)} %pad_add_fusion.1.sc_ref, bf16[4,2,384,512]{3,2,1,0:T(8,128)(2,1)} %bitcast.28, bf16[2,1344,512]{2,1,0:T(8,128)(2,1)} %bitcast.24, bf16[512,768]{1,0:T(8,128)(2,1)S(1)} %get-tuple-element.94.refs_0_.refs_2_, ...), custom_call_target="tpu_custom_call" | custom-call | flops 3449999872 | tf_op jit(solution)/shard_map/down_mid/pallas_call | solution.py:88
  143.2 5.1 %collective-permute-done.25.refs_5_ = bf16[5,192,768]{2,1,0:T(8,128)(2,1)S(1)} collective-permute-done((bf16[5,192,768]{2,1,0:T(8,128)(2,1)S(1)}, bf16[5,192,768]{2,1,0:T(8,128)(2,1)S(1)}, u32[]{:S(2)}, u32[]{:S(2)}) %collective-permute-start.25) | collective-permute-done | bytes 1474592 | tf_op jit(solution)/shard_map/ppermute | solution.py:783
  148.3 5.0 %up_keep.1 = (bf16[2,240,768]{2,1,0:T(8,128)(2,1)S(1)}, bf16[2,240,768]{2,1,0:T(8,128)(2,1)S(1)}) custom-call(s32[4]{0:T(128)S(1)} %pad_add_fusion.1.sc_ref, bf16[4,192,512]{2,1,0:T(8,128)(2,1)} %bitcast.37, bf16[4,192,512]{2,1,0:T(8,128)(2,1)} %bitcast.34, bf16[2,7,192,512]{3,2,1,0:T(8,128)(2,1)} %copy-done.2, ...), custom_call_target="tpu_custom_call" | custom-call | flops 115000000512 | tf_op jit(solution)/shard_map/up_keep/pallas_call | solution.py:88
  155.0 3.2 %collective-permute-done.24.refs_1_ = bf16[2,192,768]{2,1,0:T(8,128)(2,1)S(1)} collective-permute-done((bf16[2,192,768]{2,1,0:T(8,128)(2,1)S(1)}, bf16[2,192,768]{2,1,0:T(8,128)(2,1)S(1)}, u32[]{:S(2)}, u32[]{:S(2)}) %collective-permute-start.24) | collective-permute-done | bytes 589856 | tf_op jit(solution)/shard_map/ppermute | solution.py:783
  158.9 3.1 %collective-permute-start.26 = (bf16[2,192,768]{2,1,0:T(8,128)(2,1)S(1)}, bf16[2,192,768]{2,1,0:T(8,128)(2,1)S(1)}, u32[]{:S(2)}, u32[]{:S(2)}) collective-permute-start(bf16[2,192,768]{2,1,0:T(8,128)(2,1)S(1)} %down_join_a.1.refs_11_.refs_0_), channel_id=1, source_target_pairs={{0,24},{4,28},{8,16},{12,20},{16,8},{20,12},{24,0},{28,4},{1,25},{... | collective-permute-start | bytes 1769480 | tf_op jit(solution)/shard_map/ppermute | solution.py:783
  162.0 5.0 %collective-permute-done.28.refs_10_ = bf16[592,768]{1,0:T(8,128)(2,1)S(1)} collective-permute-done((bf16[592,768]{1,0:T(8,128)(2,1)S(1)}, bf16[592,768]{1,0:T(8,128)(2,1)S(1)}, u32[]{:S(2)}, u32[]{:S(2)}) %collective-permute-start.28) | collective-permute-done | bytes 909344 | tf_op jit(solution)/shard_map/ppermute | solution.py:783
  166.9 3.0 %qkv_keep.1 = (bf16[2,160,768]{2,1,0:T(8,128)(2,1)S(1)}, bf16[2,160,768]{2,1,0:T(8,128)(2,1)S(1)}) custom-call(s32[4]{0:T(128)S(1)} %pad_add_fusion.1.sc_ref, bf16[4,192,512]{2,1,0:T(8,128)(2,1)} %bitcast.31, bf16[2,7,192,512]{3,2,1,0:T(8,128)(2,1)} %copy-done.2, f32[2,16,256]{2,1,0:T(8,128)S(1)} %get-tuple-element.110.refs_2_.refs_6_, ...), custom_call_target="tpu_custom_call" | custom-call | tf_op jit(solution)/shard_map/qkv_keep/pallas_call | solution.py:88
  172.6 9.9 %collective-permute-done.30.refs_1_ = bf16[2,160,768]{2,1,0:T(8,128)(2,1)S(1)} collective-permute-done((bf16[2,160,768]{2,1,0:T(8,128)(2,1)S(1)}, bf16[2,160,768]{2,1,0:T(8,128)(2,1)S(1)}, u32[]{:S(2)}, u32[]{:S(2)}) %collective-permute-start.30) | collective-permute-done | bytes 491552 | tf_op jit(solution)/shard_map/ppermute | solution.py:783
  184.1 3.4 %collective-permute-start.40 = (bf16[240,768]{1,0:T(8,128)(2,1)S(1)}, bf16[240,768]{1,0:T(8,128)(2,1)S(1)}, u32[]{:S(2)}, u32[]{:S(2)}) collective-permute-start(bf16[240,768]{1,0:T(8,128)(2,1)S(1)} %up_join_a.1.refs_2_.refs_0_), channel_id=1, source_target_pairs={{0,24},{4,28},{8,16},{12,20},{16,8},{20,12},{24,0},{28,4},{1,25},{... | collective-permute-start | bytes 1105928 | tf_op jit(solution)/shard_map/ppermute | solution.py:783
  191.6 6.6 %collective-permute-done.31.refs_1_ = bf16[192,768]{1,0:T(8,128)(2,1)S(1)} collective-permute-done((bf16[192,768]{1,0:T(8,128)(2,1)S(1)}, bf16[192,768]{1,0:T(8,128)(2,1)S(1)}, u32[]{:S(2)}, u32[]{:S(2)}) %collective-permute-start.31) | collective-permute-done | bytes 294944 | tf_op jit(solution)/shard_map/ppermute | solution.py:783
  207.6 6.1 %collective-permute-done.38.refs_2_ = bf16[192,768]{1,0:T(8,128)(2,1)S(1)} collective-permute-done((bf16[192,768]{1,0:T(8,128)(2,1)S(1)}, bf16[192,768]{1,0:T(8,128)(2,1)S(1)}, u32[]{:S(2)}, u32[]{:S(2)}) %collective-permute-start.38) | collective-permute-done | bytes 294944 | tf_op jit(solution)/shard_map/ppermute | solution.py:783
  229.0 2.6 %tokens_order.1 = bf16[4,128,768]{2,1,0:T(8,128)(2,1)} custom-call(s32[8]{0:T(128)S(1)} %pad_add_fusion.sc_ref, bf16[128,768]{1,0:T(8,128)(2,1)S(1)} %get-tuple-element.139.refs_0_, bf16[128,768]{1,0:T(8,128)(2,1)} %collective-permute-done.33.refs_1_, bf16[128,768]{1,0:T(8,128)(2,1)} %collective-permute-done.34.refs_2_, ...), custom_call_target="tpu_custom_call" | custom-call | tf_op jit(solution)/shard_map/tokens_order/pallas_call | solution.py:88
  232.1 3.4 %collective-permute-done.45.refs_2_ = bf16[240,768]{1,0:T(8,128)(2,1)S(1)} collective-permute-done((bf16[240,768]{1,0:T(8,128)(2,1)S(1)}, bf16[240,768]{1,0:T(8,128)(2,1)S(1)}, u32[]{:S(2)}, u32[]{:S(2)}) %collective-permute-start.45) | collective-permute-done | bytes 368672 | tf_op jit(solution)/shard_map/ppermute | solution.py:783
  238.5 3.4 %collective-permute-done.43.refs_3_ = bf16[160,768]{1,0:T(8,128)(2,1)S(1)} collective-permute-done((bf16[160,768]{1,0:T(8,128)(2,1)S(1)}, bf16[160,768]{1,0:T(8,128)(2,1)S(1)}, u32[]{:S(2)}, u32[]{:S(2)}) %collective-permute-start.43) | collective-permute-done | bytes 245792 | tf_op jit(solution)/shard_map/ppermute | solution.py:783
  (151 shorter events, 85.6 us)
Async XLA Ops:
  7.2 66.6 %all-gather.2.cloned.1.call-start = ((), (), s32[]{:S(2)}) async-start(), calls=%async_computation | async-start | bytes 1892352 | tf_op jit(solution)/shard_map/all_gather | solution.py:900
  19.2 19.6 %collective-permute-start.3 = (bf16[128,768]{1,0:T(8,128)(2,1)S(1)}, bf16[128,768]{1,0:T(8,128)(2,1)S(1)}, u32[]{:S(2)}, u32[]{:S(2)}) collective-permute-start(bf16[128,768]{1,0:T(8,128)(2,1)S(1)} %get-tuple-element.82), channel_id=1, source_target_pairs={{0,1},{1,0},{2,3},{3,2},{4,5},{5,4},{6,7},{7,6},{8,9},{9,8},{10,11... | collective-permute-start | bytes 589832 | tf_op jit(solution)/shard_map/ppermute | solution.py:783
  19.4 19.5 %collective-permute-start.4 = (bf16[128,768]{1,0:T(8,128)(2,1)S(1)}, bf16[128,768]{1,0:T(8,128)(2,1)S(1)}, u32[]{:S(2)}, u32[]{:S(2)}) collective-permute-start(bf16[128,768]{1,0:T(8,128)(2,1)S(1)} %get-tuple-element.83), channel_id=1, source_target_pairs={{0,2},{1,3},{2,0},{3,1},{4,6},{5,7},{6,4},{7,5},{8,10},{9,11},{10,... | collective-permute-start | bytes 589832 | tf_op jit(solution)/shard_map/ppermute | solution.py:783
  21.3 17.6 %collective-permute-start.5 = (bf16[128,768]{1,0:T(8,128)(2,1)S(1)}, bf16[128,768]{1,0:T(8,128)(2,1)S(1)}, u32[]{:S(2)}, u32[]{:S(2)}) collective-permute-start(bf16[128,768]{1,0:T(8,128)(2,1)S(1)} %get-tuple-element.84), channel_id=1, source_target_pairs={{0,3},{1,2},{2,1},{3,0},{4,7},{5,6},{6,5},{7,4},{8,11},{9,10},{10,... | collective-permute-start | bytes 589832 | tf_op jit(solution)/shard_map/ppermute | solution.py:783
  105.0 34.2 %collective-permute-start.18 = (bf16[2,384,768]{2,1,0:T(8,128)(2,1)S(1)}, bf16[2,384,768]{2,1,0:T(8,128)(2,1)S(1)}, u32[]{:S(2)}, u32[]{:S(2)}) collective-permute-start(bf16[2,384,768]{2,1,0:T(8,128)(2,1)S(1)} %down_send.1.refs_5_), channel_id=1, source_target_pairs={{0,4},{4,0},{8,12},{12,8},{16,20},{20,16},{24,28},{28,24},{1,5},{5... | collective-permute-start | bytes 3538952 | tf_op jit(solution)/shard_map/ppermute | solution.py:783
  113.1 35.2 %collective-permute-start.25 = (bf16[5,192,768]{2,1,0:T(8,128)(2,1)S(1)}, bf16[5,192,768]{2,1,0:T(8,128)(2,1)S(1)}, u32[]{:S(2)}, u32[]{:S(2)}) collective-permute-start(bf16[5,192,768]{2,1,0:T(8,128)(2,1)S(1)} %up_send.1.refs_9_), channel_id=1, source_target_pairs={{0,2},{1,3},{2,0},{3,1},{4,6},{5,7},{6,4},{7,5},{8,10},{9,11},{10,... | collective-permute-start | bytes 4423688 | tf_op jit(solution)/shard_map/ppermute | solution.py:783
  138.0 28.9 %collective-permute-start.28 = (bf16[592,768]{1,0:T(8,128)(2,1)S(1)}, bf16[592,768]{1,0:T(8,128)(2,1)S(1)}, u32[]{:S(2)}, u32[]{:S(2)}) collective-permute-start(bf16[592,768]{1,0:T(8,128)(2,1)S(1)} %qkv_send.1.refs_5_), channel_id=1, source_target_pairs={{0,2},{1,3},{2,0},{3,1},{4,6},{5,7},{6,4},{7,5},{8,10},{9,11},{10,... | collective-permute-start | bytes 2727944 | tf_op jit(solution)/shard_map/ppermute | solution.py:783
  142.9 15.4 %collective-permute-start.24 = (bf16[2,192,768]{2,1,0:T(8,128)(2,1)S(1)}, bf16[2,192,768]{2,1,0:T(8,128)(2,1)S(1)}, u32[]{:S(2)}, u32[]{:S(2)}) collective-permute-start(bf16[2,192,768]{2,1,0:T(8,128)(2,1)S(1)} %get-tuple-element.116), channel_id=1, source_target_pairs={{0,8},{4,12},{8,0},{12,4},{16,24},{20,28},{24,16},{28,20},{1,9},{5... | collective-permute-start | bytes 1769480 | tf_op jit(solution)/shard_map/ppermute | solution.py:783
  153.3 18.4 %collective-permute-start.27 = (bf16[2,240,768]{2,1,0:T(8,128)(2,1)S(1)}, bf16[2,240,768]{2,1,0:T(8,128)(2,1)S(1)}, u32[]{:S(2)}, u32[]{:S(2)}) collective-permute-start(bf16[2,240,768]{2,1,0:T(8,128)(2,1)S(1)} %get-tuple-element.118), channel_id=1, source_target_pairs={{0,4},{4,0},{8,12},{12,8},{16,20},{20,16},{24,28},{28,24},{1,5},{5... | collective-permute-start | bytes 2211848 | tf_op jit(solution)/shard_map/ppermute | solution.py:783
  158.9 28.6 %collective-permute-start.26 = (bf16[2,192,768]{2,1,0:T(8,128)(2,1)S(1)}, bf16[2,192,768]{2,1,0:T(8,128)(2,1)S(1)}, u32[]{:S(2)}, u32[]{:S(2)}) collective-permute-start(bf16[2,192,768]{2,1,0:T(8,128)(2,1)S(1)} %down_join_a.1.refs_11_.refs_0_), channel_id=1, source_target_pairs={{0,24},{4,28},{8,16},{12,20},{16,8},{20,12},{24,0},{28,4},{1,25},{... | collective-permute-start | bytes 1769480 | tf_op jit(solution)/shard_map/ppermute | solution.py:783
  170.0 12.5 %collective-permute-start.30 = (bf16[2,160,768]{2,1,0:T(8,128)(2,1)S(1)}, bf16[2,160,768]{2,1,0:T(8,128)(2,1)S(1)}, u32[]{:S(2)}, u32[]{:S(2)}) collective-permute-start(bf16[2,160,768]{2,1,0:T(8,128)(2,1)S(1)} %get-tuple-element.122), channel_id=1, source_target_pairs={{0,4},{4,0},{8,12},{12,8},{16,20},{20,16},{24,28},{28,24},{1,5},{5... | collective-permute-start | bytes 1474568 | tf_op jit(solution)/shard_map/ppermute | solution.py:783
  184.1 17.5 %collective-permute-start.40 = (bf16[240,768]{1,0:T(8,128)(2,1)S(1)}, bf16[240,768]{1,0:T(8,128)(2,1)S(1)}, u32[]{:S(2)}, u32[]{:S(2)}) collective-permute-start(bf16[240,768]{1,0:T(8,128)(2,1)S(1)} %up_join_a.1.refs_2_.refs_0_), channel_id=1, source_target_pairs={{0,24},{4,28},{8,16},{12,20},{16,8},{20,12},{24,0},{28,4},{1,25},{... | collective-permute-start | bytes 1105928 | tf_op jit(solution)/shard_map/ppermute | solution.py:783
  189.1 14.8 %collective-permute-start.7 = (bf16[128,768]{1,0:T(8,128)(2,1)S(1)}, bf16[128,768]{1,0:T(8,128)(2,1)S(1)}, u32[]{:S(2)}, u32[]{:S(2)}) collective-permute-start(bf16[128,768]{1,0:T(8,128)(2,1)S(1)} %get-tuple-element.141), channel_id=1, source_target_pairs={{0,2},{1,3},{2,0},{3,1},{4,6},{5,7},{6,4},{7,5},{8,10},{9,11},{10,... | collective-permute-start | bytes 589832 | tf_op jit(solution)/shard_map/ppermute | solution.py:783
  190.5 15.6 %collective-permute-start.6 = (bf16[128,768]{1,0:T(8,128)(2,1)S(1)}, bf16[128,768]{1,0:T(8,128)(2,1)S(1)}, u32[]{:S(2)}, u32[]{:S(2)}) collective-permute-start(bf16[128,768]{1,0:T(8,128)(2,1)S(1)} %get-tuple-element.142), channel_id=1, source_target_pairs={{0,1},{1,0},{2,3},{3,2},{4,5},{5,4},{6,7},{7,6},{8,9},{9,8},{10,11... | collective-permute-start | bytes 589832 | tf_op jit(solution)/shard_map/ppermute | solution.py:783
  200.1 13.6 %collective-permute-start.38 = (bf16[192,768]{1,0:T(8,128)(2,1)S(1)}, bf16[192,768]{1,0:T(8,128)(2,1)S(1)}, u32[]{:S(2)}, u32[]{:S(2)}) collective-permute-start(bf16[192,768]{1,0:T(8,128)(2,1)S(1)} %down_join_x.1.refs_4_.refs_2_.refs_0_), channel_id=1, source_target_pairs={{0,4},{4,0},{8,12},{12,8},{16,20},{20,16},{24,28},{28,24},{1,5},{5... | collective-permute-start | bytes 884744 | tf_op jit(solution)/shard_map/ppermute | solution.py:783
  201.6 13.0 %collective-permute-start.37 = (bf16[192,768]{1,0:T(8,128)(2,1)S(1)}, bf16[192,768]{1,0:T(8,128)(2,1)S(1)}, u32[]{:S(2)}, u32[]{:S(2)}) collective-permute-start(bf16[192,768]{1,0:T(8,128)(2,1)S(1)} %down_join_x.1.refs_4_.refs_2_.refs_0_), channel_id=1, source_target_pairs={{0,8},{4,12},{8,0},{12,4},{16,24},{20,28},{24,16},{28,20},{1,9},{5... | collective-permute-start | bytes 884744 | tf_op jit(solution)/shard_map/ppermute | solution.py:783
  204.0 17.3 %collective-permute-start.36 = (bf16[160,768]{1,0:T(8,128)(2,1)S(1)}, bf16[160,768]{1,0:T(8,128)(2,1)S(1)}, u32[]{:S(2)}, u32[]{:S(2)}) collective-permute-start(bf16[160,768]{1,0:T(8,128)(2,1)S(1)} %qkv_join_a.1.refs_2_.refs_0_), channel_id=1, source_target_pairs={{0,24},{4,28},{8,16},{12,20},{16,8},{20,12},{24,0},{28,4},{1,25},{... | collective-permute-start | bytes 737288 | tf_op jit(solution)/shard_map/ppermute | solution.py:783
  206.2 22.0 %collective-permute-start.46 = (bf16[240,768]{1,0:T(8,128)(2,1)S(1)}, bf16[240,768]{1,0:T(8,128)(2,1)S(1)}, u32[]{:S(2)}, u32[]{:S(2)}) collective-permute-start(bf16[240,768]{1,0:T(8,128)(2,1)S(1)} %up_join_b.1.refs_4_.refs_0_), channel_id=1, source_target_pairs={{0,12},{4,8},{8,4},{12,0},{16,28},{20,24},{24,20},{28,16},{1,13},{... | collective-permute-start | bytes 1105928 | tf_op jit(solution)/shard_map/ppermute | solution.py:783
  207.6 17.0 %collective-permute-start.35 = (bf16[128,768]{1,0:T(8,128)(2,1)}, bf16[128,768]{1,0:T(8,128)(2,1)}, u32[]{:S(2)}, u32[]{:S(2)}) collective-permute-start(bf16[128,768]{1,0:T(8,128)(2,1)} %get-tuple-element.136), channel_id=1, source_target_pairs={{0,3},{1,2},{2,1},{3,0},{4,7},{5,6},{6,5},{7,4},{8,11},{9,10},{10,... | collective-permute-start | bytes 589832 | tf_op jit(solution)/shard_map/ppermute | solution.py:783
  214.6 12.5 %collective-permute-start.33 = (bf16[128,768]{1,0:T(8,128)(2,1)}, bf16[128,768]{1,0:T(8,128)(2,1)}, u32[]{:S(2)}, u32[]{:S(2)}) collective-permute-start(bf16[128,768]{1,0:T(8,128)(2,1)} %get-tuple-element.138), channel_id=1, source_target_pairs={{0,1},{1,0},{2,3},{3,2},{4,5},{5,4},{6,7},{7,6},{8,9},{9,8},{10,11... | collective-permute-start | bytes 589832 | tf_op jit(solution)/shard_map/ppermute | solution.py:783
  221.3 14.3 %collective-permute-start.45 = (bf16[240,768]{1,0:T(8,128)(2,1)S(1)}, bf16[240,768]{1,0:T(8,128)(2,1)S(1)}, u32[]{:S(2)}, u32[]{:S(2)}) collective-permute-start(bf16[240,768]{1,0:T(8,128)(2,1)S(1)} %up_join_b.1.refs_4_.refs_0_), channel_id=1, source_target_pairs={{0,4},{4,0},{8,12},{12,8},{16,20},{20,16},{24,28},{28,24},{1,5},{5... | collective-permute-start | bytes 1105928 | tf_op jit(solution)/shard_map/ppermute | solution.py:783
  224.7 17.2 %collective-permute-start.43 = (bf16[160,768]{1,0:T(8,128)(2,1)S(1)}, bf16[160,768]{1,0:T(8,128)(2,1)S(1)}, u32[]{:S(2)}, u32[]{:S(2)}) collective-permute-start(bf16[160,768]{1,0:T(8,128)(2,1)S(1)} %qkv_join_b.1.refs_4_.refs_0_), channel_id=1, source_target_pairs={{0,12},{4,8},{8,4},{12,0},{16,28},{20,24},{24,20},{28,16},{1,13},{... | collective-permute-start | bytes 737288 | tf_op jit(solution)/shard_map/ppermute | solution.py:783
  227.1 17.3 %collective-permute-start.42 = (bf16[160,768]{1,0:T(8,128)(2,1)S(1)}, bf16[160,768]{1,0:T(8,128)(2,1)S(1)}, u32[]{:S(2)}, u32[]{:S(2)}) collective-permute-start(bf16[160,768]{1,0:T(8,128)(2,1)S(1)} %qkv_join_b.1.refs_4_.refs_0_), channel_id=1, source_target_pairs={{0,4},{4,0},{8,12},{12,8},{16,20},{20,16},{24,28},{28,24},{1,5},{5... | collective-permute-start | bytes 737288 | tf_op jit(solution)/shard_map/ppermute | solution.py:783
  228.2 17.0 %collective-permute-start.41 = (bf16[160,768]{1,0:T(8,128)(2,1)S(1)}, bf16[160,768]{1,0:T(8,128)(2,1)S(1)}, u32[]{:S(2)}, u32[]{:S(2)}) collective-permute-start(bf16[160,768]{1,0:T(8,128)(2,1)S(1)} %qkv_join_b.1.refs_4_.refs_0_), channel_id=1, source_target_pairs={{0,8},{4,12},{8,0},{12,4},{16,24},{20,28},{24,16},{28,20},{1,9},{5... | collective-permute-start | bytes 737288 | tf_op jit(solution)/shard_map/ppermute | solution.py:783
  (32 other events, 244.1 us)
Sparse Core Ops, SparseCore 0:
  11.4 59.9 all-gather.1

commit v6 on v5

--- a/solution.py
+++ b/solution.py
@@ -13,7 +13,7 @@
 CH = 32
 SLOT = 8
 GROUP = 4
-SUB = 384
+SUB = 768
 SCALE = HEAD ** (-0.5)
 
 norm_eps = 1e-05
@@ -381,7 +381,7 @@
 def retrieval(sc, code_all, pooled, cot, xhat, inv, gain, piece, places, devices, deps):
     count, width = code_all.shape
     length, d = cot.shape
-    block = 256
+    block = 512 if pooled.shape[0] <= 512 else 256
     steps, pieces = count // block, length // piece
     first = lambda i: jnp.minimum(i, steps - 1)
     second = lambda i: jnp.maximum(i - steps, 0)

time: 258 us -> 255 us (0.988)
  no operation moved by 1% of the time
where the time goes in v6:
time: 255 us; the launch traced here: 251 us
  Pallas kernels  115 us (45%)
  waiting for transfers between devices  67.1 us (26%)
  starting transfers between devices  43 us (17%)
  between operations  14.5 us (6%)
  local copies, waits for them, and re-layouts  11.4 us (4%)
    pallas_call x29, Pallas kernels, call(): pl.pallas_call(body, grid_spec=pltpu.PrefetchScalarGridSpec(num_scalar_pr...  115 us
    ppermute x46, waiting for transfers between devices, flip(): return lax.ppermute(value, axis, [(i, i ^ mask) for i in range(count)])  66.1 us
    ppermute x46, starting transfers between devices, flip(): return lax.ppermute(value, axis, [(i, i ^ mask) for i in range(count)])  40.4 us
    reshape x8, local copies, waits for them, and re-layouts, per_device(): row = lambda v: v.reshape(1, -1)  5.51 us
  transfers between devices with their start and end apart: 48, of which 26 were waited for; matrix products, arithmetic and copies ran while one was open for 4% of the time, Pallas kernels for 35%

profile of v6, /device:TPU:0, one launch (start us, length us, event | category | flops | bytes accessed | tf_op | source)
XLA Modules:
  0.0 251.4 jit_solution(11377254438763319887)
XLA Ops:
  21.8 16.9 %attention_forward.1 = (bf16[512,768]{1,0:T(8,128)(2,1)}, bf16[512,768]{1,0:T(8,128)(2,1)}, bf16[512,768]{1,0:T(8,128)(2,1)}, bf16[768,512]{1,0:T(8,128)(2,1)}, ...) custom-call(s32[8]{0:T(128)S(1)} %pad_add_fusion.sc_ref, ...), custom_call_target="tpu_custom_call" | custom-call | tf_op jit(solution)/shard_map/attention_forward/pallas_call | solution.py:88
  39.5 13.0 %feed_forward.1 = (bf16[3072,512]{1,0:T(8,128)(2,1)}, bf16[4,512,768]{2,1,0:T(8,128)(2,1)}, f32[512,768]{1,0:T(8,128)}, f32[512,1]{1,0:T(8,128)}, bf16[512,768]{1,0:T(8,128)(2,1)}, /*index=5*/f32[8,768]{1,0:T(8,128)S(1)}) custom-call(s32[8]{0:T(128)S(1)} %pad_add_fusion.sc_ref, bf16[512,768]{1,0:T(8,128)(2,1)S(1)} %get-tuple-element.80.refs_0_, ...), custom_call_target="tpu_custom_call" | custom-call | tf_op jit(solution)/shard_map/feed_forward/pallas_call | solution.py:88
  62.0 2.7 %collective-permute-start.15 = (bf16[32,768]{1,0:T(8,128)(2,1)S(1)}, bf16[32,768]{1,0:T(8,128)(2,1)S(1)}, u32[]{:S(2)}, u32[]{:S(2)}) collective-permute-start(bf16[32,768]{1,0:T(8,128)(2,1)S(1)} %pad_maximum_fusion.1.refs_4_), channel_id=1, source_target_pairs={{0,16},{4,20},{8,24},{12,28},{16,0},{20,4},{24,8},{28,12},{1,17},{... | collective-permute-start | bytes 147464 | tf_op jit(solution)/shard_map/ppermute | solution.py:783
  66.3 4.9 %collective-permute-done.13 = bf16[32,768]{1,0:T(8,128)(2,1)S(1)} collective-permute-done((bf16[32,768]{1,0:T(8,128)(2,1)S(1)}, bf16[32,768]{1,0:T(8,128)(2,1)S(1)}, u32[]{:S(2)}, u32[]{:S(2)}) %collective-permute-start.13) | collective-permute-done | bytes 49184 | tf_op jit(solution)/shard_map/ppermute | solution.py:783
  72.8 12.7 %retrieval.1 = (f32[1024,1]{1,0:T(8,128)S(1)}, bf16[512,768]{1,0:T(8,128)(2,1)S(1)}, f32[512,768]{1,0:T(8,128)S(1)}, f32[8,768]{1,0:T(8,128)S(1)}) custom-call(s32[8]{0:T(128)S(1)} %pad_add_fusion.sc_ref, bf16[1024,832]{1,0:T(8,128)(2,1)} %all-gather.2.cloned.1.call-done.refs_0_, bf16[256,768]{1,0:T(8,128)(2,1)S(1)} %constant_dynamic-update-slice_fusion.11.refs_1_, ...), custom_call_target="tpu_custom_call" | custom-call | tf_op jit(solution)/shard_map/retrieval/pallas_call | solution.py:88
  87.9 11.5 %feed_back.1 = (bf16[5,512,768]{2,1,0:T(8,128)(2,1)S(1)}, f32[4,1,768]{2,1,0:T(1,128)S(1)}, f32[512,768]{1,0:T(8,128)S(1)}, bf16[512,768]{1,0:T(8,128)(2,1)S(1)}, f32[8,768]{1,0:T(8,128)S(1)}) custom-call(s32[8]{0:T(128)S(1)} %pad_add_fusion.sc_ref, bf16[512,768]{1,0:T(8,128)(2,1)S(1)} %get-tuple-element.94.refs_0_.refs_2_, ...), custom_call_target="tpu_custom_call" | custom-call | tf_op jit(solution)/shard_map/feed_back/pallas_call | solution.py:88
  99.7 3.3 %down_send.1.refs_5_ = bf16[2,384,768]{2,1,0:T(8,128)(2,1)S(1)} custom-call(s32[4]{0:T(128)S(1)} %pad_add_fusion.1.sc_ref, bf16[4,2,384,512]{3,2,1,0:T(8,128)(2,1)} %bitcast.27, bf16[2,1344,512]{2,1,0:T(8,128)(2,1)} %bitcast.23, bf16[512,768]{1,0:T(8,128)(2,1)S(1)} %get-tuple-element.94.refs_0_.refs_2_, ...), custom_call_target="tpu_custom_call" | custom-call | tf_op jit(solution)/shard_map/down_send/pallas_call | solution.py:88
  106.3 4.7 %up_send.1.refs_9_ = bf16[5,192,768]{2,1,0:T(8,128)(2,1)S(1)} custom-call(s32[4]{0:T(128)S(1)} %pad_add_fusion.1.sc_ref, bf16[4,192,512]{2,1,0:T(8,128)(2,1)} %bitcast.36, bf16[4,192,512]{2,1,0:T(8,128)(2,1)} %bitcast.33, bf16[2,7,192,512]{3,2,1,0:T(8,128)(2,1)} %copy-done.2, bf16[5,512,768]{2,1,0:T(8,128)(2,1)S(1)} %get-tuple-element.99.refs_4_.refs_3_, ...), custom_call_target="tpu_custom_call" | custom-call | tf_op jit(solution)/shard_map/up_send/pallas_call | solution.py:88
  111.9 16.0 %attention_back.1 = (bf16[512,768]{1,0:T(8,128)(2,1)S(1)}, bf16[512,768]{1,0:T(8,128)(2,1)S(1)}, bf16[512,768]{1,0:T(8,128)(2,1)S(1)}, bf16[512,768]{1,0:T(8,128)(2,1)S(1)}, f32[8,768]{1,0:T(8,128)S(1)}) custom-call(s32[8]{0:T(128)S(1)} %pad_add_fusion.sc_ref, bf16[512,768]{1,0:T(8,128)(2,1)} %get-tuple-element.100.refs_0_, ...), custom_call_target="tpu_custom_call" | custom-call | tf_op jit(solution)/shard_map/attention_back/pallas_call | solution.py:88
  133.4 2.7 %qkv_send.1.refs_5_ = bf16[592,768]{1,0:T(8,128)(2,1)S(1)} custom-call(s32[4]{0:T(128)S(1)} %pad_add_fusion.1.sc_ref, bf16[4,192,512]{2,1,0:T(8,128)(2,1)} %bitcast.30, bf16[2,7,192,512]{3,2,1,0:T(8,128)(2,1)} %copy-done.2, f32[2,16,256]{2,1,0:T(8,128)S(1)} %get-tuple-element.110.refs_2_.refs_6_, f32[2,16,256]{2,1,0:T(8,128)S(1)} %collective-permute-done.20.refs_3_, ...), custom_call_target="tpu_custom_call" | custom-call | tf_op jit(solution)/shard_map/qkv_send/pallas_call | solution.py:88
  137.3 3.4 %down_mid.1 = (bf16[2,192,768]{2,1,0:T(8,128)(2,1)S(1)}, bf16[2,192,768]{2,1,0:T(8,128)(2,1)S(1)}) custom-call(s32[4]{0:T(128)S(1)} %pad_add_fusion.1.sc_ref, bf16[4,2,384,512]{3,2,1,0:T(8,128)(2,1)} %bitcast.28, bf16[2,1344,512]{2,1,0:T(8,128)(2,1)} %bitcast.24, bf16[512,768]{1,0:T(8,128)(2,1)S(1)} %get-tuple-element.94.refs_0_.refs_2_, ...), custom_call_target="tpu_custom_call" | custom-call | flops 3449999872 | tf_op jit(solution)/shard_map/down_mid/pallas_call | solution.py:88
  141.6 4.6 %collective-permute-done.25.refs_5_ = bf16[5,192,768]{2,1,0:T(8,128)(2,1)S(1)} collective-permute-done((bf16[5,192,768]{2,1,0:T(8,128)(2,1)S(1)}, bf16[5,192,768]{2,1,0:T(8,128)(2,1)S(1)}, u32[]{:S(2)}, u32[]{:S(2)}) %collective-permute-start.25) | collective-permute-done | bytes 1474592 | tf_op jit(solution)/shard_map/ppermute | solution.py:783
  146.2 5.0 %up_keep.1 = (bf16[2,240,768]{2,1,0:T(8,128)(2,1)S(1)}, bf16[2,240,768]{2,1,0:T(8,128)(2,1)S(1)}) custom-call(s32[4]{0:T(128)S(1)} %pad_add_fusion.1.sc_ref, bf16[4,192,512]{2,1,0:T(8,128)(2,1)} %bitcast.37, bf16[4,192,512]{2,1,0:T(8,128)(2,1)} %bitcast.34, bf16[2,7,192,512]{3,2,1,0:T(8,128)(2,1)} %copy-done.2, ...), custom_call_target="tpu_custom_call" | custom-call | flops 115000000512 | tf_op jit(solution)/shard_map/up_keep/pallas_call | solution.py:88
  152.9 3.2 %collective-permute-done.24.refs_1_ = bf16[2,192,768]{2,1,0:T(8,128)(2,1)S(1)} collective-permute-done((bf16[2,192,768]{2,1,0:T(8,128)(2,1)S(1)}, bf16[2,192,768]{2,1,0:T(8,128)(2,1)S(1)}, u32[]{:S(2)}, u32[]{:S(2)}) %collective-permute-start.24) | collective-permute-done | bytes 589856 | tf_op jit(solution)/shard_map/ppermute | solution.py:783
  156.9 2.9 %collective-permute-start.26 = (bf16[2,192,768]{2,1,0:T(8,128)(2,1)S(1)}, bf16[2,192,768]{2,1,0:T(8,128)(2,1)S(1)}, u32[]{:S(2)}, u32[]{:S(2)}) collective-permute-start(bf16[2,192,768]{2,1,0:T(8,128)(2,1)S(1)} %down_join_a.1.refs_11_.refs_0_), channel_id=1, source_target_pairs={{0,24},{4,28},{8,16},{12,20},{16,8},{20,12},{24,0},{28,4},{1,25},{... | collective-permute-start | bytes 1769480 | tf_op jit(solution)/shard_map/ppermute | solution.py:783
  159.7 5.2 %collective-permute-done.28.refs_10_ = bf16[592,768]{1,0:T(8,128)(2,1)S(1)} collective-permute-done((bf16[592,768]{1,0:T(8,128)(2,1)S(1)}, bf16[592,768]{1,0:T(8,128)(2,1)S(1)}, u32[]{:S(2)}, u32[]{:S(2)}) %collective-permute-start.28) | collective-permute-done | bytes 909344 | tf_op jit(solution)/shard_map/ppermute | solution.py:783
  164.9 3.3 %qkv_keep.1 = (bf16[2,160,768]{2,1,0:T(8,128)(2,1)S(1)}, bf16[2,160,768]{2,1,0:T(8,128)(2,1)S(1)}) custom-call(s32[4]{0:T(128)S(1)} %pad_add_fusion.1.sc_ref, bf16[4,192,512]{2,1,0:T(8,128)(2,1)} %bitcast.31, bf16[2,7,192,512]{3,2,1,0:T(8,128)(2,1)} %copy-done.2, f32[2,16,256]{2,1,0:T(8,128)S(1)} %get-tuple-element.110.refs_2_.refs_6_, ...), custom_call_target="tpu_custom_call" | custom-call | tf_op jit(solution)/shard_map/qkv_keep/pallas_call | solution.py:88
  171.3 9.4 %collective-permute-done.30.refs_1_ = bf16[2,160,768]{2,1,0:T(8,128)(2,1)S(1)} collective-permute-done((bf16[2,160,768]{2,1,0:T(8,128)(2,1)S(1)}, bf16[2,160,768]{2,1,0:T(8,128)(2,1)S(1)}, u32[]{:S(2)}, u32[]{:S(2)}) %collective-permute-start.30) | collective-permute-done | bytes 491552 | tf_op jit(solution)/shard_map/ppermute | solution.py:783
  182.9 2.7 %collective-permute-start.40 = (bf16[240,768]{1,0:T(8,128)(2,1)S(1)}, bf16[240,768]{1,0:T(8,128)(2,1)S(1)}, u32[]{:S(2)}, u32[]{:S(2)}) collective-permute-start(bf16[240,768]{1,0:T(8,128)(2,1)S(1)} %up_join_a.1.refs_2_.refs_0_), channel_id=1, source_target_pairs={{0,24},{4,28},{8,16},{12,20},{16,8},{20,12},{24,0},{28,4},{1,25},{... | collective-permute-start | bytes 1105928 | tf_op jit(solution)/shard_map/ppermute | solution.py:783
  189.7 6.5 %collective-permute-done.31.refs_1_ = bf16[192,768]{1,0:T(8,128)(2,1)S(1)} collective-permute-done((bf16[192,768]{1,0:T(8,128)(2,1)S(1)}, bf16[192,768]{1,0:T(8,128)(2,1)S(1)}, u32[]{:S(2)}, u32[]{:S(2)}) %collective-permute-start.31) | collective-permute-done | bytes 294944 | tf_op jit(solution)/shard_map/ppermute | solution.py:783
  205.8 6.3 %collective-permute-done.38.refs_2_ = bf16[192,768]{1,0:T(8,128)(2,1)S(1)} collective-permute-done((bf16[192,768]{1,0:T(8,128)(2,1)S(1)}, bf16[192,768]{1,0:T(8,128)(2,1)S(1)}, u32[]{:S(2)}, u32[]{:S(2)}) %collective-permute-start.38) | collective-permute-done | bytes 294944 | tf_op jit(solution)/shard_map/ppermute | solution.py:783
  222.2 2.9 %collective-permute-start.43 = (bf16[160,768]{1,0:T(8,128)(2,1)S(1)}, bf16[160,768]{1,0:T(8,128)(2,1)S(1)}, u32[]{:S(2)}, u32[]{:S(2)}) collective-permute-start(bf16[160,768]{1,0:T(8,128)(2,1)S(1)} %qkv_join_b.1.refs_4_.refs_0_), channel_id=1, source_target_pairs={{0,12},{4,8},{8,4},{12,0},{16,28},{20,24},{24,20},{28,16},{1,13},{... | collective-permute-start | bytes 737288 | tf_op jit(solution)/shard_map/ppermute | solution.py:783
  229.6 5.0 %collective-permute-done.45.refs_2_ = bf16[240,768]{1,0:T(8,128)(2,1)S(1)} collective-permute-done((bf16[240,768]{1,0:T(8,128)(2,1)S(1)}, bf16[240,768]{1,0:T(8,128)(2,1)S(1)}, u32[]{:S(2)}, u32[]{:S(2)}) %collective-permute-start.45) | collective-permute-done | bytes 368672 | tf_op jit(solution)/shard_map/ppermute | solution.py:783
  236.9 2.9 %collective-permute-done.43.refs_3_ = bf16[160,768]{1,0:T(8,128)(2,1)S(1)} collective-permute-done((bf16[160,768]{1,0:T(8,128)(2,1)S(1)}, bf16[160,768]{1,0:T(8,128)(2,1)S(1)}, u32[]{:S(2)}, u32[]{:S(2)}) %collective-permute-start.43) | collective-permute-done | bytes 245792 | tf_op jit(solution)/shard_map/ppermute | solution.py:783
  (151 shorter events, 85.2 us)
Async XLA Ops:
  7.2 65.6 %all-gather.2.cloned.1.call-start = ((), (), s32[]{:S(2)}) async-start(), calls=%async_computation | async-start | bytes 1892352 | tf_op jit(solution)/shard_map/all_gather | solution.py:900
  19.2 19.6 %collective-permute-start.3 = (bf16[128,768]{1,0:T(8,128)(2,1)S(1)}, bf16[128,768]{1,0:T(8,128)(2,1)S(1)}, u32[]{:S(2)}, u32[]{:S(2)}) collective-permute-start(bf16[128,768]{1,0:T(8,128)(2,1)S(1)} %get-tuple-element.82), channel_id=1, source_target_pairs={{0,1},{1,0},{2,3},{3,2},{4,5},{5,4},{6,7},{7,6},{8,9},{9,8},{10,11... | collective-permute-start | bytes 589832 | tf_op jit(solution)/shard_map/ppermute | solution.py:783
  19.4 19.5 %collective-permute-start.4 = (bf16[128,768]{1,0:T(8,128)(2,1)S(1)}, bf16[128,768]{1,0:T(8,128)(2,1)S(1)}, u32[]{:S(2)}, u32[]{:S(2)}) collective-permute-start(bf16[128,768]{1,0:T(8,128)(2,1)S(1)} %get-tuple-element.83), channel_id=1, source_target_pairs={{0,2},{1,3},{2,0},{3,1},{4,6},{5,7},{6,4},{7,5},{8,10},{9,11},{10,... | collective-permute-start | bytes 589832 | tf_op jit(solution)/shard_map/ppermute | solution.py:783
  21.3 17.6 %collective-permute-start.5 = (bf16[128,768]{1,0:T(8,128)(2,1)S(1)}, bf16[128,768]{1,0:T(8,128)(2,1)S(1)}, u32[]{:S(2)}, u32[]{:S(2)}) collective-permute-start(bf16[128,768]{1,0:T(8,128)(2,1)S(1)} %get-tuple-element.84), channel_id=1, source_target_pairs={{0,3},{1,2},{2,1},{3,0},{4,7},{5,6},{6,5},{7,4},{8,11},{9,10},{10,... | collective-permute-start | bytes 589832 | tf_op jit(solution)/shard_map/ppermute | solution.py:783
  102.9 34.4 %collective-permute-start.18 = (bf16[2,384,768]{2,1,0:T(8,128)(2,1)S(1)}, bf16[2,384,768]{2,1,0:T(8,128)(2,1)S(1)}, u32[]{:S(2)}, u32[]{:S(2)}) collective-permute-start(bf16[2,384,768]{2,1,0:T(8,128)(2,1)S(1)} %down_send.1.refs_5_), channel_id=1, source_target_pairs={{0,4},{4,0},{8,12},{12,8},{16,20},{20,16},{24,28},{28,24},{1,5},{5... | collective-permute-start | bytes 3538952 | tf_op jit(solution)/shard_map/ppermute | solution.py:783
  111.0 35.2 %collective-permute-start.25 = (bf16[5,192,768]{2,1,0:T(8,128)(2,1)S(1)}, bf16[5,192,768]{2,1,0:T(8,128)(2,1)S(1)}, u32[]{:S(2)}, u32[]{:S(2)}) collective-permute-start(bf16[5,192,768]{2,1,0:T(8,128)(2,1)S(1)} %up_send.1.refs_9_), channel_id=1, source_target_pairs={{0,2},{1,3},{2,0},{3,1},{4,6},{5,7},{6,4},{7,5},{8,10},{9,11},{10,... | collective-permute-start | bytes 4423688 | tf_op jit(solution)/shard_map/ppermute | solution.py:783
  136.1 28.8 %collective-permute-start.28 = (bf16[592,768]{1,0:T(8,128)(2,1)S(1)}, bf16[592,768]{1,0:T(8,128)(2,1)S(1)}, u32[]{:S(2)}, u32[]{:S(2)}) collective-permute-start(bf16[592,768]{1,0:T(8,128)(2,1)S(1)} %qkv_send.1.refs_5_), channel_id=1, source_target_pairs={{0,2},{1,3},{2,0},{3,1},{4,6},{5,7},{6,4},{7,5},{8,10},{9,11},{10,... | collective-permute-start | bytes 2727944 | tf_op jit(solution)/shard_map/ppermute | solution.py:783
  140.8 15.4 %collective-permute-start.24 = (bf16[2,192,768]{2,1,0:T(8,128)(2,1)S(1)}, bf16[2,192,768]{2,1,0:T(8,128)(2,1)S(1)}, u32[]{:S(2)}, u32[]{:S(2)}) collective-permute-start(bf16[2,192,768]{2,1,0:T(8,128)(2,1)S(1)} %get-tuple-element.116), channel_id=1, source_target_pairs={{0,8},{4,12},{8,0},{12,4},{16,24},{20,28},{24,16},{28,20},{1,9},{5... | collective-permute-start | bytes 1769480 | tf_op jit(solution)/shard_map/ppermute | solution.py:783
  151.2 18.7 %collective-permute-start.27 = (bf16[2,240,768]{2,1,0:T(8,128)(2,1)S(1)}, bf16[2,240,768]{2,1,0:T(8,128)(2,1)S(1)}, u32[]{:S(2)}, u32[]{:S(2)}) collective-permute-start(bf16[2,240,768]{2,1,0:T(8,128)(2,1)S(1)} %get-tuple-element.118), channel_id=1, source_target_pairs={{0,4},{4,0},{8,12},{12,8},{16,20},{20,16},{24,28},{28,24},{1,5},{5... | collective-permute-start | bytes 2211848 | tf_op jit(solution)/shard_map/ppermute | solution.py:783
  156.9 28.7 %collective-permute-start.26 = (bf16[2,192,768]{2,1,0:T(8,128)(2,1)S(1)}, bf16[2,192,768]{2,1,0:T(8,128)(2,1)S(1)}, u32[]{:S(2)}, u32[]{:S(2)}) collective-permute-start(bf16[2,192,768]{2,1,0:T(8,128)(2,1)S(1)} %down_join_a.1.refs_11_.refs_0_), channel_id=1, source_target_pairs={{0,24},{4,28},{8,16},{12,20},{16,8},{20,12},{24,0},{28,4},{1,25},{... | collective-permute-start | bytes 1769480 | tf_op jit(solution)/shard_map/ppermute | solution.py:783
  182.9 16.4 %collective-permute-start.40 = (bf16[240,768]{1,0:T(8,128)(2,1)S(1)}, bf16[240,768]{1,0:T(8,128)(2,1)S(1)}, u32[]{:S(2)}, u32[]{:S(2)}) collective-permute-start(bf16[240,768]{1,0:T(8,128)(2,1)S(1)} %up_join_a.1.refs_2_.refs_0_), channel_id=1, source_target_pairs={{0,24},{4,28},{8,16},{12,20},{16,8},{20,12},{24,0},{28,4},{1,25},{... | collective-permute-start | bytes 1105928 | tf_op jit(solution)/shard_map/ppermute | solution.py:783
  187.3 14.4 %collective-permute-start.7 = (bf16[128,768]{1,0:T(8,128)(2,1)S(1)}, bf16[128,768]{1,0:T(8,128)(2,1)S(1)}, u32[]{:S(2)}, u32[]{:S(2)}) collective-permute-start(bf16[128,768]{1,0:T(8,128)(2,1)S(1)} %get-tuple-element.141), channel_id=1, source_target_pairs={{0,2},{1,3},{2,0},{3,1},{4,6},{5,7},{6,4},{7,5},{8,10},{9,11},{10,... | collective-permute-start | bytes 589832 | tf_op jit(solution)/shard_map/ppermute | solution.py:783
  189.0 15.2 %collective-permute-start.6 = (bf16[128,768]{1,0:T(8,128)(2,1)S(1)}, bf16[128,768]{1,0:T(8,128)(2,1)S(1)}, u32[]{:S(2)}, u32[]{:S(2)}) collective-permute-start(bf16[128,768]{1,0:T(8,128)(2,1)S(1)} %get-tuple-element.142), channel_id=1, source_target_pairs={{0,1},{1,0},{2,3},{3,2},{4,5},{5,4},{6,7},{7,6},{8,9},{9,8},{10,11... | collective-permute-start | bytes 589832 | tf_op jit(solution)/shard_map/ppermute | solution.py:783
  198.3 13.9 %collective-permute-start.38 = (bf16[192,768]{1,0:T(8,128)(2,1)S(1)}, bf16[192,768]{1,0:T(8,128)(2,1)S(1)}, u32[]{:S(2)}, u32[]{:S(2)}) collective-permute-start(bf16[192,768]{1,0:T(8,128)(2,1)S(1)} %down_join_x.1.refs_4_.refs_2_.refs_0_), channel_id=1, source_target_pairs={{0,4},{4,0},{8,12},{12,8},{16,20},{20,16},{24,28},{28,24},{1,5},{5... | collective-permute-start | bytes 884744 | tf_op jit(solution)/shard_map/ppermute | solution.py:783
  199.3 13.1 %collective-permute-start.37 = (bf16[192,768]{1,0:T(8,128)(2,1)S(1)}, bf16[192,768]{1,0:T(8,128)(2,1)S(1)}, u32[]{:S(2)}, u32[]{:S(2)}) collective-permute-start(bf16[192,768]{1,0:T(8,128)(2,1)S(1)} %down_join_x.1.refs_4_.refs_2_.refs_0_), channel_id=1, source_target_pairs={{0,8},{4,12},{8,0},{12,4},{16,24},{20,28},{24,16},{28,20},{1,9},{5... | collective-permute-start | bytes 884744 | tf_op jit(solution)/shard_map/ppermute | solution.py:783
  201.7 17.6 %collective-permute-start.36 = (bf16[160,768]{1,0:T(8,128)(2,1)S(1)}, bf16[160,768]{1,0:T(8,128)(2,1)S(1)}, u32[]{:S(2)}, u32[]{:S(2)}) collective-permute-start(bf16[160,768]{1,0:T(8,128)(2,1)S(1)} %qkv_join_a.1.refs_2_.refs_0_), channel_id=1, source_target_pairs={{0,24},{4,28},{8,16},{12,20},{16,8},{20,12},{24,0},{28,4},{1,25},{... | collective-permute-start | bytes 737288 | tf_op jit(solution)/shard_map/ppermute | solution.py:783
  204.2 21.5 %collective-permute-start.46 = (bf16[240,768]{1,0:T(8,128)(2,1)S(1)}, bf16[240,768]{1,0:T(8,128)(2,1)S(1)}, u32[]{:S(2)}, u32[]{:S(2)}) collective-permute-start(bf16[240,768]{1,0:T(8,128)(2,1)S(1)} %up_join_b.1.refs_4_.refs_0_), channel_id=1, source_target_pairs={{0,12},{4,8},{8,4},{12,0},{16,28},{20,24},{24,20},{28,16},{1,13},{... | collective-permute-start | bytes 1105928 | tf_op jit(solution)/shard_map/ppermute | solution.py:783
  205.8 16.2 %collective-permute-start.35 = (bf16[128,768]{1,0:T(8,128)(2,1)}, bf16[128,768]{1,0:T(8,128)(2,1)}, u32[]{:S(2)}, u32[]{:S(2)}) collective-permute-start(bf16[128,768]{1,0:T(8,128)(2,1)} %get-tuple-element.136), channel_id=1, source_target_pairs={{0,3},{1,2},{2,1},{3,0},{4,7},{5,6},{6,5},{7,4},{8,11},{9,10},{10,... | collective-permute-start | bytes 589832 | tf_op jit(solution)/shard_map/ppermute | solution.py:783
  212.4 12.6 %collective-permute-start.33 = (bf16[128,768]{1,0:T(8,128)(2,1)}, bf16[128,768]{1,0:T(8,128)(2,1)}, u32[]{:S(2)}, u32[]{:S(2)}) collective-permute-start(bf16[128,768]{1,0:T(8,128)(2,1)} %get-tuple-element.138), channel_id=1, source_target_pairs={{0,1},{1,0},{2,3},{3,2},{4,5},{5,4},{6,7},{7,6},{8,9},{9,8},{10,11... | collective-permute-start | bytes 589832 | tf_op jit(solution)/shard_map/ppermute | solution.py:783
  219.2 15.4 %collective-permute-start.45 = (bf16[240,768]{1,0:T(8,128)(2,1)S(1)}, bf16[240,768]{1,0:T(8,128)(2,1)S(1)}, u32[]{:S(2)}, u32[]{:S(2)}) collective-permute-start(bf16[240,768]{1,0:T(8,128)(2,1)S(1)} %up_join_b.1.refs_4_.refs_0_), channel_id=1, source_target_pairs={{0,4},{4,0},{8,12},{12,8},{16,20},{20,16},{24,28},{28,24},{1,5},{5... | collective-permute-start | bytes 1105928 | tf_op jit(solution)/shard_map/ppermute | solution.py:783
  222.1 12.5 %collective-permute-start.44 = (bf16[240,768]{1,0:T(8,128)(2,1)S(1)}, bf16[240,768]{1,0:T(8,128)(2,1)S(1)}, u32[]{:S(2)}, u32[]{:S(2)}) collective-permute-start(bf16[240,768]{1,0:T(8,128)(2,1)S(1)} %up_join_b.1.refs_4_.refs_0_), channel_id=1, source_target_pairs={{0,8},{4,12},{8,0},{12,4},{16,24},{20,28},{24,16},{28,20},{1,9},{5... | collective-permute-start | bytes 1105928 | tf_op jit(solution)/shard_map/ppermute | solution.py:783
  222.2 17.7 %collective-permute-start.43 = (bf16[160,768]{1,0:T(8,128)(2,1)S(1)}, bf16[160,768]{1,0:T(8,128)(2,1)S(1)}, u32[]{:S(2)}, u32[]{:S(2)}) collective-permute-start(bf16[160,768]{1,0:T(8,128)(2,1)S(1)} %qkv_join_b.1.refs_4_.refs_0_), channel_id=1, source_target_pairs={{0,12},{4,8},{8,4},{12,0},{16,28},{20,24},{24,20},{28,16},{1,13},{... | collective-permute-start | bytes 737288 | tf_op jit(solution)/shard_map/ppermute | solution.py:783
  225.1 17.4 %collective-permute-start.42 = (bf16[160,768]{1,0:T(8,128)(2,1)S(1)}, bf16[160,768]{1,0:T(8,128)(2,1)S(1)}, u32[]{:S(2)}, u32[]{:S(2)}) collective-permute-start(bf16[160,768]{1,0:T(8,128)(2,1)S(1)} %qkv_join_b.1.refs_4_.refs_0_), channel_id=1, source_target_pairs={{0,4},{4,0},{8,12},{12,8},{16,20},{20,16},{24,28},{28,24},{1,5},{5... | collective-permute-start | bytes 737288 | tf_op jit(solution)/shard_map/ppermute | solution.py:783
  225.6 17.0 %collective-permute-start.41 = (bf16[160,768]{1,0:T(8,128)(2,1)S(1)}, bf16[160,768]{1,0:T(8,128)(2,1)S(1)}, u32[]{:S(2)}, u32[]{:S(2)}) collective-permute-start(bf16[160,768]{1,0:T(8,128)(2,1)S(1)} %qkv_join_b.1.refs_4_.refs_0_), channel_id=1, source_target_pairs={{0,8},{4,12},{8,0},{12,4},{16,24},{20,28},{24,16},{28,20},{1,9},{5... | collective-permute-start | bytes 737288 | tf_op jit(solution)/shard_map/ppermute | solution.py:783
  (32 other events, 243.6 us)
Sparse Core Ops, SparseCore 0:
  11.4 59.4 all-gather.1

commit v7 on v6

--- a/solution.py
+++ b/solution.py
@@ -19,7 +19,7 @@
 norm_eps = 1e-05
 f32 = jnp.float32
 bf16 = jnp.bfloat16
-VMEM_BYTES = 28 * 1024 * 1024
+VMEM_BYTES = 24 * 1024 * 1024
 PIN = 100
 EXTRA = 16
 SMALL = 128

time: 255 us -> 255 us (level)
  no operation moved by 1% of the time
where the time goes in v7:
time: 255 us; the launch traced here: 251 us
  Pallas kernels  115 us (45%)
  waiting for transfers between devices  67.1 us (26%)
  starting transfers between devices  43 us (17%)
  between operations  14.5 us (6%)
  local copies, waits for them, and re-layouts  11.4 us (4%)
    pallas_call x29, Pallas kernels, call(): pl.pallas_call(body, grid_spec=pltpu.PrefetchScalarGridSpec(num_scalar_pr...  115 us
    ppermute x46, waiting for transfers between devices, flip(): return lax.ppermute(value, axis, [(i, i ^ mask) for i in range(count)])  66.1 us
    ppermute x46, starting transfers between devices, flip(): return lax.ppermute(value, axis, [(i, i ^ mask) for i in range(count)])  40.4 us
    reshape x8, local copies, waits for them, and re-layouts, per_device(): row = lambda v: v.reshape(1, -1)  5.51 us
  transfers between devices with their start and end apart: 48, of which 26 were waited for; matrix products, arithmetic and copies ran while one was open for 4% of the time, Pallas kernels for 35%

profile of v7, /device:TPU:0, one launch (start us, length us, event | category | flops | bytes accessed | tf_op | source)
XLA Modules:
  0.0 251.4 jit_solution(2856941090785860332)
XLA Ops:
  21.8 16.9 %attention_forward.1 = (bf16[512,768]{1,0:T(8,128)(2,1)}, bf16[512,768]{1,0:T(8,128)(2,1)}, bf16[512,768]{1,0:T(8,128)(2,1)}, bf16[768,512]{1,0:T(8,128)(2,1)}, ...) custom-call(s32[8]{0:T(128)S(1)} %pad_add_fusion.sc_ref, ...), custom_call_target="tpu_custom_call" | custom-call | tf_op jit(solution)/shard_map/attention_forward/pallas_call | solution.py:88
  39.5 13.0 %feed_forward.1 = (bf16[3072,512]{1,0:T(8,128)(2,1)}, bf16[4,512,768]{2,1,0:T(8,128)(2,1)}, f32[512,768]{1,0:T(8,128)}, f32[512,1]{1,0:T(8,128)}, bf16[512,768]{1,0:T(8,128)(2,1)}, /*index=5*/f32[8,768]{1,0:T(8,128)S(1)}) custom-call(s32[8]{0:T(128)S(1)} %pad_add_fusion.sc_ref, bf16[512,768]{1,0:T(8,128)(2,1)S(1)} %get-tuple-element.80.refs_0_, ...), custom_call_target="tpu_custom_call" | custom-call | tf_op jit(solution)/shard_map/feed_forward/pallas_call | solution.py:88
  62.0 2.7 %collective-permute-start.15 = (bf16[32,768]{1,0:T(8,128)(2,1)S(1)}, bf16[32,768]{1,0:T(8,128)(2,1)S(1)}, u32[]{:S(2)}, u32[]{:S(2)}) collective-permute-start(bf16[32,768]{1,0:T(8,128)(2,1)S(1)} %pad_maximum_fusion.1.refs_4_), channel_id=1, source_target_pairs={{0,16},{4,20},{8,24},{12,28},{16,0},{20,4},{24,8},{28,12},{1,17},{... | collective-permute-start | bytes 147464 | tf_op jit(solution)/shard_map/ppermute | solution.py:783
  66.3 4.9 %collective-permute-done.13 = bf16[32,768]{1,0:T(8,128)(2,1)S(1)} collective-permute-done((bf16[32,768]{1,0:T(8,128)(2,1)S(1)}, bf16[32,768]{1,0:T(8,128)(2,1)S(1)}, u32[]{:S(2)}, u32[]{:S(2)}) %collective-permute-start.13) | collective-permute-done | bytes 49184 | tf_op jit(solution)/shard_map/ppermute | solution.py:783
  72.8 12.7 %retrieval.1 = (f32[1024,1]{1,0:T(8,128)S(1)}, bf16[512,768]{1,0:T(8,128)(2,1)S(1)}, f32[512,768]{1,0:T(8,128)S(1)}, f32[8,768]{1,0:T(8,128)S(1)}) custom-call(s32[8]{0:T(128)S(1)} %pad_add_fusion.sc_ref, bf16[1024,832]{1,0:T(8,128)(2,1)} %all-gather.2.cloned.1.call-done.refs_0_, bf16[256,768]{1,0:T(8,128)(2,1)S(1)} %constant_dynamic-update-slice_fusion.11.refs_1_, ...), custom_call_target="tpu_custom_call" | custom-call | tf_op jit(solution)/shard_map/retrieval/pallas_call | solution.py:88
  87.9 11.5 %feed_back.1 = (bf16[5,512,768]{2,1,0:T(8,128)(2,1)S(1)}, f32[4,1,768]{2,1,0:T(1,128)S(1)}, f32[512,768]{1,0:T(8,128)S(1)}, bf16[512,768]{1,0:T(8,128)(2,1)S(1)}, f32[8,768]{1,0:T(8,128)S(1)}) custom-call(s32[8]{0:T(128)S(1)} %pad_add_fusion.sc_ref, bf16[512,768]{1,0:T(8,128)(2,1)S(1)} %get-tuple-element.94.refs_0_.refs_2_, ...), custom_call_target="tpu_custom_call" | custom-call | tf_op jit(solution)/shard_map/feed_back/pallas_call | solution.py:88
  99.7 3.3 %down_send.1.refs_5_ = bf16[2,384,768]{2,1,0:T(8,128)(2,1)S(1)} custom-call(s32[4]{0:T(128)S(1)} %pad_add_fusion.1.sc_ref, bf16[4,2,384,512]{3,2,1,0:T(8,128)(2,1)} %bitcast.27, bf16[2,1344,512]{2,1,0:T(8,128)(2,1)} %bitcast.23, bf16[512,768]{1,0:T(8,128)(2,1)S(1)} %get-tuple-element.94.refs_0_.refs_2_, ...), custom_call_target="tpu_custom_call" | custom-call | tf_op jit(solution)/shard_map/down_send/pallas_call | solution.py:88
  106.3 4.7 %up_send.1.refs_9_ = bf16[5,192,768]{2,1,0:T(8,128)(2,1)S(1)} custom-call(s32[4]{0:T(128)S(1)} %pad_add_fusion.1.sc_ref, bf16[4,192,512]{2,1,0:T(8,128)(2,1)} %bitcast.36, bf16[4,192,512]{2,1,0:T(8,128)(2,1)} %bitcast.33, bf16[2,7,192,512]{3,2,1,0:T(8,128)(2,1)} %copy-done.2, bf16[5,512,768]{2,1,0:T(8,128)(2,1)S(1)} %get-tuple-element.99.refs_4_.refs_3_, ...), custom_call_target="tpu_custom_call" | custom-call | tf_op jit(solution)/shard_map/up_send/pallas_call | solution.py:88
  111.9 16.0 %attention_back.1 = (bf16[512,768]{1,0:T(8,128)(2,1)S(1)}, bf16[512,768]{1,0:T(8,128)(2,1)S(1)}, bf16[512,768]{1,0:T(8,128)(2,1)S(1)}, bf16[512,768]{1,0:T(8,128)(2,1)S(1)}, f32[8,768]{1,0:T(8,128)S(1)}) custom-call(s32[8]{0:T(128)S(1)} %pad_add_fusion.sc_ref, bf16[512,768]{1,0:T(8,128)(2,1)} %get-tuple-element.100.refs_0_, ...), custom_call_target="tpu_custom_call" | custom-call | tf_op jit(solution)/shard_map/attention_back/pallas_call | solution.py:88
  133.4 2.7 %qkv_send.1.refs_5_ = bf16[592,768]{1,0:T(8,128)(2,1)S(1)} custom-call(s32[4]{0:T(128)S(1)} %pad_add_fusion.1.sc_ref, bf16[4,192,512]{2,1,0:T(8,128)(2,1)} %bitcast.30, bf16[2,7,192,512]{3,2,1,0:T(8,128)(2,1)} %copy-done.2, f32[2,16,256]{2,1,0:T(8,128)S(1)} %get-tuple-element.110.refs_2_.refs_6_, f32[2,16,256]{2,1,0:T(8,128)S(1)} %collective-permute-done.20.refs_3_, ...), custom_call_target="tpu_custom_call" | custom-call | tf_op jit(solution)/shard_map/qkv_send/pallas_call | solution.py:88
  137.3 3.4 %down_mid.1 = (bf16[2,192,768]{2,1,0:T(8,128)(2,1)S(1)}, bf16[2,192,768]{2,1,0:T(8,128)(2,1)S(1)}) custom-call(s32[4]{0:T(128)S(1)} %pad_add_fusion.1.sc_ref, bf16[4,2,384,512]{3,2,1,0:T(8,128)(2,1)} %bitcast.28, bf16[2,1344,512]{2,1,0:T(8,128)(2,1)} %bitcast.24, bf16[512,768]{1,0:T(8,128)(2,1)S(1)} %get-tuple-element.94.refs_0_.refs_2_, ...), custom_call_target="tpu_custom_call" | custom-call | flops 3449999872 | tf_op jit(solution)/shard_map/down_mid/pallas_call | solution.py:88
  141.6 4.6 %collective-permute-done.25.refs_5_ = bf16[5,192,768]{2,1,0:T(8,128)(2,1)S(1)} collective-permute-done((bf16[5,192,768]{2,1,0:T(8,128)(2,1)S(1)}, bf16[5,192,768]{2,1,0:T(8,128)(2,1)S(1)}, u32[]{:S(2)}, u32[]{:S(2)}) %collective-permute-start.25) | collective-permute-done | bytes 1474592 | tf_op jit(solution)/shard_map/ppermute | solution.py:783
  146.2 5.0 %up_keep.1 = (bf16[2,240,768]{2,1,0:T(8,128)(2,1)S(1)}, bf16[2,240,768]{2,1,0:T(8,128)(2,1)S(1)}) custom-call(s32[4]{0:T(128)S(1)} %pad_add_fusion.1.sc_ref, bf16[4,192,512]{2,1,0:T(8,128)(2,1)} %bitcast.37, bf16[4,192,512]{2,1,0:T(8,128)(2,1)} %bitcast.34, bf16[2,7,192,512]{3,2,1,0:T(8,128)(2,1)} %copy-done.2, ...), custom_call_target="tpu_custom_call" | custom-call | flops 115000000512 | tf_op jit(solution)/shard_map/up_keep/pallas_call | solution.py:88
  152.9 3.2 %collective-permute-done.24.refs_1_ = bf16[2,192,768]{2,1,0:T(8,128)(2,1)S(1)} collective-permute-done((bf16[2,192,768]{2,1,0:T(8,128)(2,1)S(1)}, bf16[2,192,768]{2,1,0:T(8,128)(2,1)S(1)}, u32[]{:S(2)}, u32[]{:S(2)}) %collective-permute-start.24) | collective-permute-done | bytes 589856 | tf_op jit(solution)/shard_map/ppermute | solution.py:783
  156.9 2.9 %collective-permute-start.26 = (bf16[2,192,768]{2,1,0:T(8,128)(2,1)S(1)}, bf16[2,192,768]{2,1,0:T(8,128)(2,1)S(1)}, u32[]{:S(2)}, u32[]{:S(2)}) collective-permute-start(bf16[2,192,768]{2,1,0:T(8,128)(2,1)S(1)} %down_join_a.1.refs_11_.refs_0_), channel_id=1, source_target_pairs={{0,24},{4,28},{8,16},{12,20},{16,8},{20,12},{24,0},{28,4},{1,25},{... | collective-permute-start | bytes 1769480 | tf_op jit(solution)/shard_map/ppermute | solution.py:783
  159.7 5.2 %collective-permute-done.28.refs_10_ = bf16[592,768]{1,0:T(8,128)(2,1)S(1)} collective-permute-done((bf16[592,768]{1,0:T(8,128)(2,1)S(1)}, bf16[592,768]{1,0:T(8,128)(2,1)S(1)}, u32[]{:S(2)}, u32[]{:S(2)}) %collective-permute-start.28) | collective-permute-done | bytes 909344 | tf_op jit(solution)/shard_map/ppermute | solution.py:783
  164.9 3.3 %qkv_keep.1 = (bf16[2,160,768]{2,1,0:T(8,128)(2,1)S(1)}, bf16[2,160,768]{2,1,0:T(8,128)(2,1)S(1)}) custom-call(s32[4]{0:T(128)S(1)} %pad_add_fusion.1.sc_ref, bf16[4,192,512]{2,1,0:T(8,128)(2,1)} %bitcast.31, bf16[2,7,192,512]{3,2,1,0:T(8,128)(2,1)} %copy-done.2, f32[2,16,256]{2,1,0:T(8,128)S(1)} %get-tuple-element.110.refs_2_.refs_6_, ...), custom_call_target="tpu_custom_call" | custom-call | tf_op jit(solution)/shard_map/qkv_keep/pallas_call | solution.py:88
  171.3 9.4 %collective-permute-done.30.refs_1_ = bf16[2,160,768]{2,1,0:T(8,128)(2,1)S(1)} collective-permute-done((bf16[2,160,768]{2,1,0:T(8,128)(2,1)S(1)}, bf16[2,160,768]{2,1,0:T(8,128)(2,1)S(1)}, u32[]{:S(2)}, u32[]{:S(2)}) %collective-permute-start.30) | collective-permute-done | bytes 491552 | tf_op jit(solution)/shard_map/ppermute | solution.py:783
  182.9 2.7 %collective-permute-start.40 = (bf16[240,768]{1,0:T(8,128)(2,1)S(1)}, bf16[240,768]{1,0:T(8,128)(2,1)S(1)}, u32[]{:S(2)}, u32[]{:S(2)}) collective-permute-start(bf16[240,768]{1,0:T(8,128)(2,1)S(1)} %up_join_a.1.refs_2_.refs_0_), channel_id=1, source_target_pairs={{0,24},{4,28},{8,16},{12,20},{16,8},{20,12},{24,0},{28,4},{1,25},{... | collective-permute-start | bytes 1105928 | tf_op jit(solution)/shard_map/ppermute | solution.py:783
  189.7 6.5 %collective-permute-done.31.refs_1_ = bf16[192,768]{1,0:T(8,128)(2,1)S(1)} collective-permute-done((bf16[192,768]{1,0:T(8,128)(2,1)S(1)}, bf16[192,768]{1,0:T(8,128)(2,1)S(1)}, u32[]{:S(2)}, u32[]{:S(2)}) %collective-permute-start.31) | collective-permute-done | bytes 294944 | tf_op jit(solution)/shard_map/ppermute | solution.py:783
  205.8 6.3 %collective-permute-done.38.refs_2_ = bf16[192,768]{1,0:T(8,128)(2,1)S(1)} collective-permute-done((bf16[192,768]{1,0:T(8,128)(2,1)S(1)}, bf16[192,768]{1,0:T(8,128)(2,1)S(1)}, u32[]{:S(2)}, u32[]{:S(2)}) %collective-permute-start.38) | collective-permute-done | bytes 294944 | tf_op jit(solution)/shard_map/ppermute | solution.py:783
  222.2 2.9 %collective-permute-start.43 = (bf16[160,768]{1,0:T(8,128)(2,1)S(1)}, bf16[160,768]{1,0:T(8,128)(2,1)S(1)}, u32[]{:S(2)}, u32[]{:S(2)}) collective-permute-start(bf16[160,768]{1,0:T(8,128)(2,1)S(1)} %qkv_join_b.1.refs_4_.refs_0_), channel_id=1, source_target_pairs={{0,12},{4,8},{8,4},{12,0},{16,28},{20,24},{24,20},{28,16},{1,13},{... | collective-permute-start | bytes 737288 | tf_op jit(solution)/shard_map/ppermute | solution.py:783
  229.6 5.0 %collective-permute-done.45.refs_2_ = bf16[240,768]{1,0:T(8,128)(2,1)S(1)} collective-permute-done((bf16[240,768]{1,0:T(8,128)(2,1)S(1)}, bf16[240,768]{1,0:T(8,128)(2,1)S(1)}, u32[]{:S(2)}, u32[]{:S(2)}) %collective-permute-start.45) | collective-permute-done | bytes 368672 | tf_op jit(solution)/shard_map/ppermute | solution.py:783
  236.9 2.9 %collective-permute-done.43.refs_3_ = bf16[160,768]{1,0:T(8,128)(2,1)S(1)} collective-permute-done((bf16[160,768]{1,0:T(8,128)(2,1)S(1)}, bf16[160,768]{1,0:T(8,128)(2,1)S(1)}, u32[]{:S(2)}, u32[]{:S(2)}) %collective-permute-start.43) | collective-permute-done | bytes 245792 | tf_op jit(solution)/shard_map/ppermute | solution.py:783
  (151 shorter events, 85.2 us)
Async XLA Ops:
  7.2 65.6 %all-gather.2.cloned.1.call-start = ((), (), s32[]{:S(2)}) async-start(), calls=%async_computation | async-start | bytes 1892352 | tf_op jit(solution)/shard_map/all_gather | solution.py:900
  19.2 19.6 %collective-permute-start.3 = (bf16[128,768]{1,0:T(8,128)(2,1)S(1)}, bf16[128,768]{1,0:T(8,128)(2,1)S(1)}, u32[]{:S(2)}, u32[]{:S(2)}) collective-permute-start(bf16[128,768]{1,0:T(8,128)(2,1)S(1)} %get-tuple-element.82), channel_id=1, source_target_pairs={{0,1},{1,0},{2,3},{3,2},{4,5},{5,4},{6,7},{7,6},{8,9},{9,8},{10,11... | collective-permute-start | bytes 589832 | tf_op jit(solution)/shard_map/ppermute | solution.py:783
  19.4 19.5 %collective-permute-start.4 = (bf16[128,768]{1,0:T(8,128)(2,1)S(1)}, bf16[128,768]{1,0:T(8,128)(2,1)S(1)}, u32[]{:S(2)}, u32[]{:S(2)}) collective-permute-start(bf16[128,768]{1,0:T(8,128)(2,1)S(1)} %get-tuple-element.83), channel_id=1, source_target_pairs={{0,2},{1,3},{2,0},{3,1},{4,6},{5,7},{6,4},{7,5},{8,10},{9,11},{10,... | collective-permute-start | bytes 589832 | tf_op jit(solution)/shard_map/ppermute | solution.py:783
  21.3 17.6 %collective-permute-start.5 = (bf16[128,768]{1,0:T(8,128)(2,1)S(1)}, bf16[128,768]{1,0:T(8,128)(2,1)S(1)}, u32[]{:S(2)}, u32[]{:S(2)}) collective-permute-start(bf16[128,768]{1,0:T(8,128)(2,1)S(1)} %get-tuple-element.84), channel_id=1, source_target_pairs={{0,3},{1,2},{2,1},{3,0},{4,7},{5,6},{6,5},{7,4},{8,11},{9,10},{10,... | collective-permute-start | bytes 589832 | tf_op jit(solution)/shard_map/ppermute | solution.py:783
  102.9 34.4 %collective-permute-start.18 = (bf16[2,384,768]{2,1,0:T(8,128)(2,1)S(1)}, bf16[2,384,768]{2,1,0:T(8,128)(2,1)S(1)}, u32[]{:S(2)}, u32[]{:S(2)}) collective-permute-start(bf16[2,384,768]{2,1,0:T(8,128)(2,1)S(1)} %down_send.1.refs_5_), channel_id=1, source_target_pairs={{0,4},{4,0},{8,12},{12,8},{16,20},{20,16},{24,28},{28,24},{1,5},{5... | collective-permute-start | bytes 3538952 | tf_op jit(solution)/shard_map/ppermute | solution.py:783
  111.0 35.2 %collective-permute-start.25 = (bf16[5,192,768]{2,1,0:T(8,128)(2,1)S(1)}, bf16[5,192,768]{2,1,0:T(8,128)(2,1)S(1)}, u32[]{:S(2)}, u32[]{:S(2)}) collective-permute-start(bf16[5,192,768]{2,1,0:T(8,128)(2,1)S(1)} %up_send.1.refs_9_), channel_id=1, source_target_pairs={{0,2},{1,3},{2,0},{3,1},{4,6},{5,7},{6,4},{7,5},{8,10},{9,11},{10,... | collective-permute-start | bytes 4423688 | tf_op jit(solution)/shard_map/ppermute | solution.py:783
  136.1 28.8 %collective-permute-start.28 = (bf16[592,768]{1,0:T(8,128)(2,1)S(1)}, bf16[592,768]{1,0:T(8,128)(2,1)S(1)}, u32[]{:S(2)}, u32[]{:S(2)}) collective-permute-start(bf16[592,768]{1,0:T(8,128)(2,1)S(1)} %qkv_send.1.refs_5_), channel_id=1, source_target_pairs={{0,2},{1,3},{2,0},{3,1},{4,6},{5,7},{6,4},{7,5},{8,10},{9,11},{10,... | collective-permute-start | bytes 2727944 | tf_op jit(solution)/shard_map/ppermute | solution.py:783
  140.8 15.4 %collective-permute-start.24 = (bf16[2,192,768]{2,1,0:T(8,128)(2,1)S(1)}, bf16[2,192,768]{2,1,0:T(8,128)(2,1)S(1)}, u32[]{:S(2)}, u32[]{:S(2)}) collective-permute-start(bf16[2,192,768]{2,1,0:T(8,128)(2,1)S(1)} %get-tuple-element.116), channel_id=1, source_target_pairs={{0,8},{4,12},{8,0},{12,4},{16,24},{20,28},{24,16},{28,20},{1,9},{5... | collective-permute-start | bytes 1769480 | tf_op jit(solution)/shard_map/ppermute | solution.py:783
  151.2 18.7 %collective-permute-start.27 = (bf16[2,240,768]{2,1,0:T(8,128)(2,1)S(1)}, bf16[2,240,768]{2,1,0:T(8,128)(2,1)S(1)}, u32[]{:S(2)}, u32[]{:S(2)}) collective-permute-start(bf16[2,240,768]{2,1,0:T(8,128)(2,1)S(1)} %get-tuple-element.118), channel_id=1, source_target_pairs={{0,4},{4,0},{8,12},{12,8},{16,20},{20,16},{24,28},{28,24},{1,5},{5... | collective-permute-start | bytes 2211848 | tf_op jit(solution)/shard_map/ppermute | solution.py:783
  156.9 28.7 %collective-permute-start.26 = (bf16[2,192,768]{2,1,0:T(8,128)(2,1)S(1)}, bf16[2,192,768]{2,1,0:T(8,128)(2,1)S(1)}, u32[]{:S(2)}, u32[]{:S(2)}) collective-permute-start(bf16[2,192,768]{2,1,0:T(8,128)(2,1)S(1)} %down_join_a.1.refs_11_.refs_0_), channel_id=1, source_target_pairs={{0,24},{4,28},{8,16},{12,20},{16,8},{20,12},{24,0},{28,4},{1,25},{... | collective-permute-start | bytes 1769480 | tf_op jit(solution)/shard_map/ppermute | solution.py:783
  182.9 16.4 %collective-permute-start.40 = (bf16[240,768]{1,0:T(8,128)(2,1)S(1)}, bf16[240,768]{1,0:T(8,128)(2,1)S(1)}, u32[]{:S(2)}, u32[]{:S(2)}) collective-permute-start(bf16[240,768]{1,0:T(8,128)(2,1)S(1)} %up_join_a.1.refs_2_.refs_0_), channel_id=1, source_target_pairs={{0,24},{4,28},{8,16},{12,20},{16,8},{20,12},{24,0},{28,4},{1,25},{... | collective-permute-start | bytes 1105928 | tf_op jit(solution)/shard_map/ppermute | solution.py:783
  187.3 14.4 %collective-permute-start.7 = (bf16[128,768]{1,0:T(8,128)(2,1)S(1)}, bf16[128,768]{1,0:T(8,128)(2,1)S(1)}, u32[]{:S(2)}, u32[]{:S(2)}) collective-permute-start(bf16[128,768]{1,0:T(8,128)(2,1)S(1)} %get-tuple-element.141), channel_id=1, source_target_pairs={{0,2},{1,3},{2,0},{3,1},{4,6},{5,7},{6,4},{7,5},{8,10},{9,11},{10,... | collective-permute-start | bytes 589832 | tf_op jit(solution)/shard_map/ppermute | solution.py:783
  189.0 15.2 %collective-permute-start.6 = (bf16[128,768]{1,0:T(8,128)(2,1)S(1)}, bf16[128,768]{1,0:T(8,128)(2,1)S(1)}, u32[]{:S(2)}, u32[]{:S(2)}) collective-permute-start(bf16[128,768]{1,0:T(8,128)(2,1)S(1)} %get-tuple-element.142), channel_id=1, source_target_pairs={{0,1},{1,0},{2,3},{3,2},{4,5},{5,4},{6,7},{7,6},{8,9},{9,8},{10,11... | collective-permute-start | bytes 589832 | tf_op jit(solution)/shard_map/ppermute | solution.py:783
  198.3 13.9 %collective-permute-start.38 = (bf16[192,768]{1,0:T(8,128)(2,1)S(1)}, bf16[192,768]{1,0:T(8,128)(2,1)S(1)}, u32[]{:S(2)}, u32[]{:S(2)}) collective-permute-start(bf16[192,768]{1,0:T(8,128)(2,1)S(1)} %down_join_x.1.refs_4_.refs_2_.refs_0_), channel_id=1, source_target_pairs={{0,4},{4,0},{8,12},{12,8},{16,20},{20,16},{24,28},{28,24},{1,5},{5... | collective-permute-start | bytes 884744 | tf_op jit(solution)/shard_map/ppermute | solution.py:783
  199.3 13.1 %collective-permute-start.37 = (bf16[192,768]{1,0:T(8,128)(2,1)S(1)}, bf16[192,768]{1,0:T(8,128)(2,1)S(1)}, u32[]{:S(2)}, u32[]{:S(2)}) collective-permute-start(bf16[192,768]{1,0:T(8,128)(2,1)S(1)} %down_join_x.1.refs_4_.refs_2_.refs_0_), channel_id=1, source_target_pairs={{0,8},{4,12},{8,0},{12,4},{16,24},{20,28},{24,16},{28,20},{1,9},{5... | collective-permute-start | bytes 884744 | tf_op jit(solution)/shard_map/ppermute | solution.py:783
  201.7 17.6 %collective-permute-start.36 = (bf16[160,768]{1,0:T(8,128)(2,1)S(1)}, bf16[160,768]{1,0:T(8,128)(2,1)S(1)}, u32[]{:S(2)}, u32[]{:S(2)}) collective-permute-start(bf16[160,768]{1,0:T(8,128)(2,1)S(1)} %qkv_join_a.1.refs_2_.refs_0_), channel_id=1, source_target_pairs={{0,24},{4,28},{8,16},{12,20},{16,8},{20,12},{24,0},{28,4},{1,25},{... | collective-permute-start | bytes 737288 | tf_op jit(solution)/shard_map/ppermute | solution.py:783
  204.2 21.5 %collective-permute-start.46 = (bf16[240,768]{1,0:T(8,128)(2,1)S(1)}, bf16[240,768]{1,0:T(8,128)(2,1)S(1)}, u32[]{:S(2)}, u32[]{:S(2)}) collective-permute-start(bf16[240,768]{1,0:T(8,128)(2,1)S(1)} %up_join_b.1.refs_4_.refs_0_), channel_id=1, source_target_pairs={{0,12},{4,8},{8,4},{12,0},{16,28},{20,24},{24,20},{28,16},{1,13},{... | collective-permute-start | bytes 1105928 | tf_op jit(solution)/shard_map/ppermute | solution.py:783
  205.8 16.2 %collective-permute-start.35 = (bf16[128,768]{1,0:T(8,128)(2,1)}, bf16[128,768]{1,0:T(8,128)(2,1)}, u32[]{:S(2)}, u32[]{:S(2)}) collective-permute-start(bf16[128,768]{1,0:T(8,128)(2,1)} %get-tuple-element.136), channel_id=1, source_target_pairs={{0,3},{1,2},{2,1},{3,0},{4,7},{5,6},{6,5},{7,4},{8,11},{9,10},{10,... | collective-permute-start | bytes 589832 | tf_op jit(solution)/shard_map/ppermute | solution.py:783
  212.4 12.6 %collective-permute-start.33 = (bf16[128,768]{1,0:T(8,128)(2,1)}, bf16[128,768]{1,0:T(8,128)(2,1)}, u32[]{:S(2)}, u32[]{:S(2)}) collective-permute-start(bf16[128,768]{1,0:T(8,128)(2,1)} %get-tuple-element.138), channel_id=1, source_target_pairs={{0,1},{1,0},{2,3},{3,2},{4,5},{5,4},{6,7},{7,6},{8,9},{9,8},{10,11... | collective-permute-start | bytes 589832 | tf_op jit(solution)/shard_map/ppermute | solution.py:783
  219.2 15.4 %collective-permute-start.45 = (bf16[240,768]{1,0:T(8,128)(2,1)S(1)}, bf16[240,768]{1,0:T(8,128)(2,1)S(1)}, u32[]{:S(2)}, u32[]{:S(2)}) collective-permute-start(bf16[240,768]{1,0:T(8,128)(2,1)S(1)} %up_join_b.1.refs_4_.refs_0_), channel_id=1, source_target_pairs={{0,4},{4,0},{8,12},{12,8},{16,20},{20,16},{24,28},{28,24},{1,5},{5... | collective-permute-start | bytes 1105928 | tf_op jit(solution)/shard_map/ppermute | solution.py:783
  222.1 12.5 %collective-permute-start.44 = (bf16[240,768]{1,0:T(8,128)(2,1)S(1)}, bf16[240,768]{1,0:T(8,128)(2,1)S(1)}, u32[]{:S(2)}, u32[]{:S(2)}) collective-permute-start(bf16[240,768]{1,0:T(8,128)(2,1)S(1)} %up_join_b.1.refs_4_.refs_0_), channel_id=1, source_target_pairs={{0,8},{4,12},{8,0},{12,4},{16,24},{20,28},{24,16},{28,20},{1,9},{5... | collective-permute-start | bytes 1105928 | tf_op jit(solution)/shard_map/ppermute | solution.py:783
  222.2 17.7 %collective-permute-start.43 = (bf16[160,768]{1,0:T(8,128)(2,1)S(1)}, bf16[160,768]{1,0:T(8,128)(2,1)S(1)}, u32[]{:S(2)}, u32[]{:S(2)}) collective-permute-start(bf16[160,768]{1,0:T(8,128)(2,1)S(1)} %qkv_join_b.1.refs_4_.refs_0_), channel_id=1, source_target_pairs={{0,12},{4,8},{8,4},{12,0},{16,28},{20,24},{24,20},{28,16},{1,13},{... | collective-permute-start | bytes 737288 | tf_op jit(solution)/shard_map/ppermute | solution.py:783
  225.1 17.4 %collective-permute-start.42 = (bf16[160,768]{1,0:T(8,128)(2,1)S(1)}, bf16[160,768]{1,0:T(8,128)(2,1)S(1)}, u32[]{:S(2)}, u32[]{:S(2)}) collective-permute-start(bf16[160,768]{1,0:T(8,128)(2,1)S(1)} %qkv_join_b.1.refs_4_.refs_0_), channel_id=1, source_target_pairs={{0,4},{4,0},{8,12},{12,8},{16,20},{20,16},{24,28},{28,24},{1,5},{5... | collective-permute-start | bytes 737288 | tf_op jit(solution)/shard_map/ppermute | solution.py:783
  225.6 17.0 %collective-permute-start.41 = (bf16[160,768]{1,0:T(8,128)(2,1)S(1)}, bf16[160,768]{1,0:T(8,128)(2,1)S(1)}, u32[]{:S(2)}, u32[]{:S(2)}) collective-permute-start(bf16[160,768]{1,0:T(8,128)(2,1)S(1)} %qkv_join_b.1.refs_4_.refs_0_), channel_id=1, source_target_pairs={{0,8},{4,12},{8,0},{12,4},{16,24},{20,28},{24,16},{28,20},{1,9},{5... | collective-permute-start | bytes 737288 | tf_op jit(solution)/shard_map/ppermute | solution.py:783
  (32 other events, 243.6 us)
Sparse Core Ops, SparseCore 0:
  11.4 59.4 all-gather.1
